TPU v7x, 32 devices: a whole 2x2x4 slice. The times are simulated.
32 devices in a mesh: rep: 2 (over y), tok: 4 (over x, core), col: 4 (over z).
Axes of the slice: x: 2, y: 2, z: 4, core: 2. Of those that a mesh axis runs over, the one named last changes fastest.
Arguments:
- request_rows: bfloat16 [64, 10240], P(('rep', 'tok', 'col')), parts along dimension 0, may hold values from -100 to 100
- key_cache: bfloat16 [96, 16, 2048], P(('rep', 'tok', 'col')), parts along dimension 0, may hold values from -3 to 3
- route_list: int32 [8, 4, 3], P('rep', 'col'), parts along dimension 0, may hold values from 0 to 7, as said below
- route_count: int32 [8, 4], P('rep', 'col'), parts along dimension 0, may hold values from 1 to 3, as said below
- norm_gain: float32 [8192], replicated, may hold values from 0.1 to 1.9
- gate_weight: bfloat16 [8192, 16384], P('tok', 'col'), may hold values from -0.0625 to 0.0625
- up_weight: bfloat16 [8192, 16384], P('tok', 'col'), may hold values from -0.0625 to 0.0625
- down_weight: bfloat16 [16384, 8192], P('col', 'tok'), may hold values from -0.046875 to 0.046875
- gate_delta: bfloat16 [4, 4, 4, 128, 128], P('tok', 'col'), may hold values from -0.29882812 to 0.29882812
- up_delta: bfloat16 [4, 4, 4, 128, 128], P('tok', 'col'), may hold values from -0.29882812 to 0.29882812
- down_delta: bfloat16 [4, 4, 4, 128, 128], P('tok', 'col'), may hold values from -0.29882812 to 0.29882812
- tile_index: int32 [4, 4, 3, 4, 3], P('tok', 'col'), may hold values from 0 to 31, as said below
Outputs:
- attended: bfloat16 [96, 8192], P(('rep', 'tok', 'col')), parts along dimension 0
- ffn_out: bfloat16 [96, 8192], P(('rep', 'col'), 'tok'), parts along dimension 0
There are 2 independent parts, one for each index of `rep`. A program takes and returns all parts, laid end to end along the dimension named above; an argument that names none is the same for every part. Nothing has to cross between parts.
Inputs may be any that keep to these rules, and one draw needn't show every extreme that they name: `route_list`: every request is placed in exactly one live slot of its own lane; each source device places at most one request with each owner of its lane; some owner of every lane holds 3 requests; entries of empty slots are 0. `route_count`: the counts of a lane sum to 8; some count of every lane is 3. `tile_index`: variant ids are below 2; row and column blocks of gate and up tiles are below 16 and 32, of down tiles the other way round; tiles may repeat.
All inputs are finite; a program needn't handle non-finite values.
Results may differ from a plain program's by a relative error of at most 0.025.
Values may be sent and summed in bfloat16 or wider, within the bound.
No kernel may reach another device: no remote copies, remote signals or barrier semaphores. Data moves between devices by JAX's collectives and lax.ppermute only.
A program may use at most 128 MiB of HBM per device.

v0:
```python
import jax
import jax.numpy as jnp
from jax import lax
from jax.sharding import PartitionSpec as P

HEADS = 64
KV_HEADS = 8
HEAD_DIM = 128


def attend(slot_rows, key_cache, live_mask):
    slot_count = slot_rows.shape[0]
    group_size = HEADS // KV_HEADS
    query_width = HEADS * HEAD_DIM
    pair_width = KV_HEADS * HEAD_DIM
    queries = slot_rows[:, :query_width].reshape(slot_count, KV_HEADS, group_size, HEAD_DIM)
    own_keys = slot_rows[:, query_width : query_width + pair_width].reshape(
        slot_count, KV_HEADS, HEAD_DIM
    )
    own_values = (
        slot_rows[:, query_width + pair_width :]
        .astype(jnp.float32)
        .reshape(slot_count, KV_HEADS, HEAD_DIM)
    )
    cached_keys = key_cache[:, :, :pair_width].reshape(slot_count, -1, KV_HEADS, HEAD_DIM)
    cached_values = key_cache[:, :, pair_width:].reshape(slot_count, -1, KV_HEADS, HEAD_DIM)
    score_scale = HEAD_DIM ** (-0.5)
    past_scores = (
        jnp.einsum("skgd,sjkd->skgj", queries, cached_keys, preferred_element_type=jnp.float32)
        * score_scale
    )
    own_scores = (
        jnp.einsum("skgd,skd->skg", queries, own_keys, preferred_element_type=jnp.float32)
        * score_scale
    )
    row_top = jnp.maximum(jnp.max(past_scores, axis=-1), own_scores)
    past_exp = jnp.exp(past_scores - row_top[..., None])
    own_exp = jnp.exp(own_scores - row_top)
    weight_total = jnp.sum(past_exp, axis=-1) + own_exp
    past_weights = (past_exp / weight_total[..., None]).astype(jnp.bfloat16)
    own_weights = (own_exp / weight_total).astype(jnp.bfloat16)
    mixed = jnp.einsum(
        "skgj,sjkd->skgd", past_weights, cached_values, preferred_element_type=jnp.float32
    )
    mixed = mixed + own_weights.astype(jnp.float32)[..., None] * own_values[:, :, None, :]
    return (mixed.reshape(slot_count, query_width) * live_mask[:, None].astype(jnp.float32)).astype(
        jnp.bfloat16
    )


def normalize(attended, norm_gain):
    values = attended.astype(jnp.float32)
    spread = jnp.mean(values * values, axis=-1, keepdims=True)
    return (values * lax.rsqrt(spread + 1e-06) * norm_gain).astype(jnp.bfloat16)


def add_tiles(partial_value, source, delta_tiles, tile_list, per_variant, out_base):
    block_width = delta_tiles.shape[-1]
    for slot_tile in range(delta_tiles.shape[0]):
        first_row = tile_list[slot_tile, 0] * per_variant
        block_in = lax.dynamic_slice(
            source, (first_row, tile_list[slot_tile, 1] * block_width), (per_variant, block_width)
        )
        product = jnp.dot(block_in, delta_tiles[slot_tile], preferred_element_type=jnp.float32)
        position = (first_row, out_base + tile_list[slot_tile, 2] * block_width)
        current = lax.dynamic_slice(partial_value, position, (per_variant, block_width))
        partial_value = lax.dynamic_update_slice(partial_value, current + product, position)
    return partial_value


def local(
    request_rows,
    key_cache,
    route_list,
    route_count,
    norm_gain,
    gate_weight,
    up_weight,
    down_weight,
    gate_delta,
    up_delta,
    down_delta,
    tile_index,
):
    tok_count = lax.axis_size("tok")
    col_count = lax.axis_size("col")
    tok_index = lax.axis_index("tok")
    capacity = key_cache.shape[0]
    lane_lists = route_list[:, 0, :]
    lane_counts = route_count[:, 0]
    own_list = lax.dynamic_index_in_dim(lane_lists, tok_index, 0, keepdims=False)
    own_count = lax.dynamic_index_in_dim(lane_counts, tok_index, 0, keepdims=False)
    positions = jnp.arange(capacity, dtype=jnp.int32)
    live_mask = positions < own_count
    everything = lax.all_gather(request_rows, "tok", axis=0, tiled=True)
    slot_rows = jnp.take(everything, own_list, axis=0)
    slot_rows = jnp.where(live_mask[:, None], slot_rows, jnp.zeros((), slot_rows.dtype))
    attended = attend(slot_rows, key_cache, live_mask)
    normed = normalize(attended, norm_gain)
    model_width = normed.shape[1]
    pieces = lax.all_to_all(
        normed.reshape(1, capacity, model_width), "tok", split_axis=2, concat_axis=0, tiled=True
    )
    feature_width = pieces.shape[2]
    lane_rows = lax.all_gather(
        pieces.reshape(tok_count, 1, capacity, feature_width), "col", axis=1, tiled=True
    )
    all_rows = lane_rows.reshape(-1, feature_width)
    slot_total = all_rows.shape[0]
    per_variant = 2 * col_count * capacity
    gate_term = add_tiles(
        jnp.dot(all_rows, gate_weight, preferred_element_type=jnp.float32),
        all_rows,
        gate_delta[0, 0],
        tile_index[0, 0, 0],
        per_variant,
        0,
    )
    up_term = add_tiles(
        jnp.dot(all_rows, up_weight, preferred_element_type=jnp.float32),
        all_rows,
        up_delta[0, 0],
        tile_index[0, 0, 1],
        per_variant,
        0,
    )
    gate_sum, up_sum = (
        lax.psum(gate_term.astype(jnp.bfloat16), "tok").astype(jnp.float32),
        lax.psum(up_term.astype(jnp.bfloat16), "tok").astype(jnp.float32),
    )
    hidden = (jax.nn.silu(gate_sum) * up_sum).astype(jnp.bfloat16)
    down_extra = add_tiles(
        jnp.zeros((slot_total, down_weight.shape[1]), jnp.float32),
        hidden,
        down_delta[0, 0],
        tile_index[0, 0, 2],
        per_variant,
        0,
    )
    ffn_share = lax.psum_scatter(
        (jnp.dot(hidden, down_weight, preferred_element_type=jnp.float32) + down_extra).astype(
            jnp.bfloat16
        ),
        "col",
        scatter_dimension=0,
        tiled=True,
    )
    return (attended, ffn_share)


def solution(mesh):
    in_specs = (
        P(("rep", "tok", "col"), None),
        P(("rep", "tok", "col"), None, None),
        P("rep", "col", None),
        P("rep", "col"),
        P(),
        P("tok", "col"),
        P("tok", "col"),
        P("col", "tok"),
        P("tok", "col", None, None, None),
        P("tok", "col", None, None, None),
        P("tok", "col", None, None, None),
        P("tok", "col", None, None, None),
    )
    out_specs = (P(("rep", "tok", "col"), None), P(("rep", "col"), "tok"))
    return jax.shard_map(local, mesh=mesh, in_specs=in_specs, out_specs=out_specs, check_vma=False)
```

profile of v0, /device:TPU:0, one launch (start us, length us, event | category | flops | bytes accessed | tf_op | source)
XLA Modules:
  0.0 220.6 jit_solution(1132018011714848766)
XLA Ops:
  7.2 1.2 constant_dynamic-slice_fusion.1
  9.3 6.9 %all-gather = bf16[4,2,10240]{2,1,0:T(2,128)(2,1)S(1)} all-gather(bf16[1,2,10240]{2,1,0:T(2,128)(2,1)} %bitcast.139), channel_id=1, replica_groups=mesh['rep'=2,'tok'=4,'col'=4] {'tok'}, dimensions={0}, use_global_device_ids=true | all-gather | bytes 204800 | tf_op jit(solution)/shard_map/all_gather | solution.py:95
  17.7 1.0 slice_bitcast_fusion.1
  19.7 0.9 multiply_convert_fusion
  20.6 6.9 %copy.40 = bf16[1,3,8192]{1,0,2:T(2,128)(2,1)} copy(bf16[1,3,8192]{2,1,0:T(4,128)(2,1)S(1)} %multiply_convert_fusion) | data formatting | bytes 98304 | tf_op jit(solution)/shard_map/convert_element_type | solution.py:54
  28.0 45.2 %reduce.4 = bf16[8192,3]{1,0:T(8,128)(2,1)S(1)} reduce(bf16[8192,1,3]{2,1,0:T(2,128)(2,1)} %bitcast.133, bf16[]{:T(256)} %broadcast.128), dimensions={1}, to_apply=%bitcast.117.reduce_sub_computation | reduce | bytes 98306
  73.2 3.8 %reshape.296 = bf16[4,2,3072]{2,1,0:T(2,128)(2,1)} reshape(bf16[8192,3]{1,0:T(8,128)(2,1)S(1)} %reduce.4) | data formatting | bytes 98304
  77.0 3.3 %all-to-all-start = ((bf16[4,2,3072]{2,1,0:T(2,128)(2,1)}), bf16[4,2,3072]{2,1,0:T(2,128)(2,1)S(1)}, u32[]{:S(2)}, u32[]{:S(2)}) async-start(bf16[4,2,3072]{2,1,0:T(2,128)(2,1)} %reshape.296), calls=%async_computation | async-start | bytes 98304 | tf_op jit(solution)/shard_map/all_to_all | solution.py:101
  80.3 0.7 fusion.72
  81.1 0.7 fusion.74
  97.8 5.4 %reshape.297 = bf16[8192,1,3]{2,1,0:T(2,128)(2,1)} reshape(bf16[4,2,3072]{2,1,0:T(2,128)(2,1)S(1)} %all-to-all-done) | data formatting | bytes 98304
  103.1 8.1 %copy.41 = bf16[1,3,8192]{2,1,0:T(4,128)(2,1)S(1)} copy(bf16[1,3,8192]{1,0,2:T(2,128)(2,1)} %bitcast.134) | data formatting | bytes 98304 | tf_op jit(solution)/shard_map/all_to_all | solution.py:101
  111.3 14.3 %all_gather.7 = bf16[4,4,3,2048]{3,0,2,1:T(4,128)(2,1)S(1)} all-gather(bf16[4,1,3,2048]{3,0,2,1:T(4,128)(2,1)S(1)} %bitcast.136), channel_id=1, replica_groups=mesh['rep'=2,'tok'=4,'col'=4] {'col'}, dimensions={1}, use_global_device_ids=true | all-gather | bytes 245760 | tf_op jit(solution)/shard_map/all_gather | solution.py:105
  125.9 8.8 %fusion.77 = f32[48,4096]{1,0:T(8,128)S(1)} fusion(bf16[48,2048]{1,0:T(8,128)(2,1)S(1)} %reshape.277, bf16[2048,4096]{1,0:T(8,128)(2,1)} %param.17), kind=kOutput, calls=%fused_computation.119 | convolution fusion | flops 805306368 | bytes 17760256 | tf_op jit(solution)/shard_map/dot_general | solution.py:112
  135.3 0.8 convert_element_type.84
  136.1 8.8 %fusion.78 = f32[48,4096]{1,0:T(8,128)S(1)} fusion(bf16[48,2048]{1,0:T(8,128)(2,1)S(1)} %reshape.277, bf16[2048,4096]{1,0:T(8,128)(2,1)} %param.18), kind=kOutput, calls=%fused_computation.120 | convolution fusion | flops 805306368 | bytes 17760256 | tf_op jit(solution)/shard_map/dot_general | solution.py:120
  145.5 0.8 convert_element_type.86
  146.4 0.7 fusion.73
  154.7 28.5 %all-reduce.5.cloned.1.call-done = (bf16[48,4096]{1,0:T(8,128)(2,1)}, bf16[48,4096]{1,0:T(8,128)(2,1)}) async-done(((bf16[48,4096]{1,0:T(8,128)(2,1)}, bf16[48,4096]{1,0:T(8,128)(2,1)}), (bf16[48,4096]{1,0:T(8,128)(2,1)}, bf16[48,4096]{1,0:T(8,128)(2,1)})) %all-reduce.5.cloned.1.call-update) | async-done | bytes 786448 | tf_op jit(solution)/shard_map/psum | solution.py:129
  183.2 1.3 fusion.17
  185.1 8.8 %fusion.1 = bf16[48,2048]{1,0:T(8,128)(2,1)S(1)} fusion(f32[48,2048]{1,0:T(8,128)S(1)} %fusion.2, bf16[48,4096]{1,0:T(8,128)(2,1)S(1)} %fusion.17, bf16[4096,2048]{1,0:T(8,128)(2,1)} %param.19), kind=kOutput, calls=%fused_computation.2 | convolution fusion | flops 805502976 | bytes 17760256 | tf_op jit(solution)/shard_map/dot_general | solution.py:141
  194.0 14.7 %fusion = bf16[16,2048]{1,0:T(8,128)(2,1)S(1)} fusion(bf16[48,2048]{1,0:T(8,128)(2,1)S(1)} %fusion.1), kind=kCustom, calls=%all-reduce-scatter | all-reduce-scatter fusion | flops 131073 | bytes 262656
  208.8 2.2 collective-permute-start
  210.9 0.7 fusion.18
  (61 shorter events, 8.5 us)
Async XLA Ops:
  7.2 1.3 copy-start
  77.0 20.8 %all-to-all-start = ((bf16[4,2,3072]{2,1,0:T(2,128)(2,1)}), bf16[4,2,3072]{2,1,0:T(2,128)(2,1)S(1)}, u32[]{:S(2)}, u32[]{:S(2)}) async-start(bf16[4,2,3072]{2,1,0:T(2,128)(2,1)} %reshape.296), calls=%async_computation | async-start | bytes 98304 | tf_op jit(solution)/shard_map/all_to_all | solution.py:101
  80.2 103.0 %all-reduce.5.cloned.1.call-start = ((), (), s32[]{:S(2)}) async-start(), calls=%async_computation.1 | async-start | bytes 1572864 | tf_op jit(solution)/shard_map/psum | solution.py:129
  97.7 37.0 %copy-start.2 = (bf16[1,1,4,128,128]{4,3,2,1,0:T(8,128)(2,1)S(1)}, bf16[1,1,4,128,128]{4,3,2,1,0:T(8,128)(2,1)}, u32[]{:S(2)}) copy-start(bf16[1,1,4,128,128]{4,3,2,1,0:T(8,128)(2,1)} %param.20) | copy-start | bytes 393220
  134.8 10.2 %copy-start.3 = (bf16[1,1,4,128,128]{4,3,2,1,0:T(8,128)(2,1)S(1)}, bf16[1,1,4,128,128]{4,3,2,1,0:T(8,128)(2,1)}, u32[]{:S(2)}) copy-start(bf16[1,1,4,128,128]{4,3,2,1,0:T(8,128)(2,1)} %param.21) | copy-start | bytes 393220
  134.8 49.8 %copy-start.4 = (bf16[1,1,4,128,128]{4,3,2,1,0:T(8,128)(2,1)S(1)}, bf16[1,1,4,128,128]{4,3,2,1,0:T(8,128)(2,1)}, u32[]{:S(2)}) copy-start(bf16[1,1,4,128,128]{4,3,2,1,0:T(8,128)(2,1)} %param.22) | copy-start | bytes 393220
  136.1 77.6 %copy-start.1 = (s32[4,1,3]{0,1,2:T(1,128)S(1)}, s32[4,1,3]{0,1,2:T(1,128)}, u32[]{:S(2)}) copy-start(s32[4,1,3]{0,1,2:T(1,128)} %param.14) | copy-start | bytes 148
  145.0 66.7 %copy-start.5 = (u32[32]{0:T(128)S(1)}, u32[32]{0:T(128)}, u32[]{:S(2)}) copy-start(u32[32]{0:T(128)} %constant.107) | copy-start | bytes 388
  208.8 4.1 %collective-permute-start = (bf16[12,2048]{1,0:T(8,128)(2,1)S(1)}, bf16[12,2048]{1,0:T(8,128)(2,1)S(1)}, u32[]{:S(2)}, u32[]{:S(2)}) collective-permute-start(bf16[12,2048]{1,0:T(8,128)(2,1)S(1)} %slice.241), channel_id=1, source_target_pairs={{0,1},{1,2},{2,3},{4,5},{5,6},{6,7},{8,9},{9,10},{10,11},{12,13},{... | collective-permute-start | bytes 147464
Sparse Core Ops, SparseCore 0:
  146.4 36.7 all-reduce.4
where the time goes:
time: 222 us; the launch traced here: 221 us
  other arithmetic  51.4 us (23%)
  between operations  37.7 us (17%)
  blocking collectives  35.9 us (16%)
  local copies, waits for them, and re-layouts  32.8 us (15%)
  matrix products  28.8 us (13%)
  waiting for transfers between devices  28.5 us (13%)
  starting transfers between devices  5.48 us (2%)
    unnamed x1, other arithmetic  45.2 us
    psum x1, waiting for transfers between devices, local(): lax.psum(up_term.astype(jnp.bfloat16), 'tok').astype(jnp.float32)  28.5 us
    unnamed x1, blocking collectives  14.7 us
    all_gather x1, blocking collectives, local(): lax.all_gather(pieces.reshape(tok_count, 1, capacity, feature_width), 'co...  14.3 us
    unnamed x23, local copies, waits for them, and re-layouts  12.2 us
    dot_general x1, matrix products, local(): jnp.dot(hidden, down_weight, preferred_element_type=jnp.float32)  8.83 us
    dot_general x1, matrix products, local(): jnp.dot(all_rows, up_weight, preferred_element_type=jnp.float32)  8.82 us
    dot_general x1, matrix products, local(): jnp.dot(all_rows, gate_weight, preferred_element_type=jnp.float32)  8.8 us
  transfers between devices with their start and end apart: 3, of which 1 were waited for; matrix products, arithmetic and copies ran while one was open for 2% of the time, Pallas kernels for 0%

commit v1 on v0

v1 whole, which is shorter than its diff:
```python
import functools

import jax
import jax.numpy as jnp
from jax import lax
from jax.experimental import pallas as pl
from jax.experimental.pallas import tpu as pltpu
from jax.sharding import PartitionSpec as P

HEADS = 64
KV_HEADS = 8
HEAD_DIM = 128
GROUP = HEADS // KV_HEADS
MIB = 1 << 20
BF16 = jnp.bfloat16
F32 = jnp.float32
VMEM = pltpu.VMEM
HBM = pltpu.HBM
SMEM = pltpu.SMEM


def call(kernel, name, ins, outs, scratch=(), limit=8, cost=None):
    arrays = [pltpu.with_memory_space_constraint(a, s) if s is not SMEM else a for a, s in ins]
    return pl.pallas_call(
        kernel,
        name=name,
        in_specs=[pl.BlockSpec(memory_space=s) for _, s in ins],
        out_specs=[pl.BlockSpec(memory_space=VMEM) for _ in outs],
        out_shape=[VMEM(shape, dtype) for shape, dtype in outs],
        scratch_shapes=list(scratch),
        cost_estimate=cost,
        compiler_params=pltpu.CompilerParams(vmem_limit_bytes=limit * MIB),
    )(*arrays)


class Sizes:
    def __init__(self, toks, cols, cap):
        self.toks, self.cols, self.cap = toks, cols, cap
        self.heads = HEADS // toks
        self.kvs = max(1, self.heads // GROUP)
        self.group = self.heads // self.kvs
        self.lane_slots = toks * cap
        self.rows = toks * cols * cap
        self.req_rows = -(-(self.heads + 2 * self.kvs) // 16) * 16
        self.blocks = 2 * self.kvs
        self.pieces = 2 * self.req_rows // 16
        self.cache_rows = None

    def first_kv(self, tok):
        return tok * self.heads // GROUP


def pack_kernel(z, ctx, req_ref, cache_ref, *rest):
    outs, (wide, rows, sems) = rest[: z.toks], rest[z.toks :]
    tok = lax.axis_index("tok")
    width = z.kvs * HEAD_DIM
    cache_rows = z.cap * ctx
    pairs = KV_HEADS * HEAD_DIM
    copies = []
    for s in range(z.toks):
        first = pl.multiple_of(z.first_kv(tok ^ s) * HEAD_DIM, HEAD_DIM)
        for half in range(2):
            for k in range(z.cap):
                copy = pltpu.make_async_copy(
                    cache_ref.at[k, :, pl.ds(half * pairs + first, width)],
                    outs[s].at[pl.ds(k * ctx, ctx), pl.ds(half * width, width)],
                    sems.at[s, half, k],
                )
                copy.start()
                copies.append(copy)
    wide[...] = req_ref[...].astype(F32)
    rows[...] = jnp.zeros_like(rows)
    for s in range(z.toks):
        to = tok ^ s
        starts = [(to * z.heads + h) * HEAD_DIM for h in range(z.heads)]
        for half in range(2):
            starts += [
                HEADS * HEAD_DIM + half * pairs + (z.first_kv(to) + j) * HEAD_DIM
                for j in range(z.kvs)
            ]
        for r in range(2):
            for n, start in enumerate(starts):
                rows[r * z.req_rows + n : r * z.req_rows + n + 1, :] = wide[
                    r : r + 1, pl.ds(pl.multiple_of(start, HEAD_DIM), HEAD_DIM)
                ]
        for p in range(z.pieces):
            at, lane = cache_rows + p // z.blocks * 16, p % z.blocks * HEAD_DIM
            outs[s][at : at + 16, lane : lane + HEAD_DIM] = rows[p * 16 : p * 16 + 16, :].astype(BF16)
    for copy in copies:
        copy.wait()


def attend_kernel(z, ctx, list_ref, count_ref, gain_ref, *rest):
    pieces, rest = rest[: z.toks], rest[z.toks :]
    send_ref, back_refs = rest[0], rest[1 : 1 + z.toks]
    cache, req, query, own_key, own_value, alive, mixed_all = rest[1 + z.toks :]
    tok = lax.axis_index("tok")
    cache_rows = z.cap * ctx
    for s in range(z.toks):
        source = tok ^ s
        cache[source] = pieces[s][:cache_rows, :]
        for p in range(z.pieces):
            at, lane = cache_rows + p // z.blocks * 16, p % z.blocks * HEAD_DIM
            r, part = p * 16 // z.req_rows, p * 16 % z.req_rows
            req[source * 2 + r, part : part + 16, :] = pieces[s][
                at : at + 16, lane : lane + HEAD_DIM
            ].astype(F32)
    for g in range(z.toks):
        for k in range(z.cap):
            live = (k < count_ref[g, 0]).astype(F32)
            rows = req[list_ref[g, 0, k]] * live
            at = (g * z.cap + k) * z.group
            for j in range(z.kvs):
                query[j, at : at + z.group, :] = rows[j * z.group : (j + 1) * z.group, :]
                key, value = z.heads + j, z.heads + z.kvs + j
                own_key[j, at : at + z.group, :] = jnp.broadcast_to(
                    rows[key : key + 1, :], (z.group, HEAD_DIM)
                )
                own_value[j, at : at + z.group, :] = jnp.broadcast_to(
                    rows[value : value + 1, :], (z.group, HEAD_DIM)
                )
            alive[at : at + z.group, :] = jnp.full((z.group, HEAD_DIM), live, F32)
    many, keys = z.lane_slots * z.group, z.toks * cache_rows
    row_slot = lax.broadcasted_iota(jnp.int32, (many, keys), 0) // z.group
    key_slot = lax.broadcasted_iota(jnp.int32, (many, keys), 1) // ctx
    same = row_slot == key_slot
    scale = HEAD_DIM ** (-0.5)
    for j in range(z.kvs):
        cached_keys = cache[:, :, j * HEAD_DIM : (j + 1) * HEAD_DIM].reshape(keys, HEAD_DIM)
        at = (z.kvs + j) * HEAD_DIM
        cached_values = cache[:, :, at : at + HEAD_DIM].reshape(keys, HEAD_DIM)
        past = (
            lax.dot_general(
                query[j].astype(BF16),
                cached_keys,
                (((1,), (1,)), ((), ())),
                preferred_element_type=F32,
            )
            * scale
        )
        own = jnp.sum(query[j] * own_key[j], axis=-1, keepdims=True) * scale
        top = jnp.maximum(jnp.max(jnp.where(same, past, -jnp.inf), axis=-1, keepdims=True), own)
        past_exp = jnp.where(same, jnp.exp(jnp.where(same, past - top, 0.0)), 0.0)
        own_exp = jnp.exp(own - top)
        total = jnp.sum(past_exp, axis=-1, keepdims=True) + own_exp
        weights = (past_exp / total).astype(BF16)
        own_weight = (own_exp / total).astype(BF16).astype(F32)
        mixed = jnp.dot(weights, cached_values, preferred_element_type=F32)
        mixed = (mixed + own_weight * own_value[j]) * alive[...]
        mixed_all[j * many : (j + 1) * many, :] = mixed.astype(BF16).astype(F32)
    block = z.cap * z.group
    for s in range(z.toks):
        for j in range(z.kvs):
            at = pl.multiple_of(j * many + (tok ^ s) * block, block if block % 8 == 0 else 4)
            back_refs[s][j * block : (j + 1) * block, :] = mixed_all[pl.ds(at, block), :].astype(BF16)
    count = z.kvs * z.lane_slots
    wide = z.group * HEAD_DIM
    row_kv = lax.broadcasted_iota(jnp.int32, (count, HEAD_DIM), 0) // z.lane_slots
    squares = jnp.zeros((count, HEAD_DIM), F32)
    for h in range(z.group):
        values = mixed_all[pl.ds(h, count, stride=z.group), :]
        squares = squares + values * values
        gain = jnp.zeros((count, HEAD_DIM), F32)
        for j in range(z.kvs):
            at = pl.multiple_of(tok * z.heads * HEAD_DIM, HEAD_DIM) + (j * z.group + h) * HEAD_DIM
            gain = jnp.where(row_kv == j, gain_ref[:, pl.ds(at, HEAD_DIM)], gain)
        send_ref[:, h * HEAD_DIM : (h + 1) * HEAD_DIM] = (values * gain).astype(BF16)
    high, low = halves(jnp.sum(squares, axis=-1, keepdims=True))
    send_ref[:, wide:] = two_lanes(high, low, count)


def halves(value):
    high = value.astype(BF16).astype(F32)
    return high, value - high


def two_lanes(high, low, rows):
    lane = lax.broadcasted_iota(jnp.int32, (rows, HEAD_DIM), 1)
    return jnp.where(lane == 0, high, jnp.where(lane == 1, low, 0.0)).astype(BF16)


def slot_of_row(z, col, shape):
    row = lax.broadcasted_iota(jnp.int32, shape, 0)
    return ((row // z.lane_slots) ^ col) * z.lane_slots + row % z.lane_slots


def tile_terms(z, col, source, delta_ref, index_ref, matrix, extra, out_base):
    side = delta_ref.shape[-1]
    variant = slot_of_row(z, col, (z.rows, side)) // (2 * z.cols * z.cap)
    for n in range(delta_ref.shape[2]):
        at = pl.multiple_of(index_ref[0, 0, matrix, n, 1] * side, side)
        to = pl.multiple_of(out_base + index_ref[0, 0, matrix, n, 2] * side, side)
        rows = jnp.where(variant == index_ref[0, 0, matrix, n, 0], source[:, pl.ds(at, side)], 0)
        extra[:, pl.ds(to, side)] += jnp.dot(
            rows.astype(BF16), delta_ref[0, 0, n], preferred_element_type=F32
        )


def project_kernel(z, step, index_ref, gate_delta, up_delta, gate_ref, up_ref, *rest):
    pieces, rest = rest[: z.cols], rest[z.cols :]
    send_ref, keep_ref, source, extra, weights, sems = rest
    col, core = lax.axis_index("col"), lax.axis_index("tok") % 2
    units = gate_ref.shape[1]
    half = units // 2
    jobs = []
    for out_ref, side in ((send_ref, 1 - core), (keep_ref, core)):
        for m, ref in enumerate((gate_ref, up_ref)):
            for at in range(0, half, step):
                jobs.append((out_ref, m, ref, pl.multiple_of(side * half, half) + at, m * half + at))
    copies = []
    for n, (_, m, ref, at, _) in enumerate(jobs):
        copy = pltpu.make_async_copy(ref.at[:, pl.ds(at, step)], weights.at[n], sems.at[n])
        copy.start()
        copies.append(copy)
    extra[...] = jnp.zeros_like(extra)
    count = z.kvs * z.lane_slots
    wide = z.group * HEAD_DIM
    slot = slot_of_row(z, col, (z.rows, count))
    lane_of, owner = slot // z.cap % z.cols, slot // (z.cols * z.cap)
    column = lax.broadcasted_iota(jnp.int32, (z.rows, count), 1)
    totals = jnp.zeros((z.rows, HEAD_DIM), F32)
    for j in range(z.kvs):
        place = j * z.lane_slots + owner * z.cap + slot % z.cap
        found = jnp.zeros((z.rows, wide + HEAD_DIM), F32)
        for s in range(z.cols):
            pick = ((lane_of == (col ^ s)) & (column == place)).astype(F32).astype(BF16)
            found += jnp.dot(pick, pieces[s][...], preferred_element_type=F32)
        source[:, j * wide : (j + 1) * wide] = found[:, :wide].astype(BF16)
        totals += found[:, wide:]
    high, low = halves(jnp.sum(totals, axis=-1, keepdims=True))
    send_ref[:, units:] = two_lanes(high, low, z.rows)
    keep_ref[:, units:] = two_lanes(high, low, z.rows)
    tile_terms(z, col, source, gate_delta, index_ref, 0, extra, 0)
    tile_terms(z, col, source, up_delta, index_ref, 1, extra, units)
    for n, (out_ref, m, _, at, to) in enumerate(jobs):
        copies[n].wait()
        value = jnp.dot(source[...], weights[n], preferred_element_type=F32)
        value += extra[:, pl.ds(m * units + at, step)]
        out_ref[:, to : to + step] = value.astype(BF16)


def add_kernel(z, mine, other, out_ref):
    units = mine.shape[1] - HEAD_DIM
    out_ref[:, :units] = (mine[:, :units].astype(F32) + other[:, :units].astype(F32)).astype(BF16)
    total = mine[:, units:].astype(F32) + other[:, units:].astype(F32)
    out_ref[:, units:] = two_lanes(*halves(jnp.sum(total, axis=-1, keepdims=True)), z.rows)


def hidden_kernel(z, width, *refs):
    parts, out_ref = refs[:-1], refs[-1]
    units = out_ref.shape[1]
    squares = sum(ref[:, 2 * units :].astype(F32) for ref in parts)
    squares = jnp.sum(squares, axis=-1, keepdims=True)
    scale = lax.rsqrt(squares * (1.0 / width) + 1e-06)
    step = min(units, 512)
    for at in range(0, units, step):
        gate = sum(ref[:, at : at + step].astype(F32) for ref in parts) * scale
        up = sum(ref[:, units + at : units + at + step].astype(F32) for ref in parts) * scale
        out_ref[:, at : at + step] = (jax.nn.silu(gate) * up).astype(BF16)


def down_kernel(z, step, index_ref, delta_ref, weight_ref, mine, other, *rest):
    outs, (source, extra, fold, weights, sems) = rest[: z.cols], rest[z.cols :]
    col, core = lax.axis_index("col"), lax.axis_index("tok") % 2
    width = weight_ref.shape[1]
    copies = []
    for n in range(width // step):
        copy = pltpu.make_async_copy(
            weight_ref.at[:, pl.ds(n * step, step)], weights.at[n], sems.at[n]
        )
        copy.start()
        copies.append(copy)
    half = mine.shape[1]
    source[:, pl.ds(pl.multiple_of(core * half, half), half)] = mine[...]
    source[:, pl.ds(pl.multiple_of((1 - core) * half, half), half)] = other[...]
    extra[...] = jnp.zeros_like(extra)
    tile_terms(z, col, source, delta_ref, index_ref, 2, extra, 0)
    for n in range(width // step):
        copies[n].wait()
        extra[:, n * step : (n + 1) * step] += jnp.dot(
            source[...], weights[n], preferred_element_type=F32
        )
    for s in range(z.cols):
        rows = slice(s * z.lane_slots, (s + 1) * z.lane_slots)
        fold[: z.lane_slots, :] = extra[rows, : width // 2]
        fold[z.lane_slots :, :] = extra[rows, width // 2 :]
        outs[s][...] = fold[...].astype(BF16)


def finish_kernel(z, *refs):
    parts, out_ref = refs[: z.cols], refs[z.cols]
    total = sum(ref[...].astype(F32) for ref in parts)
    half = total.shape[1]
    out_ref[:, :half] = total[: z.lane_slots].astype(BF16)
    out_ref[:, half:] = total[z.lane_slots :].astype(BF16)


def return_kernel(z, *refs):
    parts, out_ref, rows = refs[: z.toks], refs[z.toks], refs[z.toks + 1]
    tok = lax.axis_index("tok")
    block = z.cap * z.group
    for s in range(z.toks):
        rows[...] = parts[s][...].astype(F32)
        first = pl.multiple_of((tok ^ s) * z.heads * HEAD_DIM, HEAD_DIM)
        for j in range(z.kvs):
            for h in range(z.group):
                to = first + (j * z.group + h) * HEAD_DIM
                out_ref[:, pl.ds(to, HEAD_DIM)] = rows[
                    pl.ds(j * block + h, z.cap, stride=z.group), :
                ].astype(BF16)


def swap(array, axis, size, distance):
    return lax.ppermute(array, axis, [(i, i ^ distance) for i in range(size)])


def local(
    request_rows,
    key_cache,
    route_list,
    route_count,
    norm_gain,
    gate_weight,
    up_weight,
    down_weight,
    gate_delta,
    up_delta,
    down_delta,
    tile_index,
):
    toks, cols = lax.axis_size("tok"), lax.axis_size("col")
    cap, ctx = key_cache.shape[0], key_cache.shape[1]
    z = Sizes(toks, cols, cap)
    width = norm_gain.shape[0]
    cache_rows = cap * ctx
    lanes = 2 * z.kvs * HEAD_DIM
    piece_rows = cache_rows + -(-z.pieces // z.blocks) * 16
    many = z.lane_slots * z.group

    pieces = call(
        functools.partial(pack_kernel, z, ctx),
        "pack",
        [(request_rows, VMEM), (key_cache, HBM)],
        [((piece_rows, lanes), BF16)] * toks,
        [
            pltpu.VMEM(request_rows.shape, F32),
            pltpu.VMEM((2 * z.req_rows, HEAD_DIM), F32),
            pltpu.SemaphoreType.DMA((toks, 2, cap)),
        ],
    )
    pieces = [pieces[0]] + [swap(pieces[s], "tok", toks, s) for s in range(1, toks)]
    block = z.kvs * cap * z.group
    send, *back = call(
        functools.partial(attend_kernel, z, ctx),
        "attend",
        [(route_list, SMEM), (route_count, SMEM), (norm_gain.reshape(1, width), VMEM)]
        + [(p, VMEM) for p in pieces],
        [((z.kvs * z.lane_slots, (z.group + 1) * HEAD_DIM), BF16)]
        + [((block, HEAD_DIM), BF16)] * toks,
        [
            pltpu.VMEM((toks, cache_rows, lanes), BF16),
            pltpu.VMEM((2 * toks, z.req_rows, HEAD_DIM), F32),
            pltpu.VMEM((z.kvs, many, HEAD_DIM), F32),
            pltpu.VMEM((z.kvs, many, HEAD_DIM), F32),
            pltpu.VMEM((z.kvs, many, HEAD_DIM), F32),
            pltpu.VMEM((many, HEAD_DIM), F32),
            pltpu.VMEM((z.kvs * many, HEAD_DIM), F32),
        ],
    )
    pieces = [send] + [swap(send, "col", cols, s) for s in range(1, cols)]
    features, units = gate_weight.shape
    step = min(units // 2, 1024)
    gate_up, kept = call(
        functools.partial(project_kernel, z, step),
        "project",
        [
            (tile_index, SMEM),
            (gate_delta, VMEM),
            (up_delta, VMEM),
            (gate_weight, HBM),
            (up_weight, HBM),
        ]
        + [(p, VMEM) for p in pieces],
        [((z.rows, units + HEAD_DIM), BF16)] * 2,
        [
            pltpu.VMEM((z.rows, features), BF16),
            pltpu.VMEM((z.rows, 2 * units), F32),
            pltpu.VMEM((2 * units // step, features, step), BF16),
            pltpu.SemaphoreType.DMA((2 * units // step,)),
        ],
        limit=48,
    )
    (total,) = call(
        functools.partial(add_kernel, z),
        "chip_sum",
        [(kept, VMEM), (swap(gate_up, "tok", toks, 1), VMEM)],
        [((z.rows, units + HEAD_DIM), BF16)],
    )
    parts = [total] + [swap(total, "tok", toks, 2 * s) for s in range(1, toks // 2)]
    (hidden,) = call(
        functools.partial(hidden_kernel, z, width),
        "hidden",
        [(p, VMEM) for p in parts],
        [((z.rows, units // 2), BF16)],
        limit=16,
    )
    back = [back[0]] + [swap(back[s], "tok", toks, s) for s in range(1, toks)]
    (attended,) = call(
        functools.partial(return_kernel, z),
        "attended",
        [(b, VMEM) for b in back],
        [((cap, width), BF16)],
        [pltpu.VMEM((block, HEAD_DIM), F32)],
    )
    out_width = down_weight.shape[1]
    step = min(out_width, 512)
    parts = call(
        functools.partial(down_kernel, z, step),
        "down",
        [
            (tile_index, SMEM),
            (down_delta, VMEM),
            (down_weight, HBM),
            (hidden, VMEM),
            (swap(hidden, "tok", toks, 1), VMEM),
        ],
        [((2 * z.lane_slots, out_width // 2), BF16)] * cols,
        [
            pltpu.VMEM((z.rows, units), BF16),
            pltpu.VMEM((z.rows, out_width), F32),
            pltpu.VMEM((2 * z.lane_slots, out_width // 2), F32),
            pltpu.VMEM((out_width // step, units, step), BF16),
            pltpu.SemaphoreType.DMA((out_width // step,)),
        ],
        limit=32,
    )
    parts = [parts[0]] + [swap(parts[s], "col", cols, s) for s in range(1, cols)]
    (ffn_out,) = call(
        functools.partial(finish_kernel, z),
        "finish",
        [(p, VMEM) for p in parts],
        [((z.lane_slots, out_width), BF16)],
    )
    return attended, ffn_out


def solution(mesh):
    in_specs = (
        P(("rep", "tok", "col"), None),
        P(("rep", "tok", "col"), None, None),
        P("rep", "col", None),
        P("rep", "col"),
        P(),
        P("tok", "col"),
        P("tok", "col"),
        P("col", "tok"),
        P("tok", "col", None, None, None),
        P("tok", "col", None, None, None),
        P("tok", "col", None, None, None),
        P("tok", "col", None, None, None),
    )
    out_specs = (P(("rep", "tok", "col"), None), P(("rep", "col"), "tok"))
    return jax.shard_map(local, mesh=mesh, in_specs=in_specs, out_specs=out_specs, check_vma=False)
```

time: 222 us -> 70.5 us (0.32)
  other arithmetic: 51.4 us -> 0 us
  between operations: 37.7 us -> 0.73 us
  blocking collectives: 35.9 us -> 0 us
  matrix products: 28.8 us -> 0 us
  local copies, waits for them, and re-layouts: 32.8 us -> 6.9 us
  Pallas kernels: 0 us -> 23.8 us
  starting transfers between devices: 5.48 us -> 15.9 us
  waiting for transfers between devices: 28.5 us -> 22.8 us
    unnamed x1 -> x0, other arithmetic: 45.2 us -> none
    dot_general x18 -> x0, matrix products: 28.8 us -> none  [the longest x1 8.83 us: local(): jnp.dot(hidden, down_weight, preferred_element_type=jnp.float32)]
    psum x1 -> x0, waiting for transfers between devices: 28.5 us -> none  [local(): lax.psum(up_term.astype(jnp.bfloat16), 'tok').astype(jnp.float32)]
    pallas_call x0 -> x8, Pallas kernels: none -> 23.8 us  [call(): pl.pallas_call(kernel, name=name, in_specs=[pl.BlockSpec(memory_space=s)...]
    ppermute x0 -> x15, waiting for transfers between devices: none -> 22.8 us  [swap(): return lax.ppermute(array, axis, [(i, i ^ distance) for i in range(size)])]
    all_gather x2 -> x0, blocking collectives: 21.2 us -> none  [the longest x1 14.3 us: local(): lax.all_gather(pieces.reshape(tok_count, 1, capacity, feature_width), 'co...]
    ppermute x0 -> x15, starting transfers between devices: none -> 15.9 us  [swap(): return lax.ppermute(array, axis, [(i, i ^ distance) for i in range(size)])]
    unnamed x1 -> x0, blocking collectives: 14.7 us -> none
  transfers between devices with their start and end apart: 3 -> 15, of which waited for: 1 -> 9; matrix products, arithmetic and copies ran while one was open for 2% -> 4% of each run, Pallas kernels for 0% -> 0%
where the time goes in v1:
time: 70.5 us; the launch traced here: 70.1 us
  Pallas kernels  23.8 us (34%)
  waiting for transfers between devices  22.8 us (32%)
  starting transfers between devices  15.9 us (23%)
  local copies, waits for them, and re-layouts  6.9 us (10%)
  between operations  0.73 us (1%)
    pallas_call x8, Pallas kernels, call(): pl.pallas_call(kernel, name=name, in_specs=[pl.BlockSpec(memory_space=s)...  23.8 us
    ppermute x15, waiting for transfers between devices, swap(): return lax.ppermute(array, axis, [(i, i ^ distance) for i in range(size)])  22.8 us
    ppermute x15, starting transfers between devices, swap(): return lax.ppermute(array, axis, [(i, i ^ distance) for i in range(size)])  15.9 us
    unnamed x15, local copies, waits for them, and re-layouts  6.9 us
  transfers between devices with their start and end apart: 15, of which 9 were waited for; matrix products, arithmetic and copies ran while one was open for 4% of the time, Pallas kernels for 0%

profile of v1, /device:TPU:0, one launch (start us, length us, event | category | flops | bytes accessed | tf_op | source)
XLA Modules:
  0.0 70.1 jit_solution(6367158713244575246)
XLA Ops:
  1.4 1.2 %pack.1 = (bf16[64,512]{1,0:T(8,128)(2,1)S(1)}, bf16[64,512]{1,0:T(8,128)(2,1)S(1)}, bf16[64,512]{1,0:T(8,128)(2,1)S(1)}, bf16[64,512]{1,0:T(8,128)(2,1)S(1)}) custom-call(bf16[2,10240]{1,0:T(2,128)(2,1)S(1)} %copy-done.3, bf16[3,16,2048]{2,1,0:T(8,128)(2,1)} %cache_ref.1), custom_call_target="tpu_custom_call" | custom-call | tf_op jit(solution)/shard_map/pack/pallas_call | solution.py:24
  3.1 2.6 %collective-permute-start.1 = (bf16[64,512]{1,0:T(8,128)(2,1)S(1)}, bf16[64,512]{1,0:T(8,128)(2,1)S(1)}, u32[]{:S(2)}, u32[]{:S(2)}) collective-permute-start(bf16[64,512]{1,0:T(8,128)(2,1)S(1)} %get-tuple-element.19), channel_id=1, source_target_pairs={{0,8},{4,12},{8,0},{12,4},{1,9},{5,13},{9,1},{13,5},{2,10},{6,14},... | collective-permute-start | bytes 196616 | tf_op jit(solution)/shard_map/ppermute | solution.py:314
  7.2 1.1 %collective-permute-done.1.rest_2_ = bf16[64,512]{1,0:T(8,128)(2,1)S(1)} collective-permute-done((bf16[64,512]{1,0:T(8,128)(2,1)S(1)}, bf16[64,512]{1,0:T(8,128)(2,1)S(1)}, u32[]{:S(2)}, u32[]{:S(2)}) %collective-permute-start.1) | collective-permute-done | bytes 65568 | tf_op jit(solution)/shard_map/ppermute | solution.py:314
  8.4 1.4 %collective-permute-done.2.rest_3_ = bf16[64,512]{1,0:T(8,128)(2,1)S(1)} collective-permute-done((bf16[64,512]{1,0:T(8,128)(2,1)S(1)}, bf16[64,512]{1,0:T(8,128)(2,1)S(1)}, u32[]{:S(2)}, u32[]{:S(2)}) %collective-permute-start.2) | collective-permute-done | bytes 65568 | tf_op jit(solution)/shard_map/ppermute | solution.py:314
  10.5 1.5 %attend.1 = (bf16[24,1152]{1,0:T(8,128)(2,1)S(1)}, bf16[48,128]{1,0:T(8,128)(2,1)S(1)}, bf16[48,128]{1,0:T(8,128)(2,1)S(1)}, bf16[48,128]{1,0:T(8,128)(2,1)S(1)}, bf16[48,128]{1,0:T(8,128)(2,1)S(1)}) custom-call(s32[4,1,3]{2,1,0:T(1,128)S(1)} %copy.14.list_ref, s32[4,1]{1,0:T(4,128)S(1)} %copy.15.count_ref, f32[1,8192]{1,0:T(1,128)S(1)} %bitcast.1, ...), custom_call_target="tpu_custom_call" | custom-call | tf_op jit(solution)/shard_map/attend/pallas_call | solution.py:24
  12.0 1.6 %collective-permute-start.6 = (bf16[24,1152]{1,0:T(8,128)(2,1)S(1)}, bf16[24,1152]{1,0:T(8,128)(2,1)S(1)}, u32[]{:S(2)}, u32[]{:S(2)}) collective-permute-start(bf16[24,1152]{1,0:T(8,128)(2,1)S(1)} %get-tuple-element.25.rest_0_), channel_id=1, source_target_pairs={{0,1},{1,0},{2,3},{3,2},{4,5},{5,4},{6,7},{7,6},{8,9},{9,8},{10,11... | collective-permute-start | bytes 165896 | tf_op jit(solution)/shard_map/ppermute | solution.py:314
  13.6 2.6 %collective-permute-start.7 = (bf16[24,1152]{1,0:T(8,128)(2,1)S(1)}, bf16[24,1152]{1,0:T(8,128)(2,1)S(1)}, u32[]{:S(2)}, u32[]{:S(2)}) collective-permute-start(bf16[24,1152]{1,0:T(8,128)(2,1)S(1)} %get-tuple-element.25.rest_0_), channel_id=1, source_target_pairs={{0,2},{1,3},{2,0},{3,1},{4,6},{5,7},{6,4},{7,5},{8,10},{9,11},{10,... | collective-permute-start | bytes 165896 | tf_op jit(solution)/shard_map/ppermute | solution.py:314
  16.5 0.8 %copy.17.index_ref = s32[1,1,3,4,3]{4,3,2,1,0:T(4,128)S(1)} copy(s32[1,1,3,4,3]{3,1,4,2,0:T(1,128)} %param.23) | data formatting | bytes 288 | tf_op args[11]
  17.2 2.7 %collective-permute-done.7.rest_2_ = bf16[24,1152]{1,0:T(8,128)(2,1)S(1)} collective-permute-done((bf16[24,1152]{1,0:T(8,128)(2,1)S(1)}, bf16[24,1152]{1,0:T(8,128)(2,1)S(1)}, u32[]{:S(2)}, u32[]{:S(2)}) %collective-permute-start.7) | collective-permute-done | bytes 55328 | tf_op jit(solution)/shard_map/ppermute | solution.py:314
  19.9 2.2 %collective-permute-done.8.rest_3_ = bf16[24,1152]{1,0:T(8,128)(2,1)S(1)} collective-permute-done((bf16[24,1152]{1,0:T(8,128)(2,1)S(1)}, bf16[24,1152]{1,0:T(8,128)(2,1)S(1)}, u32[]{:S(2)}, u32[]{:S(2)}) %collective-permute-start.8) | collective-permute-done | bytes 55328 | tf_op jit(solution)/shard_map/ppermute | solution.py:314
  22.2 0.9 %copy-done = bf16[1,1,4,128,128]{4,3,2,1,0:T(8,128)(2,1)S(1)} copy-done((bf16[1,1,4,128,128]{4,3,2,1,0:T(8,128)(2,1)S(1)}, bf16[1,1,4,128,128]{4,3,2,1,0:T(8,128)(2,1)}, u32[]{:S(2)}) %copy-start) | copy-done | bytes 131096
  23.1 0.9 %copy-done.1 = bf16[1,1,4,128,128]{4,3,2,1,0:T(8,128)(2,1)S(1)} copy-done((bf16[1,1,4,128,128]{4,3,2,1,0:T(8,128)(2,1)S(1)}, bf16[1,1,4,128,128]{4,3,2,1,0:T(8,128)(2,1)}, u32[]{:S(2)}) %copy-start.1) | copy-done | bytes 131096
  24.0 13.0 %project.1 = (bf16[48,4224]{1,0:T(8,128)(2,1)S(1)}, bf16[48,4224]{1,0:T(8,128)(2,1)S(1)}) custom-call(s32[1,1,3,4,3]{4,3,2,1,0:T(4,128)S(1)} %copy.17.index_ref, bf16[1,1,4,128,128]{4,3,2,1,0:T(8,128)(2,1)S(1)} %copy-done, bf16[1,1,4,128,128]{4,3,2,1,0:T(8,128)(2,1)S(1)} %copy-done.1, bf16[2048,4096]{1,0:T(8,128)(2,1)} %gate_ref.1, ...), custom_call_target="tpu_custom_call" | custom-call | tf_op jit(solution)/shard_map/project/pallas_call | solution.py:24
  37.1 1.7 %collective-permute-done.9.other = bf16[48,4224]{1,0:T(8,128)(2,1)S(1)} collective-permute-done((bf16[48,4224]{1,0:T(8,128)(2,1)S(1)}, bf16[48,4224]{1,0:T(8,128)(2,1)S(1)}, u32[]{:S(2)}, u32[]{:S(2)}) %collective-permute-start.9) | collective-permute-done | bytes 405536 | tf_op jit(solution)/shard_map/ppermute | solution.py:314
  39.0 1.4 %collective-permute-start.10 = (bf16[48,4224]{1,0:T(8,128)(2,1)S(1)}, bf16[48,4224]{1,0:T(8,128)(2,1)S(1)}, u32[]{:S(2)}, u32[]{:S(2)}) collective-permute-start(bf16[48,4224]{1,0:T(8,128)(2,1)S(1)} %chip_sum.1.refs_0_), channel_id=1, source_target_pairs={{0,8},{4,12},{8,0},{12,4},{1,9},{5,13},{9,1},{13,5},{2,10},{6,14},... | collective-permute-start | bytes 1216520 | tf_op jit(solution)/shard_map/ppermute | solution.py:314
  40.4 10.1 %collective-permute-done.10.refs_1_ = bf16[48,4224]{1,0:T(8,128)(2,1)S(1)} collective-permute-done((bf16[48,4224]{1,0:T(8,128)(2,1)S(1)}, bf16[48,4224]{1,0:T(8,128)(2,1)S(1)}, u32[]{:S(2)}, u32[]{:S(2)}) %collective-permute-start.10) | collective-permute-done | bytes 405536 | tf_op jit(solution)/shard_map/ppermute | solution.py:314
  50.8 1.4 %collective-permute-done.11.other = bf16[48,2048]{1,0:T(8,128)(2,1)S(1)} collective-permute-done((bf16[48,2048]{1,0:T(8,128)(2,1)S(1)}, bf16[48,2048]{1,0:T(8,128)(2,1)S(1)}, u32[]{:S(2)}, u32[]{:S(2)}) %collective-permute-start.11) | collective-permute-done | bytes 196640 | tf_op jit(solution)/shard_map/ppermute | solution.py:314
  52.2 7.5 %down.1 = (bf16[24,1024]{1,0:T(8,128)(2,1)S(1)}, bf16[24,1024]{1,0:T(8,128)(2,1)S(1)}, bf16[24,1024]{1,0:T(8,128)(2,1)S(1)}, bf16[24,1024]{1,0:T(8,128)(2,1)S(1)}) custom-call(s32[1,1,3,4,3]{4,3,2,1,0:T(4,128)S(1)} %copy.17.index_ref, bf16[1,1,4,128,128]{4,3,2,1,0:T(8,128)(2,1)S(1)} %copy-done.2, bf16[4096,2048]{1,0:T(8,128)(2,1)} %weight_ref.1, ...), custom_call_target="tpu_custom_call" | custom-call | tf_op jit(solution)/shard_map/down/pallas_call | solution.py:24
  59.8 2.0 %collective-permute-start.13 = (bf16[24,1024]{1,0:T(8,128)(2,1)S(1)}, bf16[24,1024]{1,0:T(8,128)(2,1)S(1)}, u32[]{:S(2)}, u32[]{:S(2)}) collective-permute-start(bf16[24,1024]{1,0:T(8,128)(2,1)S(1)} %get-tuple-element.30), channel_id=1, source_target_pairs={{0,2},{1,3},{2,0},{3,1},{4,6},{5,7},{6,4},{7,5},{8,10},{9,11},{10,... | collective-permute-start | bytes 147464 | tf_op jit(solution)/shard_map/ppermute | solution.py:314
  61.8 2.4 %collective-permute-start.14 = (bf16[24,1024]{1,0:T(8,128)(2,1)S(1)}, bf16[24,1024]{1,0:T(8,128)(2,1)S(1)}, u32[]{:S(2)}, u32[]{:S(2)}) collective-permute-start(bf16[24,1024]{1,0:T(8,128)(2,1)S(1)} %get-tuple-element.31), channel_id=1, source_target_pairs={{0,3},{1,2},{2,1},{3,0},{4,7},{5,6},{6,5},{7,4},{8,11},{9,10},{10,... | collective-permute-start | bytes 147464 | tf_op jit(solution)/shard_map/ppermute | solution.py:314
  64.2 1.3 %collective-permute-start.4 = (bf16[48,128]{1,0:T(8,128)(2,1)S(1)}, bf16[48,128]{1,0:T(8,128)(2,1)S(1)}, u32[]{:S(2)}, u32[]{:S(2)}) collective-permute-start(bf16[48,128]{1,0:T(8,128)(2,1)S(1)} %get-tuple-element.23), channel_id=1, source_target_pairs={{0,8},{4,12},{8,0},{12,4},{1,9},{5,13},{9,1},{13,5},{2,10},{6,14},... | collective-permute-start | bytes 36872 | tf_op jit(solution)/shard_map/ppermute | solution.py:314
  65.5 0.9 %collective-permute-start.5 = (bf16[48,128]{1,0:T(8,128)(2,1)S(1)}, bf16[48,128]{1,0:T(8,128)(2,1)S(1)}, u32[]{:S(2)}, u32[]{:S(2)}) collective-permute-start(bf16[48,128]{1,0:T(8,128)(2,1)S(1)} %get-tuple-element.24), channel_id=1, source_target_pairs={{0,12},{4,8},{8,4},{12,0},{1,13},{5,9},{9,5},{13,1},{2,14},{6,10},... | collective-permute-start | bytes 36872 | tf_op jit(solution)/shard_map/ppermute | solution.py:314
  66.5 1.4 %collective-permute-done.4.refs_2_ = bf16[48,128]{1,0:T(8,128)(2,1)S(1)} collective-permute-done((bf16[48,128]{1,0:T(8,128)(2,1)S(1)}, bf16[48,128]{1,0:T(8,128)(2,1)S(1)}, u32[]{:S(2)}, u32[]{:S(2)}) %collective-permute-start.4) | collective-permute-done | bytes 12320 | tf_op jit(solution)/shard_map/ppermute | solution.py:314
  67.9 0.8 %collective-permute-done.5.refs_3_ = bf16[48,128]{1,0:T(8,128)(2,1)S(1)} collective-permute-done((bf16[48,128]{1,0:T(8,128)(2,1)S(1)}, bf16[48,128]{1,0:T(8,128)(2,1)S(1)}, u32[]{:S(2)}, u32[]{:S(2)}) %collective-permute-start.5) | collective-permute-done | bytes 12320 | tf_op jit(solution)/shard_map/ppermute | solution.py:314
  (29 shorter events, 5.9 us)
Async XLA Ops:
  0.6 0.8 %copy-start.3 = (bf16[2,10240]{1,0:T(2,128)(2,1)S(1)}, bf16[2,10240]{1,0:T(2,128)(2,1)}, u32[]{:S(2)}) copy-start(bf16[2,10240]{1,0:T(2,128)(2,1)} %req_ref.1) | copy-start | bytes 122884
  2.6 4.7 %collective-permute-start = (bf16[64,512]{1,0:T(8,128)(2,1)S(1)}, bf16[64,512]{1,0:T(8,128)(2,1)S(1)}, u32[]{:S(2)}, u32[]{:S(2)}) collective-permute-start(bf16[64,512]{1,0:T(8,128)(2,1)S(1)} %get-tuple-element.18), channel_id=1, source_target_pairs={{0,4},{4,0},{8,12},{12,8},{1,5},{5,1},{9,13},{13,9},{2,6},{6,2},{1... | collective-permute-start | bytes 196616 | tf_op jit(solution)/shard_map/ppermute | solution.py:314
  3.1 5.3 %collective-permute-start.1 = (bf16[64,512]{1,0:T(8,128)(2,1)S(1)}, bf16[64,512]{1,0:T(8,128)(2,1)S(1)}, u32[]{:S(2)}, u32[]{:S(2)}) collective-permute-start(bf16[64,512]{1,0:T(8,128)(2,1)S(1)} %get-tuple-element.19), channel_id=1, source_target_pairs={{0,8},{4,12},{8,0},{12,4},{1,9},{5,13},{9,1},{13,5},{2,10},{6,14},... | collective-permute-start | bytes 196616 | tf_op jit(solution)/shard_map/ppermute | solution.py:314
  5.7 4.0 %collective-permute-start.2 = (bf16[64,512]{1,0:T(8,128)(2,1)S(1)}, bf16[64,512]{1,0:T(8,128)(2,1)S(1)}, u32[]{:S(2)}, u32[]{:S(2)}) collective-permute-start(bf16[64,512]{1,0:T(8,128)(2,1)S(1)} %get-tuple-element.20), channel_id=1, source_target_pairs={{0,12},{4,8},{8,4},{12,0},{1,13},{5,9},{9,5},{13,1},{2,14},{6,10},... | collective-permute-start | bytes 196616 | tf_op jit(solution)/shard_map/ppermute | solution.py:314
  9.7 0.8 %copy-start.4 = (f32[8192]{0:T(1024)S(1)}, f32[8192]{0:T(1024)}, u32[]{:S(2)}) copy-start(f32[8192]{0:T(1024)} %param.16) | copy-start | bytes 98308
  12.0 5.2 %collective-permute-start.6 = (bf16[24,1152]{1,0:T(8,128)(2,1)S(1)}, bf16[24,1152]{1,0:T(8,128)(2,1)S(1)}, u32[]{:S(2)}, u32[]{:S(2)}) collective-permute-start(bf16[24,1152]{1,0:T(8,128)(2,1)S(1)} %get-tuple-element.25.rest_0_), channel_id=1, source_target_pairs={{0,1},{1,0},{2,3},{3,2},{4,5},{5,4},{6,7},{7,6},{8,9},{9,8},{10,11... | collective-permute-start | bytes 165896 | tf_op jit(solution)/shard_map/ppermute | solution.py:314
  13.6 6.3 %collective-permute-start.7 = (bf16[24,1152]{1,0:T(8,128)(2,1)S(1)}, bf16[24,1152]{1,0:T(8,128)(2,1)S(1)}, u32[]{:S(2)}, u32[]{:S(2)}) collective-permute-start(bf16[24,1152]{1,0:T(8,128)(2,1)S(1)} %get-tuple-element.25.rest_0_), channel_id=1, source_target_pairs={{0,2},{1,3},{2,0},{3,1},{4,6},{5,7},{6,4},{7,5},{8,10},{9,11},{10,... | collective-permute-start | bytes 165896 | tf_op jit(solution)/shard_map/ppermute | solution.py:314
  16.2 6.0 %collective-permute-start.8 = (bf16[24,1152]{1,0:T(8,128)(2,1)S(1)}, bf16[24,1152]{1,0:T(8,128)(2,1)S(1)}, u32[]{:S(2)}, u32[]{:S(2)}) collective-permute-start(bf16[24,1152]{1,0:T(8,128)(2,1)S(1)} %get-tuple-element.25.rest_0_), channel_id=1, source_target_pairs={{0,3},{1,2},{2,1},{3,0},{4,7},{5,6},{6,5},{7,4},{8,11},{9,10},{10,... | collective-permute-start | bytes 165896 | tf_op jit(solution)/shard_map/ppermute | solution.py:314
  22.2 0.9 %copy-start = (bf16[1,1,4,128,128]{4,3,2,1,0:T(8,128)(2,1)S(1)}, bf16[1,1,4,128,128]{4,3,2,1,0:T(8,128)(2,1)}, u32[]{:S(2)}) copy-start(bf16[1,1,4,128,128]{4,3,2,1,0:T(8,128)(2,1)} %gate_delta.1) | copy-start | bytes 393220
  23.1 0.9 %copy-start.1 = (bf16[1,1,4,128,128]{4,3,2,1,0:T(8,128)(2,1)S(1)}, bf16[1,1,4,128,128]{4,3,2,1,0:T(8,128)(2,1)}, u32[]{:S(2)}) copy-start(bf16[1,1,4,128,128]{4,3,2,1,0:T(8,128)(2,1)} %up_delta.1) | copy-start | bytes 393220
  24.0 28.2 %copy-start.2 = (bf16[1,1,4,128,128]{4,3,2,1,0:T(8,128)(2,1)S(1)}, bf16[1,1,4,128,128]{4,3,2,1,0:T(8,128)(2,1)}, u32[]{:S(2)}) copy-start(bf16[1,1,4,128,128]{4,3,2,1,0:T(8,128)(2,1)} %delta_ref.1) | copy-start | bytes 393220
  37.0 1.8 %collective-permute-start.9 = (bf16[48,4224]{1,0:T(8,128)(2,1)S(1)}, bf16[48,4224]{1,0:T(8,128)(2,1)S(1)}, u32[]{:S(2)}, u32[]{:S(2)}) collective-permute-start(bf16[48,4224]{1,0:T(8,128)(2,1)S(1)} %get-tuple-element.27), channel_id=1, source_target_pairs={{0,4},{4,0},{8,12},{12,8},{1,5},{5,1},{9,13},{13,9},{2,6},{6,2},{1... | collective-permute-start | bytes 1216520 | tf_op jit(solution)/shard_map/ppermute | solution.py:314
  39.0 11.5 %collective-permute-start.10 = (bf16[48,4224]{1,0:T(8,128)(2,1)S(1)}, bf16[48,4224]{1,0:T(8,128)(2,1)S(1)}, u32[]{:S(2)}, u32[]{:S(2)}) collective-permute-start(bf16[48,4224]{1,0:T(8,128)(2,1)S(1)} %chip_sum.1.refs_0_), channel_id=1, source_target_pairs={{0,8},{4,12},{8,0},{12,4},{1,9},{5,13},{9,1},{13,5},{2,10},{6,14},... | collective-permute-start | bytes 1216520 | tf_op jit(solution)/shard_map/ppermute | solution.py:314
  50.7 1.5 %collective-permute-start.11 = (bf16[48,2048]{1,0:T(8,128)(2,1)S(1)}, bf16[48,2048]{1,0:T(8,128)(2,1)S(1)}, u32[]{:S(2)}, u32[]{:S(2)}) collective-permute-start(bf16[48,2048]{1,0:T(8,128)(2,1)S(1)} %hidden.1.mine), channel_id=1, source_target_pairs={{0,4},{4,0},{8,12},{12,8},{1,5},{5,1},{9,13},{13,9},{2,6},{6,2},{1... | collective-permute-start | bytes 589832 | tf_op jit(solution)/shard_map/ppermute | solution.py:314
  59.7 9.7 %collective-permute-start.12 = (bf16[24,1024]{1,0:T(8,128)(2,1)S(1)}, bf16[24,1024]{1,0:T(8,128)(2,1)S(1)}, u32[]{:S(2)}, u32[]{:S(2)}) collective-permute-start(bf16[24,1024]{1,0:T(8,128)(2,1)S(1)} %get-tuple-element.29), channel_id=1, source_target_pairs={{0,1},{1,0},{2,3},{3,2},{4,5},{5,4},{6,7},{7,6},{8,9},{9,8},{10,11... | collective-permute-start | bytes 147464 | tf_op jit(solution)/shard_map/ppermute | solution.py:314
  59.8 9.7 %collective-permute-start.13 = (bf16[24,1024]{1,0:T(8,128)(2,1)S(1)}, bf16[24,1024]{1,0:T(8,128)(2,1)S(1)}, u32[]{:S(2)}, u32[]{:S(2)}) collective-permute-start(bf16[24,1024]{1,0:T(8,128)(2,1)S(1)} %get-tuple-element.30), channel_id=1, source_target_pairs={{0,2},{1,3},{2,0},{3,1},{4,6},{5,7},{6,4},{7,5},{8,10},{9,11},{10,... | collective-permute-start | bytes 147464 | tf_op jit(solution)/shard_map/ppermute | solution.py:314
  61.8 7.6 %collective-permute-start.14 = (bf16[24,1024]{1,0:T(8,128)(2,1)S(1)}, bf16[24,1024]{1,0:T(8,128)(2,1)S(1)}, u32[]{:S(2)}, u32[]{:S(2)}) collective-permute-start(bf16[24,1024]{1,0:T(8,128)(2,1)S(1)} %get-tuple-element.31), channel_id=1, source_target_pairs={{0,3},{1,2},{2,1},{3,0},{4,7},{5,6},{6,5},{7,4},{8,11},{9,10},{10,... | collective-permute-start | bytes 147464 | tf_op jit(solution)/shard_map/ppermute | solution.py:314
  64.2 1.3 %collective-permute-start.3 = (bf16[48,128]{1,0:T(8,128)(2,1)S(1)}, bf16[48,128]{1,0:T(8,128)(2,1)S(1)}, u32[]{:S(2)}, u32[]{:S(2)}) collective-permute-start(bf16[48,128]{1,0:T(8,128)(2,1)S(1)} %get-tuple-element.22), channel_id=1, source_target_pairs={{0,4},{4,0},{8,12},{12,8},{1,5},{5,1},{9,13},{13,9},{2,6},{6,2},{1... | collective-permute-start | bytes 36872 | tf_op jit(solution)/shard_map/ppermute | solution.py:314
  64.2 3.7 %collective-permute-start.4 = (bf16[48,128]{1,0:T(8,128)(2,1)S(1)}, bf16[48,128]{1,0:T(8,128)(2,1)S(1)}, u32[]{:S(2)}, u32[]{:S(2)}) collective-permute-start(bf16[48,128]{1,0:T(8,128)(2,1)S(1)} %get-tuple-element.23), channel_id=1, source_target_pairs={{0,8},{4,12},{8,0},{12,4},{1,9},{5,13},{9,1},{13,5},{2,10},{6,14},... | collective-permute-start | bytes 36872 | tf_op jit(solution)/shard_map/ppermute | solution.py:314
  65.5 3.1 %collective-permute-start.5 = (bf16[48,128]{1,0:T(8,128)(2,1)S(1)}, bf16[48,128]{1,0:T(8,128)(2,1)S(1)}, u32[]{:S(2)}, u32[]{:S(2)}) collective-permute-start(bf16[48,128]{1,0:T(8,128)(2,1)S(1)} %get-tuple-element.24), channel_id=1, source_target_pairs={{0,12},{4,8},{8,4},{12,0},{1,13},{5,9},{9,5},{13,1},{2,14},{6,10},... | collective-permute-start | bytes 36872 | tf_op jit(solution)/shard_map/ppermute | solution.py:314

commit v2 on v1

v2 whole, which is shorter than its diff:
```python
import functools

import jax
import jax.numpy as jnp
from jax import lax
from jax.experimental import pallas as pl
from jax.experimental.pallas import tpu as pltpu
from jax.sharding import PartitionSpec as P

HEADS = 64
KV_HEADS = 8
HEAD_DIM = 128
GROUP = HEADS // KV_HEADS
MIB = 1 << 20
FETCH = (5, 7, 13)
DOWN_FIRST = 3
CUTS = (4, 6)
BF16 = jnp.bfloat16
F32 = jnp.float32
VMEM = pltpu.VMEM
HBM = pltpu.HBM


def call(kernel, name, ins, outs, scratch=(), limit=8, cost=None, after=()):
    if cost is None:
        cost = pl.CostEstimate(flops=0, bytes_accessed=1024, transcendentals=0)
    count = len(ins)
    ins = ins + [(a, VMEM) for a in after]

    def body(*refs):
        kernel(*refs[:count], *refs[count + len(after) :])

    return list(
        pl.pallas_call(
            body,
            name=name,
            in_specs=[pl.BlockSpec(memory_space=s) for _, s in ins],
            out_specs=[pl.BlockSpec(memory_space=VMEM) for _ in outs],
            out_shape=[VMEM(shape, dtype) for shape, dtype in outs],
            scratch_shapes=list(scratch),
            cost_estimate=cost,
            compiler_params=pltpu.CompilerParams(vmem_limit_bytes=limit * MIB),
        )(*[pltpu.with_memory_space_constraint(a, space) for a, space in ins])
    )


class Sizes:
    def __init__(self, toks, cols, cap, units):
        self.toks, self.cols, self.cap = toks, cols, cap
        half = units // 2
        cuts = [half * n // 8 for n in CUTS]
        self.parts = list(zip([0] + cuts, [b - a for a, b in zip([0] + cuts, cuts + [half])]))
        self.chunks = len(self.parts)
        self.step = min(512, min(size for _, size in self.parts))
        self.blocks_of = [
            [
                (q, keep, m, first + at)
                for keep in (False, True)
                for m in range(2)
                for at in range(0, size, self.step)
            ]
            for q, (first, size) in enumerate(self.parts)
        ]
        self.downs = [(mine, n * half // 4) for mine in (True, False) for n in range(4)]
        self.tail = 2 * self.parts[0][1]
        self.heads = HEADS // toks
        self.kvs = max(1, self.heads // GROUP)
        self.group = self.heads // self.kvs
        self.lane_slots = toks * cap
        self.rows = toks * cols * cap
        self.req_rows = -(-(self.heads + 2 * self.kvs) // 16) * 16
        self.blocks = 2 * self.kvs
        self.pieces = 2 * self.req_rows // 16

    def first_kv(self, tok):
        return tok * self.heads // GROUP


def pack_kernel(z, ctx, req_ref, cache_ref, *rest):
    outs, (narrow, wide, rows, req_sem, sems) = rest[: z.toks], rest[z.toks :]
    tok = lax.axis_index("tok")
    width = z.kvs * HEAD_DIM
    cache_rows = z.cap * ctx
    pairs = KV_HEADS * HEAD_DIM
    fetch = pltpu.make_async_copy(req_ref, narrow, req_sem)
    fetch.start()
    copies = []
    for s in reversed(range(z.toks)):
        first = pl.multiple_of(z.first_kv(tok ^ s) * HEAD_DIM, HEAD_DIM)
        for half in range(2):
            for k in range(z.cap):
                copy = pltpu.make_async_copy(
                    cache_ref.at[k, :, pl.ds(half * pairs + first, width)],
                    outs[s].at[pl.ds(k * ctx, ctx), pl.ds(half * width, width)],
                    sems.at[s, half, k],
                )
                copy.start()
                copies.append(copy)
    rows[...] = jnp.zeros_like(rows)
    fetch.wait()
    wide[...] = narrow[...].astype(F32)
    for s in range(z.toks):
        to = tok ^ s
        starts = [(to * z.heads + h) * HEAD_DIM for h in range(z.heads)]
        for half in range(2):
            starts += [
                HEADS * HEAD_DIM + half * pairs + (z.first_kv(to) + j) * HEAD_DIM
                for j in range(z.kvs)
            ]
        for r in range(2):
            for n, start in enumerate(starts):
                rows[r * z.req_rows + n : r * z.req_rows + n + 1, :] = wide[
                    r : r + 1, pl.ds(pl.multiple_of(start, HEAD_DIM), HEAD_DIM)
                ]
        for p in range(z.pieces):
            at, lane = cache_rows + p // z.blocks * 16, p % z.blocks * HEAD_DIM
            outs[s][at : at + 16, lane : lane + HEAD_DIM] = rows[p * 16 : p * 16 + 16, :].astype(BF16)
    for copy in copies:
        copy.wait()


def start_copies(pairs, sems):
    copies = [pltpu.make_async_copy(src, dst, sems.at[n]) for n, (src, dst) in enumerate(pairs)]
    for copy in copies:
        copy.start()
    return copies


def after_starts(compute):
    pl.when(lax.axis_index("tok") >= 0)(compute)


def weight_blocks(z, jobs, refs):
    core = lax.axis_index("tok") % 2
    half = refs[0].shape[1] // 2
    found = []
    for job in jobs:
        at = pl.multiple_of((core if job[-3 if len(job) > 2 else 0] else 1 - core) * half, half)
        if len(job) > 2:
            _, _, matrix, first = job
            found.append(refs[matrix].at[:, pl.ds(at + first, z.step)])
        else:
            found.append(refs[2].at[pl.ds(at + job[1], half // 4), :])
    return found


def fetch_kernel(z, jobs, whole, gain_size, *refs):
    weights, rest = refs[:3], refs[3:]
    sources, rest = list(rest[: len(whole)]), rest[len(whole) :]
    outs, sems = rest[:-1], rest[-1]
    if gain_size:
        tok = lax.axis_index("tok")
        at = pl.multiple_of(tok * gain_size, gain_size)
        sources[0] = sources[0].at[:, pl.ds(at, gain_size)]
    sources += weight_blocks(z, jobs, weights)
    for copy in start_copies(list(zip(sources, outs)), sems):
        copy.wait()


def attend_kernel(z, ctx, jobs, list_hbm, count_hbm, *rest):
    weights, pieces, rest = rest[:3], rest[3 : 3 + z.toks], rest[3 + z.toks :]
    send_ref, back_refs, rest = rest[0], rest[1 : 1 + z.toks], rest[1 + z.toks :]
    blocks, rest = rest[: len(jobs)], rest[len(jobs) :]
    cache, req, query, own_key, own_value, alive, mixed_all, list_ref, count_ref, table_sems, sems = rest
    tables = start_copies([(list_hbm, list_ref), (count_hbm, count_ref)], table_sems)
    copies = start_copies(list(zip(weight_blocks(z, jobs, weights), blocks)), sems)
    tok = lax.axis_index("tok")
    cache_rows = z.cap * ctx
    for s in range(z.toks):
        source = tok ^ s
        cache[source] = pieces[s][:cache_rows, :]
        for p in range(z.pieces):
            at, lane = cache_rows + p // z.blocks * 16, p % z.blocks * HEAD_DIM
            r, part = p * 16 // z.req_rows, p * 16 % z.req_rows
            req[source * 2 + r, part : part + 16, :] = pieces[s][
                at : at + 16, lane : lane + HEAD_DIM
            ].astype(F32)
    for table in tables:
        table.wait()
    for g in range(z.toks):
        for k in range(z.cap):
            live = (k < count_ref[0, g]).astype(F32)
            rows = req[list_ref[k, 0, g]] * live
            at = (g * z.cap + k) * z.group
            for j in range(z.kvs):
                query[j, at : at + z.group, :] = rows[j * z.group : (j + 1) * z.group, :]
                key, value = z.heads + j, z.heads + z.kvs + j
                own_key[j, at : at + z.group, :] = jnp.broadcast_to(
                    rows[key : key + 1, :], (z.group, HEAD_DIM)
                )
                own_value[j, at : at + z.group, :] = jnp.broadcast_to(
                    rows[value : value + 1, :], (z.group, HEAD_DIM)
                )
            alive[at : at + z.group, :] = jnp.full((z.group, HEAD_DIM), live, F32)
    many, keys = z.lane_slots * z.group, z.toks * cache_rows
    row_slot = lax.broadcasted_iota(jnp.int32, (many, keys), 0) // z.group
    key_slot = lax.broadcasted_iota(jnp.int32, (many, keys), 1) // ctx
    same = row_slot == key_slot
    scale = HEAD_DIM ** (-0.5)
    for j in range(z.kvs):
        cached_keys = cache[:, :, j * HEAD_DIM : (j + 1) * HEAD_DIM].reshape(keys, HEAD_DIM)
        at = (z.kvs + j) * HEAD_DIM
        cached_values = cache[:, :, at : at + HEAD_DIM].reshape(keys, HEAD_DIM)
        past = (
            lax.dot_general(
                query[j].astype(BF16),
                cached_keys,
                (((1,), (1,)), ((), ())),
                preferred_element_type=F32,
            )
            * scale
        )
        own = jnp.sum(query[j] * own_key[j], axis=-1, keepdims=True) * scale
        top = jnp.maximum(jnp.max(jnp.where(same, past, -jnp.inf), axis=-1, keepdims=True), own)
        past_exp = jnp.where(same, jnp.exp(jnp.where(same, past - top, 0.0)), 0.0)
        own_exp = jnp.exp(own - top)
        total = jnp.sum(past_exp, axis=-1, keepdims=True) + own_exp
        weights = (past_exp / total).astype(BF16)
        own_weight = (own_exp / total).astype(BF16).astype(F32)
        mixed = jnp.dot(weights, cached_values, preferred_element_type=F32)
        mixed = (mixed + own_weight * own_value[j]) * alive[...]
        mixed_all[j * many : (j + 1) * many, :] = mixed.astype(BF16).astype(F32)
    block = z.cap * z.group
    for s in range(z.toks):
        for j in range(z.kvs):
            at = pl.multiple_of(j * many + (tok ^ s) * block, block if block % 8 == 0 else 4)
            back_refs[s][j * block : (j + 1) * block, :] = mixed_all[pl.ds(at, block), :].astype(BF16)
    count = z.kvs * z.lane_slots
    for h in range(z.group):
        send_ref[:, h * HEAD_DIM : (h + 1) * HEAD_DIM] = mixed_all[
            pl.ds(h, count, stride=z.group), :
        ].astype(BF16)
    for copy in copies:
        copy.wait()


def halves(value):
    high = value.astype(BF16).astype(F32)
    return high, value - high


def two_lanes(high, low, rows):
    lane = lax.broadcasted_iota(jnp.int32, (rows, HEAD_DIM), 1)
    return jnp.where(lane == 0, high, jnp.where(lane == 1, low, 0.0)).astype(BF16)


def slot_of_row(z, col, shape):
    row = lax.broadcasted_iota(jnp.int32, shape, 0)
    return ((row // z.lane_slots) ^ col) * z.lane_slots + row % z.lane_slots


def tile_terms(z, source, delta_ref, index_ref, matrix, extra, out_base):
    side = delta_ref.shape[-1]
    col = lax.axis_index("col")
    variant = slot_of_row(z, col, (z.rows, side)) // (2 * z.cols * z.cap)
    for n in range(delta_ref.shape[2]):
        at = pl.multiple_of(index_ref[0, matrix, 1, 0, n] * side, side)
        to = pl.multiple_of(out_base + index_ref[0, matrix, 2, 0, n] * side, side)
        rows = jnp.where(variant == index_ref[0, matrix, 0, 0, n], source[:, pl.ds(at, side)], 0)
        extra[:, pl.ds(to, side)] += jnp.dot(
            rows.astype(BF16), delta_ref[0, 0, n], preferred_element_type=F32
        )


def project_blocks(z, chunk, source, extra, blocks, send_ref, keep_ref):
    core = lax.axis_index("tok") % 2
    units = extra.shape[1] // 2
    first, size = z.parts[chunk]
    for n, (out_ref, side) in enumerate(((send_ref, 1 - core), (keep_ref, core))):
        for m in range(2):
            for p in range(size // z.step):
                block = blocks[(2 * n + m) * (size // z.step) + p]
                at = side * (units // 2) + m * units + first + p * z.step
                value = jnp.dot(source[...], block[...], preferred_element_type=F32)
                value += extra[:, pl.ds(pl.multiple_of(at, HEAD_DIM), z.step)]
                to = m * size + p * z.step
                out_ref[:, to : to + z.step] = value.astype(BF16)


def first_project_kernel(z, jobs, index_hbm, gain_ref, gate_delta, up_delta, *rest):
    pieces, rest = rest[: z.cols], rest[z.cols :]
    odd_backs, rest = rest[: z.toks // 2], rest[z.toks // 2 :]
    count = len(z.blocks_of[0])
    weights, blocks, rest = rest[:3], rest[3 : 3 + count], rest[3 + count :]
    send_ref, keep_ref, source, extra, *fetched = rest[: 4 + len(jobs)]
    index_ref, index_sem, sems = rest[4 + len(jobs) :]
    table = pltpu.make_async_copy(index_hbm, index_ref, index_sem)
    table.start()
    copies = start_copies(list(zip(weight_blocks(z, jobs, weights), fetched)), sems)
    col = lax.axis_index("col")
    units = extra.shape[1] // 2
    extra[...] = jnp.zeros_like(extra)
    count = z.kvs * z.lane_slots
    wide = z.group * HEAD_DIM
    slot = slot_of_row(z, col, (z.rows, count))
    lane_of, owner = slot // z.cap % z.cols, slot // (z.cols * z.cap)
    column = lax.broadcasted_iota(jnp.int32, (z.rows, count), 1)
    squares = jnp.zeros((z.rows, 1), F32)
    for j in range(z.kvs):
        place = j * z.lane_slots + owner * z.cap + slot % z.cap
        found = jnp.zeros((z.rows, wide), F32)
        for s in range(z.cols):
            pick = ((lane_of == (col ^ s)) & (column == place)).astype(F32).astype(BF16)
            found += jnp.dot(pick, pieces[s][...], preferred_element_type=F32)
        squares += jnp.sum(found * found, axis=-1, keepdims=True)
        lanes = slice(j * wide, (j + 1) * wide)
        source[:, lanes] = (found * gain_ref[:, lanes]).astype(BF16)
    tail = z.tail
    for ref in (send_ref, keep_ref):
        ref[:, tail : tail + HEAD_DIM] = two_lanes(*halves(squares), z.rows)
    send_ref[:, tail + HEAD_DIM :] = jnp.zeros((z.rows, z.toks // 2 * HEAD_DIM), BF16)
    for n, ref in enumerate(odd_backs):
        lane = tail + (n + 1) * HEAD_DIM
        send_ref[: ref.shape[0], lane : lane + HEAD_DIM] = ref[...]
    table.wait()
    tile_terms(z, source, gate_delta, index_ref, 0, extra, 0)
    tile_terms(z, source, up_delta, index_ref, 1, extra, units)
    after_starts(lambda: project_blocks(z, 0, source, extra, blocks, send_ref, keep_ref))
    for copy in copies:
        copy.wait()


def next_project_kernel(z, jobs, delta_hbm, *rest):
    count = sum(len(some) for some in z.blocks_of[1:])
    weights, (source, extra), blocks, rest = rest[:3], rest[3:5], rest[5 : 5 + count], rest[5 + count :]
    sums = 2 * (z.chunks - 1)
    outs, (delta_ref, *fetched, sems) = rest[:sums], rest[sums:]
    copies = start_copies(
        list(zip(weight_blocks(z, jobs, weights) + [delta_hbm], fetched + [delta_ref])), sems
    )

    @after_starts
    def _():
        at = 0
        for q in range(1, z.chunks):
            refs = blocks[at : at + len(z.blocks_of[q])]
            at += len(refs)
            project_blocks(z, q, source, extra, refs, outs[2 * q - 2], outs[2 * q - 1])

    for copy in copies:
        copy.wait()


def add_kernel(z, mine, other, *rest):
    chips = z.toks // 2
    evens, outs = rest[: len(rest) - (chips - 1)], rest[len(rest) - (chips - 1) :]
    tail = z.tail if evens else mine.shape[1]
    sums = (mine[:, :tail].astype(F32) + other[:, :tail].astype(F32)).astype(BF16)
    for s, out_ref in enumerate(outs):
        out_ref[:, :tail] = sums
        if not evens:
            continue
        lanes = slice(tail, tail + HEAD_DIM)
        total = mine[:, lanes].astype(F32) + other[:, lanes].astype(F32)
        out_ref[:, lanes] = two_lanes(*halves(jnp.sum(total, axis=-1, keepdims=True)), z.rows)
        block = evens[s].shape[0]
        out_ref[:, tail + HEAD_DIM :] = jnp.zeros((z.rows, 2 * HEAD_DIM), BF16)
        out_ref[:block, tail + HEAD_DIM : tail + 2 * HEAD_DIM] = evens[s][...]
        lane = tail + (s + 2) * HEAD_DIM
        out_ref[:block, tail + 2 * HEAD_DIM :] = other[:block, lane : lane + HEAD_DIM]


def hidden_kernel(z, width, *refs):
    chips = z.toks // 2
    out_ref = refs[-1]
    squares = sum(ref[:, z.tail : z.tail + HEAD_DIM].astype(F32) for ref in refs[:chips])
    squares = jnp.sum(squares, axis=-1, keepdims=True)
    scale = lax.rsqrt(squares * (1.0 / width) + 1e-06)
    for q, (first, size) in enumerate(z.parts):
        parts = refs[q * chips : (q + 1) * chips]
        step = min(size, 256)
        for at in range(0, size, step):
            gate = sum(ref[:, at : at + step].astype(F32) for ref in parts) * scale
            up = sum(ref[:, size + at : size + at + step].astype(F32) for ref in parts) * scale
            out_ref[:, first + at : first + at + step] = (jax.nn.silu(gate) * up).astype(BF16)


def down_kernel(z, index_hbm, delta_ref, mine, other, *rest):
    weights, rest = rest[: len(z.downs)], rest[len(z.downs) :]
    outs, (source, total, fold, index_ref, index_sem) = rest[: z.cols], rest[z.cols :]
    table = pltpu.make_async_copy(index_hbm, index_ref, index_sem)
    table.start()
    core = lax.axis_index("tok") % 2
    half = mine.shape[1]
    source[:, pl.ds(pl.multiple_of(core * half, half), half)] = mine[...]
    source[:, pl.ds(pl.multiple_of((1 - core) * half, half), half)] = other[...]
    width = total.shape[1]
    step = min(width, 512)
    for to in range(0, width, step):
        value = jnp.zeros((z.rows, step), F32)
        for (is_mine, at), weight in zip(z.downs, weights):
            units = (mine if is_mine else other)[:, at : at + weight.shape[0]]
            value += jnp.dot(units, weight[:, to : to + step], preferred_element_type=F32)
        total[:, to : to + step] = value
    table.wait()
    tile_terms(z, source, delta_ref, index_ref, 2, total, 0)
    for s in range(z.cols):
        rows = slice(s * z.lane_slots, (s + 1) * z.lane_slots)
        fold[: z.lane_slots, :] = total[rows, : width // 2]
        fold[z.lane_slots :, :] = total[rows, width // 2 :]
        outs[s][...] = fold[...].astype(BF16)


def finish_kernel(z, *refs):
    parts, out_ref = refs[: z.cols], refs[z.cols]
    total = sum(ref[...].astype(F32) for ref in parts)
    half = total.shape[1]
    out_ref[:, :half] = total[: z.lane_slots].astype(BF16)
    out_ref[:, half:] = total[z.lane_slots :].astype(BF16)


def return_kernel(z, own, from_core, *refs):
    chips = z.toks // 2
    parts, (out_ref, rows) = refs[: chips - 1], refs[chips - 1 :]
    tok = lax.axis_index("tok")
    block = z.cap * z.group
    count = z.kvs * block
    tail = z.tail + HEAD_DIM
    for s in range(z.toks):
        if s == 0:
            rows[...] = own[...].astype(F32)
        elif s == 1:
            rows[...] = from_core[:count, tail : tail + HEAD_DIM].astype(F32)
        else:
            lane = tail + s % 2 * HEAD_DIM
            rows[...] = parts[s // 2 - 1][:count, lane : lane + HEAD_DIM].astype(F32)
        first = pl.multiple_of((tok ^ s) * z.heads * HEAD_DIM, HEAD_DIM)
        for j in range(z.kvs):
            for h in range(z.group):
                to = first + (j * z.group + h) * HEAD_DIM
                out_ref[:, pl.ds(to, HEAD_DIM)] = rows[
                    pl.ds(j * block + h, z.cap, stride=z.group), :
                ].astype(BF16)


def swap(array, axis, size, distance):
    return lax.ppermute(array, axis, [(i, i ^ distance) for i in range(size)])


def local(
    request_rows,
    key_cache,
    route_list,
    route_count,
    norm_gain,
    gate_weight,
    up_weight,
    down_weight,
    gate_delta,
    up_delta,
    down_delta,
    tile_index,
):
    toks, cols = lax.axis_size("tok"), lax.axis_size("col")
    cap, ctx = key_cache.shape[0], key_cache.shape[1]
    features, units = gate_weight.shape
    z = Sizes(toks, cols, cap, units)
    width = norm_gain.shape[0]
    cache_rows = cap * ctx
    lanes = 2 * z.kvs * HEAD_DIM
    piece_rows = cache_rows + -(-z.pieces // z.blocks) * 16
    many = z.lane_slots * z.group
    chips = toks // 2
    gain = norm_gain.reshape(1, width)
    route_list = route_list.transpose(2, 1, 0)
    route_count = route_count.transpose(1, 0)
    tile_index = tile_index.transpose(0, 2, 4, 1, 3)
    dma = pltpu.SemaphoreType.DMA

    jobs = [job for some in z.blocks_of for job in some]
    cuts = [0] + [-(-len(jobs) * n // 16) for n in FETCH]
    early, middle, late, beside = [jobs[a:b] for a, b in zip(cuts, cuts[1:] + [len(jobs)])]
    beside, last = beside + z.downs[:DOWN_FIRST], z.downs[DOWN_FIRST:]
    weights = [(gate_weight, HBM), (up_weight, HBM), (down_weight, HBM)]

    def shapes(some):
        up, down = (features, z.step), (units // 8, down_weight.shape[1])
        return [(up if len(job) > 2 else down, BF16) for job in some]

    def traffic(some):
        moved = sum(a * b * 2 for (a, b), _ in shapes(some))
        return pl.CostEstimate(flops=0, bytes_accessed=moved, transcendentals=0)

    pieces = call(
        functools.partial(pack_kernel, z, ctx),
        "pack",
        [(request_rows, HBM), (key_cache, HBM)],
        [((piece_rows, lanes), BF16)] * toks,
        [
            pltpu.VMEM(request_rows.shape, BF16),
            pltpu.VMEM(request_rows.shape, F32),
            pltpu.VMEM((2 * z.req_rows, HEAD_DIM), F32),
            dma,
            dma((toks, 2, cap)),
        ],
    )
    whole = [gain, gate_delta, up_delta]
    gain, gate_delta, up_delta, *blocks = call(
        functools.partial(fetch_kernel, z, early, whole, features),
        "fetch_early",
        weights + [(a, HBM) for a in whole],
        [((1, features), F32), (gate_delta.shape, BF16), (up_delta.shape, BF16)]
        + shapes(early),
        [dma((len(early) + 3,))],
        after=pieces[:1],
        cost=traffic(early),
    )
    pieces = [pieces[0]] + [swap(pieces[s], "tok", toks, s) for s in range(1, toks)]
    back_rows = z.kvs * cap * z.group
    send, *rest = call(
        functools.partial(attend_kernel, z, ctx, middle),
        "attend",
        [(route_list, HBM), (route_count, HBM)] + weights + [(p, VMEM) for p in pieces],
        [((z.kvs * z.lane_slots, z.group * HEAD_DIM), BF16)]
        + [((back_rows, HEAD_DIM), BF16)] * toks
        + shapes(middle),
        [
            pltpu.VMEM((toks, cache_rows, lanes), BF16),
            pltpu.VMEM((2 * toks, z.req_rows, HEAD_DIM), F32),
            pltpu.VMEM((z.kvs, many, HEAD_DIM), F32),
            pltpu.VMEM((z.kvs, many, HEAD_DIM), F32),
            pltpu.VMEM((z.kvs, many, HEAD_DIM), F32),
            pltpu.VMEM((many, HEAD_DIM), F32),
            pltpu.VMEM((z.kvs * many, HEAD_DIM), F32),
            pltpu.SMEM(route_list.shape, jnp.int32),
            pltpu.SMEM(route_count.shape, jnp.int32),
            dma((2,)),
            dma((max(1, len(middle)),)),
        ],
        after=[gain],
    )
    back = rest[:toks]
    blocks += rest[toks:]
    blocks += call(
        functools.partial(fetch_kernel, z, late, [], 0),
        "fetch_late",
        weights,
        shapes(late),
        [dma((len(late),))],
        after=[send],
        cost=traffic(late),
    )
    pieces = [send] + [swap(send, "col", cols, s) for s in range(1, cols)]
    out_width = down_weight.shape[1]
    table = pltpu.SMEM(tile_index.shape, jnp.int32)
    sent, kept, source, extra, *fetched = call(
        functools.partial(first_project_kernel, z, beside),
        "project_first",
        [
            (tile_index, HBM),
            (gain, VMEM),
            (gate_delta, VMEM),
            (up_delta, VMEM),
        ]
        + [(p, VMEM) for p in pieces + back[1::2]]
        + weights
        + [(p, VMEM) for p in blocks[: len(z.blocks_of[0])]],
        [
            ((z.rows, z.tail + (1 + chips) * HEAD_DIM), BF16),
            ((z.rows, z.tail + HEAD_DIM), BF16),
            ((z.rows, features), BF16),
            ((z.rows, 2 * units), F32),
        ]
        + shapes(beside),
        [table, dma, dma((len(beside),))],
        after=blocks[-1:],
    )
    blocks = blocks[len(z.blocks_of[0]) :] + fetched[: len(beside) - DOWN_FIRST]
    down_blocks = fetched[len(beside) - DOWN_FIRST :]
    from_core = swap(sent, "tok", toks, 1)
    totals = [
        call(
            functools.partial(add_kernel, z),
            "chip_sum_first",
            [(a, VMEM) for a in [kept, from_core] + back[2::2]],
            [((z.rows, z.tail + 3 * HEAD_DIM), BF16)] * (chips - 1),
        )
    ]
    sizes = [2 * size for _, size in z.parts[1:]]
    *sums, down_delta = call(
        functools.partial(next_project_kernel, z, last),
        "project_next",
        [(down_delta, HBM)] + weights + [(a, VMEM) for a in [source, extra] + blocks],
        [((z.rows, size), BF16) for size in sizes for _ in range(2)]
        + [(down_delta.shape, BF16)]
        + shapes(last),
        [dma((len(last) + 1,))],
        cost=pl.CostEstimate(
            flops=4 * z.rows * features * sum(sizes),
            bytes_accessed=4 * features * sum(sizes),
            transcendentals=0,
        ),
        after=totals[0][:1],
    )
    rest = sums[2 * len(sizes) :] + [down_delta]
    down_delta, down_blocks = rest[0], down_blocks + rest[1:]
    for q, size in enumerate(sizes):
        sent, kept = sums[2 * q : 2 * q + 2]
        totals.append(
            call(
                functools.partial(add_kernel, z),
                "chip_sum_next",
                [(kept, VMEM), (swap(sent, "tok", toks, 1), VMEM)],
                [((z.rows, size), BF16)] * (chips - 1),
            )
        )
    parts = [
        total[:1] + [swap(total[s - 1], "tok", toks, 2 * s) for s in range(1, chips)]
        for total in totals
    ]
    (hidden,) = call(
        functools.partial(hidden_kernel, z, width),
        "hidden",
        [(a, VMEM) for part in parts for a in part],
        [((z.rows, units // 2), BF16)],
    )
    firsts = parts[0]
    (attended,) = call(
        functools.partial(return_kernel, z),
        "attended",
        [(a, VMEM) for a in [back[0], from_core] + firsts[1:]],
        [((cap, width), BF16)],
        [pltpu.VMEM((back_rows, HEAD_DIM), F32)],
    )
    parts = call(
        functools.partial(down_kernel, z),
        "down",
        [(tile_index, HBM)]
        + [(a, VMEM) for a in [down_delta, hidden, swap(hidden, "tok", toks, 1)] + down_blocks],
        [((2 * z.lane_slots, out_width // 2), BF16)] * cols,
        [
            pltpu.VMEM((z.rows, units), BF16),
            pltpu.VMEM((z.rows, out_width), F32),
            pltpu.VMEM((2 * z.lane_slots, out_width // 2), F32),
            table,
            dma,
        ],
    )
    parts = [parts[0]] + [swap(parts[s], "col", cols, s) for s in range(1, cols)]
    (ffn_out,) = call(
        functools.partial(finish_kernel, z),
        "finish",
        [(p, VMEM) for p in parts],
        [((z.lane_slots, out_width), BF16)],
    )
    return attended, ffn_out


def solution(mesh):
    in_specs = (
        P(("rep", "tok", "col"), None),
        P(("rep", "tok", "col"), None, None),
        P("rep", "col", None),
        P("rep", "col"),
        P(),
        P("tok", "col"),
        P("tok", "col"),
        P("col", "tok"),
        P("tok", "col", None, None, None),
        P("tok", "col", None, None, None),
        P("tok", "col", None, None, None),
        P("tok", "col", None, None, None),
    )
    out_specs = (P(("rep", "tok", "col"), None), P(("rep", "col"), "tok"))
    return jax.shard_map(local, mesh=mesh, in_specs=in_specs, out_specs=out_specs, check_vma=False)
```

time: 70.5 us -> 58.4 us (0.83)
  waiting for transfers between devices: 22.8 us -> 13.4 us
  local copies, waits for them, and re-layouts: 6.9 us -> 1.26 us
  Pallas kernels: 23.8 us -> 26 us
  starting transfers between devices: 15.9 us -> 16.7 us
    ppermute x15 -> x16, waiting for transfers between devices: 22.8 us -> 13.4 us  [swap(): return lax.ppermute(array, axis, [(i, i ^ distance) for i in range(size)])]
    unnamed x15 -> x2, local copies, waits for them, and re-layouts: 6.9 us -> 1.26 us
    pallas_call x8 -> x13, Pallas kernels: 23.8 us -> 26 us  [call(): pl.pallas_call(body, name=name, in_specs=[pl.BlockSpec(memory_space=s) fo...]
    ppermute x15 -> x16, starting transfers between devices: 15.9 us -> 16.7 us  [swap(): return lax.ppermute(array, axis, [(i, i ^ distance) for i in range(size)])]
  transfers between devices with their start and end apart: 15 -> 16, of which waited for: 9 -> 7; matrix products, arithmetic and copies ran while one was open for 4% -> 1% of each run, Pallas kernels for 0% -> 23%
where the time goes in v2:
time: 58.4 us; the launch traced here: 58.2 us
  Pallas kernels  26 us (45%)
  starting transfers between devices  16.7 us (29%)
  waiting for transfers between devices  13.4 us (23%)
  local copies, waits for them, and re-layouts  1.26 us (2%)
  between operations  0.79 us (1%)
    pallas_call x13, Pallas kernels, call(): pl.pallas_call(body, name=name, in_specs=[pl.BlockSpec(memory_space=s) fo...  26 us
    ppermute x16, starting transfers between devices, swap(): return lax.ppermute(array, axis, [(i, i ^ distance) for i in range(size)])  16.7 us
    ppermute x16, waiting for transfers between devices, swap(): return lax.ppermute(array, axis, [(i, i ^ distance) for i in range(size)])  13.4 us
    unnamed x2, local copies, waits for them, and re-layouts  1.26 us
  transfers between devices with their start and end apart: 16, of which 7 were waited for; matrix products, arithmetic and copies ran while one was open for 1% of the time, Pallas kernels for 23%

profile of v2, /device:TPU:0, one launch (start us, length us, event | category | flops | bytes accessed | tf_op | source)
XLA Modules:
  0.0 58.2 jit_solution(7658748914387400527)
XLA Ops:
  0.6 1.4 %pack.1 = (bf16[64,512]{1,0:T(8,128)(2,1)S(1)}, bf16[64,512]{1,0:T(8,128)(2,1)S(1)}, bf16[64,512]{1,0:T(8,128)(2,1)S(1)}, bf16[64,512]{1,0:T(8,128)(2,1)S(1)}) custom-call(bf16[2,10240]{1,0:T(2,128)(2,1)} %refs_0_.4, bf16[3,16,2048]{2,1,0:T(8,128)(2,1)} %refs_1_.4), custom_call_target="tpu_custom_call" | custom-call | bytes 1024 | tf_op jit(solution)/shard_map/pack/pallas_call | solution.py:34
  2.0 0.5 collective-permute-start
  2.5 2.6 %collective-permute-start.1 = (bf16[64,512]{1,0:T(8,128)(2,1)S(1)}, bf16[64,512]{1,0:T(8,128)(2,1)S(1)}, u32[]{:S(2)}, u32[]{:S(2)}) collective-permute-start(bf16[64,512]{1,0:T(8,128)(2,1)S(1)} %get-tuple-element.53), channel_id=1, source_target_pairs={{0,8},{4,12},{8,0},{12,4},{1,9},{5,13},{9,1},{13,5},{2,10},{6,14},... | collective-permute-start | bytes 196616 | tf_op jit(solution)/shard_map/ppermute | solution.py:437
  5.2 4.4 %fetch_early.1 = (f32[1,2048]{1,0:T(1,128)S(1)}, bf16[1,1,4,128,128]{4,3,2,1,0:T(8,128)(2,1)S(1)}, bf16[1,1,4,128,128]{4,3,2,1,0:T(8,128)(2,1)S(1)}, bf16[2048,5...) custom-call(bf16[2048,4096]{1,0:T(8,128)(2,1)} %refs_1_.7, ...), custom_call_target="tpu_custom_call" | custom-call | bytes 10485760 | tf_op jit(solution)/shard_map/fetch_early/pallas_call | solution.py:34
  9.6 2.3 %attend.1 = (bf16[24,1024]{1,0:T(8,128)(2,1)S(1)}, bf16[48,128]{1,0:T(8,128)(2,1)S(1)}, bf16[48,128]{1,0:T(8,128)(2,1)S(1)}, bf16[48,128]{1,0:T(8,128)(2,1)S(1)}...) custom-call(s32[3,1,4]{2,1,0:T(1,128)} %bitcast.7, s32[1,4]{1,0:T(1,128)} %bitcast.8, ...), custom_call_target="tpu_custom_call" | custom-call | bytes 1024 | tf_op jit(solution)/shard_map/attend/pallas_call | solution.py:34
  11.9 3.9 %collective-permute-start.5 = (bf16[24,1024]{1,0:T(8,128)(2,1)S(1)}, bf16[24,1024]{1,0:T(8,128)(2,1)S(1)}, u32[]{:S(2)}, u32[]{:S(2)}) collective-permute-start(bf16[24,1024]{1,0:T(8,128)(2,1)S(1)} %get-tuple-element.59.refs_3_.refs_4_), channel_id=1, source_target_pairs={{0,3},{1,2},{2,1},{3,0},{4,7},{5,6},{6,5},{7,4},{8,11},{9,10},{10,... | collective-permute-start | bytes 147464 | tf_op jit(solution)/shard_map/ppermute | solution.py:437
  15.8 0.6 %collective-permute-start.3 = (bf16[24,1024]{1,0:T(8,128)(2,1)S(1)}, bf16[24,1024]{1,0:T(8,128)(2,1)S(1)}, u32[]{:S(2)}, u32[]{:S(2)}) collective-permute-start(bf16[24,1024]{1,0:T(8,128)(2,1)S(1)} %get-tuple-element.59.refs_3_.refs_4_), channel_id=1, source_target_pairs={{0,1},{1,0},{2,3},{3,2},{4,5},{5,4},{6,7},{7,6},{8,9},{9,8},{10,11... | collective-permute-start | bytes 147464 | tf_op jit(solution)/shard_map/ppermute | solution.py:437
  16.4 4.8 %fetch_late.1 = (bf16[2048,512]{1,0:T(8,128)(2,1)S(1)}, bf16[2048,512]{1,0:T(8,128)(2,1)S(1)}, bf16[2048,512]{1,0:T(8,128)(2,1)S(1)}, bf16[2048,512]{1,0:T(8,128...) custom-call(bf16[2048,4096]{1,0:T(8,128)(2,1)} %refs_1_.7, bf16[2048,4096]{1,0:T(8,128)(2,1)} %refs_2_.7, ...), custom_call_target="tpu_custom_call" | custom-call | bytes 12582912 | tf_op jit(solution)/shard_map/fetch_late/pallas_call | solution.py:34
  21.3 5.2 %project_first.1 = (bf16[48,2432]{1,0:T(8,128)(2,1)S(1)}, bf16[48,2176]{1,0:T(8,128)(2,1)S(1)}, bf16[48,2048]{1,0:T(8,128)(2,1)S(1)}, f32[48,8192]{1,0:T(8,128)S...) custom-call(s32[1,3,3,1,4]{4,3,2,1,0:T(1,128)} %bitcast.5, ...), custom_call_target="tpu_custom_call" | custom-call | bytes 1024 | tf_op jit(solution)/shard_map/project_first/pallas_call | solution.py:34
  26.5 1.5 %collective-permute-done.6.refs_1_ = bf16[48,2432]{1,0:T(8,128)(2,1)S(1)} collective-permute-done((bf16[48,2432]{1,0:T(8,128)(2,1)S(1)}, bf16[48,2432]{1,0:T(8,128)(2,1)S(1)}, u32[]{:S(2)}, u32[]{:S(2)}) %collective-permute-start.6) | collective-permute-done | bytes 233504 | tf_op jit(solution)/shard_map/ppermute | solution.py:437
  28.2 1.7 %collective-permute-start.7 = (bf16[48,2432]{1,0:T(8,128)(2,1)S(1)}, bf16[48,2432]{1,0:T(8,128)(2,1)S(1)}, u32[]{:S(2)}, u32[]{:S(2)}) collective-permute-start(bf16[48,2432]{1,0:T(8,128)(2,1)S(1)} %chip_sum_first.1.refs_14_.refs_0_), channel_id=1, source_target_pairs={{0,8},{4,12},{8,0},{12,4},{1,9},{5,13},{9,1},{13,5},{2,10},{6,14},... | collective-permute-start | bytes 700424 | tf_op jit(solution)/shard_map/ppermute | solution.py:437
  29.9 4.1 %project_next.1 = (bf16[48,1024]{1,0:T(8,128)(2,1)S(1)}, bf16[48,1024]{1,0:T(8,128)(2,1)S(1)}, bf16[48,1024]{1,0:T(8,128)(2,1)S(1)}, bf16[48,1024]{1,0:T(8,128)(...) custom-call(bf16[1,1,4,128,128]{4,3,2,1,0:T(8,128)(2,1)} %refs_0_.7,, ...), custom_call_target="tpu_custom_call" | custom-call | flops 805306368 | bytes 16777216 | tf_op jit(solution)/shard_map/project_next/pallas_call | solution.py:34
  34.6 0.8 %collective-permute-done.8.refs_1_ = bf16[48,1024]{1,0:T(8,128)(2,1)S(1)} collective-permute-done((bf16[48,1024]{1,0:T(8,128)(2,1)S(1)}, bf16[48,1024]{1,0:T(8,128)(2,1)S(1)}, u32[]{:S(2)}, u32[]{:S(2)}) %collective-permute-start.8) | collective-permute-done | bytes 98336 | tf_op jit(solution)/shard_map/ppermute | solution.py:437
  35.9 1.7 %collective-permute-start.11 = (bf16[48,1024]{1,0:T(8,128)(2,1)S(1)}, bf16[48,1024]{1,0:T(8,128)(2,1)S(1)}, u32[]{:S(2)}, u32[]{:S(2)}) collective-permute-start(bf16[48,1024]{1,0:T(8,128)(2,1)S(1)} %chip_sum_next.3.refs_4_), channel_id=1, source_target_pairs={{0,8},{4,12},{8,0},{12,4},{1,9},{5,13},{9,1},{13,5},{2,10},{6,14},... | collective-permute-start | bytes 294920 | tf_op jit(solution)/shard_map/ppermute | solution.py:437
  37.6 3.5 %collective-permute-done.9.refs_3_ = bf16[48,1024]{1,0:T(8,128)(2,1)S(1)} collective-permute-done((bf16[48,1024]{1,0:T(8,128)(2,1)S(1)}, bf16[48,1024]{1,0:T(8,128)(2,1)S(1)}, u32[]{:S(2)}, u32[]{:S(2)}) %collective-permute-start.9) | collective-permute-done | bytes 98336 | tf_op jit(solution)/shard_map/ppermute | solution.py:437
  41.1 1.3 %collective-permute-done.11.refs_5_ = bf16[48,1024]{1,0:T(8,128)(2,1)S(1)} collective-permute-done((bf16[48,1024]{1,0:T(8,128)(2,1)S(1)}, bf16[48,1024]{1,0:T(8,128)(2,1)S(1)}, u32[]{:S(2)}, u32[]{:S(2)}) %collective-permute-start.11) | collective-permute-done | bytes 98336 | tf_op jit(solution)/shard_map/ppermute | solution.py:437
  42.7 1.4 %collective-permute-done.12.refs_3_ = bf16[48,2048]{1,0:T(8,128)(2,1)S(1)} collective-permute-done((bf16[48,2048]{1,0:T(8,128)(2,1)S(1)}, bf16[48,2048]{1,0:T(8,128)(2,1)S(1)}, u32[]{:S(2)}, u32[]{:S(2)}) %collective-permute-start.12) | collective-permute-done | bytes 196640 | tf_op jit(solution)/shard_map/ppermute | solution.py:437
  44.1 3.3 %down.1 = (bf16[24,1024]{1,0:T(8,128)(2,1)S(1)}, bf16[24,1024]{1,0:T(8,128)(2,1)S(1)}, bf16[24,1024]{1,0:T(8,128)(2,1)S(1)}, bf16[24,1024]{1,0:T(8,128)(2,1)S(1)}) custom-call(s32[1,3,3,1,4]{4,3,2,1,0:T(1,128)} %bitcast.6, bf16[1,1,4,128,128]{4,3,2,1,0:T(8,128)(2,1)S(1)} %get-tuple-element.83.refs_1_, bf16[48,2048]{1,0:T(8,128)(2,1)S(1)} %hidden.1.refs_2_, ...), custom_call_target="tpu_custom_call" | custom-call | bytes 1024 | tf_op jit(solution)/shard_map/down/pallas_call | solution.py:34
  47.4 1.3 %collective-permute-start.13 = (bf16[24,1024]{1,0:T(8,128)(2,1)S(1)}, bf16[24,1024]{1,0:T(8,128)(2,1)S(1)}, u32[]{:S(2)}, u32[]{:S(2)}) collective-permute-start(bf16[24,1024]{1,0:T(8,128)(2,1)S(1)} %get-tuple-element.97), channel_id=1, source_target_pairs={{0,1},{1,0},{2,3},{3,2},{4,5},{5,4},{6,7},{7,6},{8,9},{9,8},{10,11... | collective-permute-start | bytes 147464 | tf_op jit(solution)/shard_map/ppermute | solution.py:437
  48.7 2.9 %collective-permute-start.14 = (bf16[24,1024]{1,0:T(8,128)(2,1)S(1)}, bf16[24,1024]{1,0:T(8,128)(2,1)S(1)}, u32[]{:S(2)}, u32[]{:S(2)}) collective-permute-start(bf16[24,1024]{1,0:T(8,128)(2,1)S(1)} %get-tuple-element.98), channel_id=1, source_target_pairs={{0,2},{1,3},{2,0},{3,1},{4,6},{5,7},{6,4},{7,5},{8,10},{9,11},{10,... | collective-permute-start | bytes 147464 | tf_op jit(solution)/shard_map/ppermute | solution.py:437
  52.0 0.6 %copy.14 = bf16[3,8192]{1,0:T(4,128)(2,1)} copy(bf16[3,8192]{1,0:T(4,128)(2,1)S(1)} %attended.1) | data formatting | bytes 98304
  52.7 2.1 %collective-permute-done.14.refs_2_ = bf16[24,1024]{1,0:T(8,128)(2,1)S(1)} collective-permute-done((bf16[24,1024]{1,0:T(8,128)(2,1)S(1)}, bf16[24,1024]{1,0:T(8,128)(2,1)S(1)}, u32[]{:S(2)}, u32[]{:S(2)}) %collective-permute-start.14) | collective-permute-done | bytes 49184 | tf_op jit(solution)/shard_map/ppermute | solution.py:437
  54.8 2.7 %collective-permute-done.15.refs_3_ = bf16[24,1024]{1,0:T(8,128)(2,1)S(1)} collective-permute-done((bf16[24,1024]{1,0:T(8,128)(2,1)S(1)}, bf16[24,1024]{1,0:T(8,128)(2,1)S(1)}, u32[]{:S(2)}, u32[]{:S(2)}) %collective-permute-start.15) | collective-permute-done | bytes 49184 | tf_op jit(solution)/shard_map/ppermute | solution.py:437
  57.6 0.6 %copy.15 = bf16[12,2048]{1,0:T(8,128)(2,1)} copy(bf16[12,2048]{1,0:T(8,128)(2,1)S(1)} %finish.1) | data formatting | bytes 98304
  (23 shorter events, 2.1 us)
Async XLA Ops:
  2.0 7.5 %collective-permute-start = (bf16[64,512]{1,0:T(8,128)(2,1)S(1)}, bf16[64,512]{1,0:T(8,128)(2,1)S(1)}, u32[]{:S(2)}, u32[]{:S(2)}) collective-permute-start(bf16[64,512]{1,0:T(8,128)(2,1)S(1)} %get-tuple-element.52), channel_id=1, source_target_pairs={{0,4},{4,0},{8,12},{12,8},{1,5},{5,1},{9,13},{13,9},{2,6},{6,2},{1... | collective-permute-start | bytes 196616 | tf_op jit(solution)/shard_map/ppermute | solution.py:437
  2.5 7.0 %collective-permute-start.1 = (bf16[64,512]{1,0:T(8,128)(2,1)S(1)}, bf16[64,512]{1,0:T(8,128)(2,1)S(1)}, u32[]{:S(2)}, u32[]{:S(2)}) collective-permute-start(bf16[64,512]{1,0:T(8,128)(2,1)S(1)} %get-tuple-element.53), channel_id=1, source_target_pairs={{0,8},{4,12},{8,0},{12,4},{1,9},{5,13},{9,1},{13,5},{2,10},{6,14},... | collective-permute-start | bytes 196616 | tf_op jit(solution)/shard_map/ppermute | solution.py:437
  5.1 4.5 %collective-permute-start.2 = (bf16[64,512]{1,0:T(8,128)(2,1)S(1)}, bf16[64,512]{1,0:T(8,128)(2,1)S(1)}, u32[]{:S(2)}, u32[]{:S(2)}) collective-permute-start(bf16[64,512]{1,0:T(8,128)(2,1)S(1)} %get-tuple-element.54), channel_id=1, source_target_pairs={{0,12},{4,8},{8,4},{12,0},{1,13},{5,9},{9,5},{13,1},{2,14},{6,10},... | collective-permute-start | bytes 196616 | tf_op jit(solution)/shard_map/ppermute | solution.py:437
  11.9 9.3 %collective-permute-start.5 = (bf16[24,1024]{1,0:T(8,128)(2,1)S(1)}, bf16[24,1024]{1,0:T(8,128)(2,1)S(1)}, u32[]{:S(2)}, u32[]{:S(2)}) collective-permute-start(bf16[24,1024]{1,0:T(8,128)(2,1)S(1)} %get-tuple-element.59.refs_3_.refs_4_), channel_id=1, source_target_pairs={{0,3},{1,2},{2,1},{3,0},{4,7},{5,6},{6,5},{7,4},{8,11},{9,10},{10,... | collective-permute-start | bytes 147464 | tf_op jit(solution)/shard_map/ppermute | solution.py:437
  15.8 5.5 %collective-permute-start.4 = (bf16[24,1024]{1,0:T(8,128)(2,1)S(1)}, bf16[24,1024]{1,0:T(8,128)(2,1)S(1)}, u32[]{:S(2)}, u32[]{:S(2)}) collective-permute-start(bf16[24,1024]{1,0:T(8,128)(2,1)S(1)} %get-tuple-element.59.refs_3_.refs_4_), channel_id=1, source_target_pairs={{0,2},{1,3},{2,0},{3,1},{4,6},{5,7},{6,4},{7,5},{8,10},{9,11},{10,... | collective-permute-start | bytes 147464 | tf_op jit(solution)/shard_map/ppermute | solution.py:437
  15.8 5.5 %collective-permute-start.3 = (bf16[24,1024]{1,0:T(8,128)(2,1)S(1)}, bf16[24,1024]{1,0:T(8,128)(2,1)S(1)}, u32[]{:S(2)}, u32[]{:S(2)}) collective-permute-start(bf16[24,1024]{1,0:T(8,128)(2,1)S(1)} %get-tuple-element.59.refs_3_.refs_4_), channel_id=1, source_target_pairs={{0,1},{1,0},{2,3},{3,2},{4,5},{5,4},{6,7},{7,6},{8,9},{9,8},{10,11... | collective-permute-start | bytes 147464 | tf_op jit(solution)/shard_map/ppermute | solution.py:437
  26.4 1.6 %collective-permute-start.6 = (bf16[48,2432]{1,0:T(8,128)(2,1)S(1)}, bf16[48,2432]{1,0:T(8,128)(2,1)S(1)}, u32[]{:S(2)}, u32[]{:S(2)}) collective-permute-start(bf16[48,2432]{1,0:T(8,128)(2,1)S(1)} %get-tuple-element.71), channel_id=1, source_target_pairs={{0,4},{4,0},{8,12},{12,8},{1,5},{5,1},{9,13},{13,9},{2,6},{6,2},{1... | collective-permute-start | bytes 700424 | tf_op jit(solution)/shard_map/ppermute | solution.py:437
  28.2 14.2 %collective-permute-start.7 = (bf16[48,2432]{1,0:T(8,128)(2,1)S(1)}, bf16[48,2432]{1,0:T(8,128)(2,1)S(1)}, u32[]{:S(2)}, u32[]{:S(2)}) collective-permute-start(bf16[48,2432]{1,0:T(8,128)(2,1)S(1)} %chip_sum_first.1.refs_14_.refs_0_), channel_id=1, source_target_pairs={{0,8},{4,12},{8,0},{12,4},{1,9},{5,13},{9,1},{13,5},{2,10},{6,14},... | collective-permute-start | bytes 700424 | tf_op jit(solution)/shard_map/ppermute | solution.py:437
  34.0 1.4 %collective-permute-start.8 = (bf16[48,1024]{1,0:T(8,128)(2,1)S(1)}, bf16[48,1024]{1,0:T(8,128)(2,1)S(1)}, u32[]{:S(2)}, u32[]{:S(2)}) collective-permute-start(bf16[48,1024]{1,0:T(8,128)(2,1)S(1)} %get-tuple-element.85), channel_id=1, source_target_pairs={{0,4},{4,0},{8,12},{12,8},{1,5},{5,1},{9,13},{13,9},{2,6},{6,2},{1... | collective-permute-start | bytes 294920 | tf_op jit(solution)/shard_map/ppermute | solution.py:437
  34.1 1.8 %collective-permute-start.10 = (bf16[48,1024]{1,0:T(8,128)(2,1)S(1)}, bf16[48,1024]{1,0:T(8,128)(2,1)S(1)}, u32[]{:S(2)}, u32[]{:S(2)}) collective-permute-start(bf16[48,1024]{1,0:T(8,128)(2,1)S(1)} %get-tuple-element.87), channel_id=1, source_target_pairs={{0,4},{4,0},{8,12},{12,8},{1,5},{5,1},{9,13},{13,9},{2,6},{6,2},{1... | collective-permute-start | bytes 294920 | tf_op jit(solution)/shard_map/ppermute | solution.py:437
  35.4 5.7 %collective-permute-start.9 = (bf16[48,1024]{1,0:T(8,128)(2,1)S(1)}, bf16[48,1024]{1,0:T(8,128)(2,1)S(1)}, u32[]{:S(2)}, u32[]{:S(2)}) collective-permute-start(bf16[48,1024]{1,0:T(8,128)(2,1)S(1)} %chip_sum_next.2.refs_2_), channel_id=1, source_target_pairs={{0,8},{4,12},{8,0},{12,4},{1,9},{5,13},{9,1},{13,5},{2,10},{6,14},... | collective-permute-start | bytes 294920 | tf_op jit(solution)/shard_map/ppermute | solution.py:437
  35.9 6.5 %collective-permute-start.11 = (bf16[48,1024]{1,0:T(8,128)(2,1)S(1)}, bf16[48,1024]{1,0:T(8,128)(2,1)S(1)}, u32[]{:S(2)}, u32[]{:S(2)}) collective-permute-start(bf16[48,1024]{1,0:T(8,128)(2,1)S(1)} %chip_sum_next.3.refs_4_), channel_id=1, source_target_pairs={{0,8},{4,12},{8,0},{12,4},{1,9},{5,13},{9,1},{13,5},{2,10},{6,14},... | collective-permute-start | bytes 294920 | tf_op jit(solution)/shard_map/ppermute | solution.py:437
  42.6 1.5 %collective-permute-start.12 = (bf16[48,2048]{1,0:T(8,128)(2,1)S(1)}, bf16[48,2048]{1,0:T(8,128)(2,1)S(1)}, u32[]{:S(2)}, u32[]{:S(2)}) collective-permute-start(bf16[48,2048]{1,0:T(8,128)(2,1)S(1)} %hidden.1.refs_2_), channel_id=1, source_target_pairs={{0,4},{4,0},{8,12},{12,8},{1,5},{5,1},{9,13},{13,9},{2,6},{6,2},{1... | collective-permute-start | bytes 589832 | tf_op jit(solution)/shard_map/ppermute | solution.py:437
  47.4 5.3 %collective-permute-start.13 = (bf16[24,1024]{1,0:T(8,128)(2,1)S(1)}, bf16[24,1024]{1,0:T(8,128)(2,1)S(1)}, u32[]{:S(2)}, u32[]{:S(2)}) collective-permute-start(bf16[24,1024]{1,0:T(8,128)(2,1)S(1)} %get-tuple-element.97), channel_id=1, source_target_pairs={{0,1},{1,0},{2,3},{3,2},{4,5},{5,4},{6,7},{7,6},{8,9},{9,8},{10,11... | collective-permute-start | bytes 147464 | tf_op jit(solution)/shard_map/ppermute | solution.py:437
  48.7 6.1 %collective-permute-start.14 = (bf16[24,1024]{1,0:T(8,128)(2,1)S(1)}, bf16[24,1024]{1,0:T(8,128)(2,1)S(1)}, u32[]{:S(2)}, u32[]{:S(2)}) collective-permute-start(bf16[24,1024]{1,0:T(8,128)(2,1)S(1)} %get-tuple-element.98), channel_id=1, source_target_pairs={{0,2},{1,3},{2,0},{3,1},{4,6},{5,7},{6,4},{7,5},{8,10},{9,11},{10,... | collective-permute-start | bytes 147464 | tf_op jit(solution)/shard_map/ppermute | solution.py:437
  51.6 5.9 %collective-permute-start.15 = (bf16[24,1024]{1,0:T(8,128)(2,1)S(1)}, bf16[24,1024]{1,0:T(8,128)(2,1)S(1)}, u32[]{:S(2)}, u32[]{:S(2)}) collective-permute-start(bf16[24,1024]{1,0:T(8,128)(2,1)S(1)} %get-tuple-element.99), channel_id=1, source_target_pairs={{0,3},{1,2},{2,1},{3,0},{4,7},{5,6},{6,5},{7,4},{8,11},{9,10},{10,... | collective-permute-start | bytes 147464 | tf_op jit(solution)/shard_map/ppermute | solution.py:437

commit v3 on v2

--- a/solution.py
+++ b/solution.py
@@ -12,8 +12,7 @@
 HEAD_DIM = 128
 GROUP = HEADS // KV_HEADS
 MIB = 1 << 20
-FETCH = (5, 7, 13)
-DOWN_FIRST = 3
+FETCH = (0, 4, 1, 5, 5, 1, 3, 5)
 CUTS = (4, 6)
 BF16 = jnp.bfloat16
 F32 = jnp.float32
@@ -76,11 +75,11 @@
         return tok * self.heads // GROUP
 
 
-def pack_kernel(z, ctx, req_ref, cache_ref, *rest):
-    outs, (narrow, wide, rows, req_sem, sems) = rest[: z.toks], rest[z.toks :]
+def pack_kernel(z, ctx, jobs, req_ref, cache_ref, *rest):
+    weights, outs, rest = rest[:3], rest[3 : 3 + z.toks], rest[3 + z.toks :]
+    blocks, (narrow, wide, rows, req_sem, sems, block_sems) = rest[: len(jobs)], rest[len(jobs) :]
     tok = lax.axis_index("tok")
     width = z.kvs * HEAD_DIM
-    cache_rows = z.cap * ctx
     pairs = KV_HEADS * HEAD_DIM
     fetch = pltpu.make_async_copy(req_ref, narrow, req_sem)
     fetch.start()
@@ -88,33 +87,38 @@
     for s in reversed(range(z.toks)):
         first = pl.multiple_of(z.first_kv(tok ^ s) * HEAD_DIM, HEAD_DIM)
         for half in range(2):
-            for k in range(z.cap):
-                copy = pltpu.make_async_copy(
-                    cache_ref.at[k, :, pl.ds(half * pairs + first, width)],
-                    outs[s].at[pl.ds(k * ctx, ctx), pl.ds(half * width, width)],
-                    sems.at[s, half, k],
-                )
-                copy.start()
-                copies.append(copy)
-    rows[...] = jnp.zeros_like(rows)
+            copy = pltpu.make_async_copy(
+                cache_ref.at[:, :, pl.ds(half * pairs + first, width)],
+                outs[s].at[: z.cap, :, pl.ds(half * width, width)],
+                sems.at[s, half],
+            )
+            copy.start()
+            copies.append(copy)
+    copies += start_copies(list(zip(weight_blocks(z, jobs, weights), blocks)), block_sems)
     fetch.wait()
-    wide[...] = narrow[...].astype(F32)
-    for s in range(z.toks):
-        to = tok ^ s
-        starts = [(to * z.heads + h) * HEAD_DIM for h in range(z.heads)]
-        for half in range(2):
-            starts += [
-                HEADS * HEAD_DIM + half * pairs + (z.first_kv(to) + j) * HEAD_DIM
-                for j in range(z.kvs)
-            ]
-        for r in range(2):
-            for n, start in enumerate(starts):
-                rows[r * z.req_rows + n : r * z.req_rows + n + 1, :] = wide[
-                    r : r + 1, pl.ds(pl.multiple_of(start, HEAD_DIM), HEAD_DIM)
+
+    @after_starts
+    def _():
+        rows[...] = jnp.zeros_like(rows)
+        wide[...] = narrow[...].astype(F32)
+        for s in range(z.toks):
+            to = tok ^ s
+            starts = [(to * z.heads + h) * HEAD_DIM for h in range(z.heads)]
+            for half in range(2):
+                starts += [
+                    HEADS * HEAD_DIM + half * pairs + (z.first_kv(to) + j) * HEAD_DIM
+                    for j in range(z.kvs)
                 ]
-        for p in range(z.pieces):
-            at, lane = cache_rows + p // z.blocks * 16, p % z.blocks * HEAD_DIM
-            outs[s][at : at + 16, lane : lane + HEAD_DIM] = rows[p * 16 : p * 16 + 16, :].astype(BF16)
+            for r in range(2):
+                for n, start in enumerate(starts):
+                    at = r * z.req_rows + n
+                    rows[s, at : at + 1, :] = wide[
+                        r : r + 1, pl.ds(pl.multiple_of(start, HEAD_DIM), HEAD_DIM)
+                    ]
+            for p in range(z.pieces):
+                at, lane = z.cap + p // z.blocks, p % z.blocks * HEAD_DIM
+                outs[s][at, :, lane : lane + HEAD_DIM] = rows[s, p * 16 : p * 16 + 16, :].astype(BF16)
+
     for copy in copies:
         copy.wait()
 
@@ -164,72 +168,76 @@
     cache, req, query, own_key, own_value, alive, mixed_all, list_ref, count_ref, table_sems, sems = rest
     tables = start_copies([(list_hbm, list_ref), (count_hbm, count_ref)], table_sems)
     copies = start_copies(list(zip(weight_blocks(z, jobs, weights), blocks)), sems)
-    tok = lax.axis_index("tok")
-    cache_rows = z.cap * ctx
-    for s in range(z.toks):
-        source = tok ^ s
-        cache[source] = pieces[s][:cache_rows, :]
-        for p in range(z.pieces):
-            at, lane = cache_rows + p // z.blocks * 16, p % z.blocks * HEAD_DIM
-            r, part = p * 16 // z.req_rows, p * 16 % z.req_rows
-            req[source * 2 + r, part : part + 16, :] = pieces[s][
-                at : at + 16, lane : lane + HEAD_DIM
-            ].astype(F32)
-    for table in tables:
-        table.wait()
-    for g in range(z.toks):
-        for k in range(z.cap):
-            live = (k < count_ref[0, g]).astype(F32)
-            rows = req[list_ref[k, 0, g]] * live
-            at = (g * z.cap + k) * z.group
+
+    @after_starts
+    def _():
+        tok = lax.axis_index("tok")
+        cache_rows = z.cap * ctx
+        for s in range(z.toks):
+            source = tok ^ s
+            cache[source] = pieces[s][: z.cap].reshape(cache_rows, cache.shape[2])
+            for p in range(z.pieces):
+                at, lane = z.cap + p // z.blocks, p % z.blocks * HEAD_DIM
+                r, part = p * 16 // z.req_rows, p * 16 % z.req_rows
+                req[source * 2 + r, part : part + 16, :] = pieces[s][
+                    at, :, lane : lane + HEAD_DIM
+                ].astype(F32)
+        for table in tables:
+            table.wait()
+        for g in range(z.toks):
+            for k in range(z.cap):
+                live = (k < count_ref[0, g]).astype(F32)
+                rows = req[list_ref[k, 0, g]] * live
+                at = (g * z.cap + k) * z.group
+                for j in range(z.kvs):
+                    query[j, at : at + z.group, :] = rows[j * z.group : (j + 1) * z.group, :]
+                    key, value = z.heads + j, z.heads + z.kvs + j
+                    own_key[j, at : at + z.group, :] = jnp.broadcast_to(
+                        rows[key : key + 1, :], (z.group, HEAD_DIM)
+                    )
+                    own_value[j, at : at + z.group, :] = jnp.broadcast_to(
+                        rows[value : value + 1, :], (z.group, HEAD_DIM)
+                    )
+                alive[at : at + z.group, :] = jnp.full((z.group, HEAD_DIM), live, F32)
+        many, keys = z.lane_slots * z.group, z.toks * cache_rows
+        row_slot = lax.broadcasted_iota(jnp.int32, (many, keys), 0) // z.group
+        key_slot = lax.broadcasted_iota(jnp.int32, (many, keys), 1) // ctx
+        same = row_slot == key_slot
+        scale = HEAD_DIM ** (-0.5)
+        for j in range(z.kvs):
+            cached_keys = cache[:, :, j * HEAD_DIM : (j + 1) * HEAD_DIM].reshape(keys, HEAD_DIM)
+            at = (z.kvs + j) * HEAD_DIM
+            cached_values = cache[:, :, at : at + HEAD_DIM].reshape(keys, HEAD_DIM)
+            past = (
+                lax.dot_general(
+                    query[j].astype(BF16),
+                    cached_keys,
+                    (((1,), (1,)), ((), ())),
+                    preferred_element_type=F32,
+                )
+                * scale
+            )
+            own = jnp.sum(query[j] * own_key[j], axis=-1, keepdims=True) * scale
+            top = jnp.maximum(jnp.max(jnp.where(same, past, -jnp.inf), axis=-1, keepdims=True), own)
+            past_exp = jnp.where(same, jnp.exp(jnp.where(same, past - top, 0.0)), 0.0)
+            own_exp = jnp.exp(own - top)
+            total = jnp.sum(past_exp, axis=-1, keepdims=True) + own_exp
+            weights = (past_exp / total).astype(BF16)
+            own_weight = (own_exp / total).astype(BF16).astype(F32)
+            mixed = jnp.dot(weights, cached_values, preferred_element_type=F32)
+            mixed = (mixed + own_weight * own_value[j]) * alive[...]
+            mixed_all[j * many : (j + 1) * many, :] = mixed.astype(BF16).astype(F32)
+        block = z.cap * z.group
+        for s in range(z.toks):
             for j in range(z.kvs):
-                query[j, at : at + z.group, :] = rows[j * z.group : (j + 1) * z.group, :]
-                key, value = z.heads + j, z.heads + z.kvs + j
-                own_key[j, at : at + z.group, :] = jnp.broadcast_to(
-                    rows[key : key + 1, :], (z.group, HEAD_DIM)
-                )
-                own_value[j, at : at + z.group, :] = jnp.broadcast_to(
-                    rows[value : value + 1, :], (z.group, HEAD_DIM)
-                )
-            alive[at : at + z.group, :] = jnp.full((z.group, HEAD_DIM), live, F32)
-    many, keys = z.lane_slots * z.group, z.toks * cache_rows
-    row_slot = lax.broadcasted_iota(jnp.int32, (many, keys), 0) // z.group
-    key_slot = lax.broadcasted_iota(jnp.int32, (many, keys), 1) // ctx
-    same = row_slot == key_slot
-    scale = HEAD_DIM ** (-0.5)
-    for j in range(z.kvs):
-        cached_keys = cache[:, :, j * HEAD_DIM : (j + 1) * HEAD_DIM].reshape(keys, HEAD_DIM)
-        at = (z.kvs + j) * HEAD_DIM
-        cached_values = cache[:, :, at : at + HEAD_DIM].reshape(keys, HEAD_DIM)
-        past = (
-            lax.dot_general(
-                query[j].astype(BF16),
-                cached_keys,
-                (((1,), (1,)), ((), ())),
-                preferred_element_type=F32,
-            )
-            * scale
-        )
-        own = jnp.sum(query[j] * own_key[j], axis=-1, keepdims=True) * scale
-        top = jnp.maximum(jnp.max(jnp.where(same, past, -jnp.inf), axis=-1, keepdims=True), own)
-        past_exp = jnp.where(same, jnp.exp(jnp.where(same, past - top, 0.0)), 0.0)
-        own_exp = jnp.exp(own - top)
-        total = jnp.sum(past_exp, axis=-1, keepdims=True) + own_exp
-        weights = (past_exp / total).astype(BF16)
-        own_weight = (own_exp / total).astype(BF16).astype(F32)
-        mixed = jnp.dot(weights, cached_values, preferred_element_type=F32)
-        mixed = (mixed + own_weight * own_value[j]) * alive[...]
-        mixed_all[j * many : (j + 1) * many, :] = mixed.astype(BF16).astype(F32)
-    block = z.cap * z.group
-    for s in range(z.toks):
-        for j in range(z.kvs):
-            at = pl.multiple_of(j * many + (tok ^ s) * block, block if block % 8 == 0 else 4)
-            back_refs[s][j * block : (j + 1) * block, :] = mixed_all[pl.ds(at, block), :].astype(BF16)
-    count = z.kvs * z.lane_slots
-    for h in range(z.group):
-        send_ref[:, h * HEAD_DIM : (h + 1) * HEAD_DIM] = mixed_all[
-            pl.ds(h, count, stride=z.group), :
-        ].astype(BF16)
+                at = pl.multiple_of(j * many + (tok ^ s) * block, block if block % 8 == 0 else 4)
+                back_refs[s][j * block : (j + 1) * block, :] = mixed_all[pl.ds(at, block), :].astype(BF16)
+        count = z.kvs * z.lane_slots
+        for h in range(z.group):
+            send_ref[:, h * HEAD_DIM : (h + 1) * HEAD_DIM] = mixed_all[
+                pl.ds(h, count, stride=z.group), :
+            ].astype(BF16)
+
     for copy in copies:
         copy.wait()
 
@@ -262,19 +270,25 @@
         )
 
 
-def project_blocks(z, chunk, source, extra, blocks, send_ref, keep_ref):
+def project_steps(z, chunk, source, extra, blocks, send_ref, keep_ref):
     core = lax.axis_index("tok") % 2
     units = extra.shape[1] // 2
     first, size = z.parts[chunk]
+    steps = []
     for n, (out_ref, side) in enumerate(((send_ref, 1 - core), (keep_ref, core))):
         for m in range(2):
             for p in range(size // z.step):
                 block = blocks[(2 * n + m) * (size // z.step) + p]
                 at = side * (units // 2) + m * units + first + p * z.step
-                value = jnp.dot(source[...], block[...], preferred_element_type=F32)
-                value += extra[:, pl.ds(pl.multiple_of(at, HEAD_DIM), z.step)]
                 to = m * size + p * z.step
-                out_ref[:, to : to + z.step] = value.astype(BF16)
+
+                def step(block=block, at=pl.multiple_of(at, HEAD_DIM), to=to, out_ref=out_ref):
+                    value = jnp.dot(source[...], block[...], preferred_element_type=F32)
+                    value += extra[:, pl.ds(at, z.step)]
+                    out_ref[:, to : to + z.step] = value.astype(BF16)
+
+                steps.append(step)
+    return steps
 
 
 def first_project_kernel(z, jobs, index_hbm, gain_ref, gate_delta, up_delta, *rest):
@@ -287,8 +301,27 @@
     table = pltpu.make_async_copy(index_hbm, index_ref, index_sem)
     table.start()
     copies = start_copies(list(zip(weight_blocks(z, jobs, weights), fetched)), sems)
+    units = extra.shape[1] // 2
+
+    @after_starts
+    def _():
+        gather_rows(z, pieces, gain_ref, odd_backs, source, extra, send_ref, keep_ref)
+
+    table.wait()
+
+    @after_starts
+    def _():
+        tile_terms(z, source, gate_delta, index_ref, 0, extra, 0)
+        tile_terms(z, source, up_delta, index_ref, 1, extra, units)
+        for step in project_steps(z, 0, source, extra, blocks, send_ref, keep_ref):
+            step()
+
+    for copy in copies:
+        copy.wait()
+
+
+def gather_rows(z, pieces, gain_ref, odd_backs, source, extra, send_ref, keep_ref):
     col = lax.axis_index("col")
-    units = extra.shape[1] // 2
     extra[...] = jnp.zeros_like(extra)
     count = z.kvs * z.lane_slots
     wide = z.group * HEAD_DIM
@@ -312,52 +345,43 @@
     for n, ref in enumerate(odd_backs):
         lane = tail + (n + 1) * HEAD_DIM
         send_ref[: ref.shape[0], lane : lane + HEAD_DIM] = ref[...]
-    table.wait()
-    tile_terms(z, source, gate_delta, index_ref, 0, extra, 0)
-    tile_terms(z, source, up_delta, index_ref, 1, extra, units)
-    after_starts(lambda: project_blocks(z, 0, source, extra, blocks, send_ref, keep_ref))
-    for copy in copies:
-        copy.wait()
 
 
 def next_project_kernel(z, jobs, delta_hbm, *rest):
     count = sum(len(some) for some in z.blocks_of[1:])
-    weights, (source, extra), blocks, rest = rest[:3], rest[3:5], rest[5 : 5 + count], rest[5 + count :]
+    here = sum(len(job) > 2 for job in jobs)
+    weights, (source, extra), rest = rest[:3], rest[3:5], rest[5:]
+    blocks, rest = rest[: count - here], rest[count - here :]
     sums = 2 * (z.chunks - 1)
-    outs, (delta_ref, *fetched, sems) = rest[:sums], rest[sums:]
+    outs, (delta_ref, *fetched) = rest[:sums], rest[sums:-1]
     copies = start_copies(
-        list(zip(weight_blocks(z, jobs, weights) + [delta_hbm], fetched + [delta_ref])), sems
-    )
+        list(zip(weight_blocks(z, jobs, weights) + [delta_hbm], fetched + [delta_ref])), rest[-1]
+    )
+    blocks = list(blocks) + fetched[:here]
+    steps = []
+    for q in range(1, z.chunks):
+        refs = blocks[len(steps) : len(steps) + len(z.blocks_of[q])]
+        steps += project_steps(z, q, source, extra, refs, outs[2 * q - 2], outs[2 * q - 1])
 
     @after_starts
     def _():
-        at = 0
-        for q in range(1, z.chunks):
-            refs = blocks[at : at + len(z.blocks_of[q])]
-            at += len(refs)
-            project_blocks(z, q, source, extra, refs, outs[2 * q - 2], outs[2 * q - 1])
-
-    for copy in copies:
+        for step in steps[: count - here]:
+            step()
+
+    for n in range(here):
+        copies[n].wait()
+        after_starts(steps[count - here + n])
+    for copy in copies[here:]:
         copy.wait()
 
 
-def add_kernel(z, mine, other, *rest):
-    chips = z.toks // 2
-    evens, outs = rest[: len(rest) - (chips - 1)], rest[len(rest) - (chips - 1) :]
-    tail = z.tail if evens else mine.shape[1]
-    sums = (mine[:, :tail].astype(F32) + other[:, :tail].astype(F32)).astype(BF16)
-    for s, out_ref in enumerate(outs):
-        out_ref[:, :tail] = sums
-        if not evens:
-            continue
-        lanes = slice(tail, tail + HEAD_DIM)
+def add_kernel(z, mine, other, out_ref):
+    size = mine.shape[1] // (2 * HEAD_DIM) * (2 * HEAD_DIM)
+    out_ref[:, :size] = (mine[:, :size].astype(F32) + other[:, :size].astype(F32)).astype(BF16)
+    if mine.shape[1] > size:
+        lanes = slice(size, size + HEAD_DIM)
         total = mine[:, lanes].astype(F32) + other[:, lanes].astype(F32)
         out_ref[:, lanes] = two_lanes(*halves(jnp.sum(total, axis=-1, keepdims=True)), z.rows)
-        block = evens[s].shape[0]
-        out_ref[:, tail + HEAD_DIM :] = jnp.zeros((z.rows, 2 * HEAD_DIM), BF16)
-        out_ref[:block, tail + HEAD_DIM : tail + 2 * HEAD_DIM] = evens[s][...]
-        lane = tail + (s + 2) * HEAD_DIM
-        out_ref[:block, tail + 2 * HEAD_DIM :] = other[:block, lane : lane + HEAD_DIM]
 
 
 def hidden_kernel(z, width, *refs):
@@ -375,25 +399,47 @@
             out_ref[:, first + at : first + at + step] = (jax.nn.silu(gate) * up).astype(BF16)
 
 
-def down_kernel(z, index_hbm, delta_ref, mine, other, *rest):
-    weights, rest = rest[: len(z.downs)], rest[len(z.downs) :]
-    outs, (source, total, fold, index_ref, index_sem) = rest[: z.cols], rest[z.cols :]
+def down_products(z, mine, units_ref, weights, total, before=None):
+    width = total.shape[1]
+    places = [at for is_mine, at in z.downs if is_mine == mine]
+    step = min(width, 512)
+    for to in range(0, width, step):
+        lanes = slice(to, to + step)
+        value = jnp.zeros((z.rows, step), F32) if before is None else before[:, lanes]
+        for at, weight in zip(places, weights):
+            units = units_ref[:, at : at + weight.shape[0]]
+            value += jnp.dot(units, weight[:, lanes], preferred_element_type=F32)
+        total[:, lanes] = value
+
+
+def down_mine_kernel(z, mine, *rest):
+    down_products(z, True, mine, rest[:-1], rest[-1])
+
+
+def down_kernel(z, index_hbm, delta_ref, before, mine, other, from_core, *rest):
+    others = z.toks // 2 - 1
+    evens, rest = rest[:others], rest[others:]
+    weights, rest = rest[: len(z.downs) // 2], rest[len(z.downs) // 2 :]
+    outs, backs, rest = rest[: z.cols], rest[z.cols : z.cols + others], rest[z.cols + others :]
+    source, total, fold, index_ref, index_sem = rest
     table = pltpu.make_async_copy(index_hbm, index_ref, index_sem)
     table.start()
-    core = lax.axis_index("tok") % 2
-    half = mine.shape[1]
-    source[:, pl.ds(pl.multiple_of(core * half, half), half)] = mine[...]
-    source[:, pl.ds(pl.multiple_of((1 - core) * half, half), half)] = other[...]
-    width = total.shape[1]
-    step = min(width, 512)
-    for to in range(0, width, step):
-        value = jnp.zeros((z.rows, step), F32)
-        for (is_mine, at), weight in zip(z.downs, weights):
-            units = (mine if is_mine else other)[:, at : at + weight.shape[0]]
-            value += jnp.dot(units, weight[:, to : to + step], preferred_element_type=F32)
-        total[:, to : to + step] = value
+
+    @after_starts
+    def _():
+        core = lax.axis_index("tok") % 2
+        half = mine.shape[1]
+        source[:, pl.ds(pl.multiple_of(core * half, half), half)] = mine[...]
+        source[:, pl.ds(pl.multiple_of((1 - core) * half, half), half)] = other[...]
+        down_products(z, False, other, weights, total, before)
+
+    for s, back in enumerate(backs):
+        back[:, :HEAD_DIM] = evens[s][...]
+        lane = z.tail + (s + 2) * HEAD_DIM
+        back[:, HEAD_DIM:] = from_core[: back.shape[0], lane : lane + HEAD_DIM]
     table.wait()
     tile_terms(z, source, delta_ref, index_ref, 2, total, 0)
+    width = total.shape[1]
     for s in range(z.cols):
         rows = slice(s * z.lane_slots, (s + 1) * z.lane_slots)
         fold[: z.lane_slots, :] = total[rows, : width // 2]
@@ -422,8 +468,8 @@
         elif s == 1:
             rows[...] = from_core[:count, tail : tail + HEAD_DIM].astype(F32)
         else:
-            lane = tail + s % 2 * HEAD_DIM
-            rows[...] = parts[s // 2 - 1][:count, lane : lane + HEAD_DIM].astype(F32)
+            lane = s % 2 * HEAD_DIM
+            rows[...] = parts[s // 2 - 1][:, lane : lane + HEAD_DIM].astype(F32)
         first = pl.multiple_of((tok ^ s) * z.heads * HEAD_DIM, HEAD_DIM)
         for j in range(z.kvs):
             for h in range(z.group):
@@ -458,7 +504,7 @@
     width = norm_gain.shape[0]
     cache_rows = cap * ctx
     lanes = 2 * z.kvs * HEAD_DIM
-    piece_rows = cache_rows + -(-z.pieces // z.blocks) * 16
+    piece_shape = (cap + -(-z.pieces // z.blocks), ctx, lanes)
     many = z.lane_slots * z.group
     chips = toks // 2
     gain = norm_gain.reshape(1, width)
@@ -468,9 +514,12 @@
     dma = pltpu.SemaphoreType.DMA
 
     jobs = [job for some in z.blocks_of for job in some]
-    cuts = [0] + [-(-len(jobs) * n // 16) for n in FETCH]
-    early, middle, late, beside = [jobs[a:b] for a, b in zip(cuts, cuts[1:] + [len(jobs)])]
-    beside, last = beside + z.downs[:DOWN_FIRST], z.downs[DOWN_FIRST:]
+    used = len(jobs)
+    jobs += z.downs
+    cuts = [0]
+    for count in FETCH:
+        cuts.append(cuts[-1] + count)
+    first, early, middle, late, beside, between, last, final = [jobs[a:b] for a, b in zip(cuts, cuts[1:])]
     weights = [(gate_weight, HBM), (up_weight, HBM), (down_weight, HBM)]
 
     def shapes(some):
@@ -482,20 +531,22 @@
         return pl.CostEstimate(flops=0, bytes_accessed=moved, transcendentals=0)
 
     pieces = call(
-        functools.partial(pack_kernel, z, ctx),
+        functools.partial(pack_kernel, z, ctx, first),
         "pack",
-        [(request_rows, HBM), (key_cache, HBM)],
-        [((piece_rows, lanes), BF16)] * toks,
+        [(request_rows, HBM), (key_cache, HBM)] + weights,
+        [(piece_shape, BF16)] * toks + shapes(first),
         [
             pltpu.VMEM(request_rows.shape, BF16),
             pltpu.VMEM(request_rows.shape, F32),
-            pltpu.VMEM((2 * z.req_rows, HEAD_DIM), F32),
+            pltpu.VMEM((toks, 2 * z.req_rows, HEAD_DIM), F32),
             dma,
-            dma((toks, 2, cap)),
+            dma((toks, 2)),
+            dma((max(1, len(first)),)),
         ],
     )
+    pieces, blocks = pieces[:toks], pieces[toks:]
     whole = [gain, gate_delta, up_delta]
-    gain, gate_delta, up_delta, *blocks = call(
+    gain, gate_delta, up_delta, *fetched = call(
         functools.partial(fetch_kernel, z, early, whole, features),
         "fetch_early",
         weights + [(a, HBM) for a in whole],
@@ -505,6 +556,7 @@
         after=pieces[:1],
         cost=traffic(early),
     )
+    blocks += fetched
     pieces = [pieces[0]] + [swap(pieces[s], "tok", toks, s) for s in range(1, toks)]
     back_rows = z.kvs * cap * z.group
     send, *rest = call(
@@ -565,22 +617,32 @@
         [table, dma, dma((len(beside),))],
         after=blocks[-1:],
     )
-    blocks = blocks[len(z.blocks_of[0]) :] + fetched[: len(beside) - DOWN_FIRST]
-    down_blocks = fetched[len(beside) - DOWN_FIRST :]
+    blocks = blocks[len(z.blocks_of[0]) :] + fetched
+    fetched = call(
+        functools.partial(fetch_kernel, z, between, [], 0),
+        "fetch_between",
+        weights,
+        shapes(between),
+        [dma((len(between),))],
+        cost=traffic(between),
+        after=[sent],
+    )
+    blocks += fetched
     from_core = swap(sent, "tok", toks, 1)
     totals = [
         call(
             functools.partial(add_kernel, z),
             "chip_sum_first",
-            [(a, VMEM) for a in [kept, from_core] + back[2::2]],
-            [((z.rows, z.tail + 3 * HEAD_DIM), BF16)] * (chips - 1),
+            [(kept, VMEM), (from_core, VMEM)],
+            [((z.rows, z.tail + HEAD_DIM), BF16)],
+            after=fetched[-1:],
         )
     ]
     sizes = [2 * size for _, size in z.parts[1:]]
     *sums, down_delta = call(
         functools.partial(next_project_kernel, z, last),
         "project_next",
-        [(down_delta, HBM)] + weights + [(a, VMEM) for a in [source, extra] + blocks],
+        [(down_delta, HBM)] + weights + [(a, VMEM) for a in [source, extra] + blocks[: used - len(z.blocks_of[0])]],
         [((z.rows, size), BF16) for size in sizes for _ in range(2)]
         + [(down_delta.shape, BF16)]
         + shapes(last),
@@ -593,41 +655,57 @@
         after=totals[0][:1],
     )
     rest = sums[2 * len(sizes) :] + [down_delta]
-    down_delta, down_blocks = rest[0], down_blocks + rest[1:]
+    down_delta, blocks = rest[0], blocks + rest[1:]
     for q, size in enumerate(sizes):
         sent, kept = sums[2 * q : 2 * q + 2]
+        other = swap(sent, "tok", toks, 1)
         totals.append(
             call(
                 functools.partial(add_kernel, z),
                 "chip_sum_next",
-                [(kept, VMEM), (swap(sent, "tok", toks, 1), VMEM)],
-                [((z.rows, size), BF16)] * (chips - 1),
+                [(kept, VMEM), (other, VMEM)],
+                [((z.rows, size), BF16)],
             )
         )
     parts = [
-        total[:1] + [swap(total[s - 1], "tok", toks, 2 * s) for s in range(1, chips)]
+        total + [swap(total[0], "tok", toks, 2 * s) for s in range(1, chips)]
         for total in totals
     ]
+    fetched = call(
+        functools.partial(fetch_kernel, z, final, [], 0),
+        "fetch_down",
+        weights,
+        shapes(final),
+        [dma((len(final),))],
+        cost=traffic(final),
+        after=totals[-1],
+    )
+    down_blocks = (blocks + fetched)[-len(z.downs) :]
     (hidden,) = call(
         functools.partial(hidden_kernel, z, width),
         "hidden",
         [(a, VMEM) for part in parts for a in part],
         [((z.rows, units // 2), BF16)],
-    )
-    firsts = parts[0]
-    (attended,) = call(
-        functools.partial(return_kernel, z),
-        "attended",
-        [(a, VMEM) for a in [back[0], from_core] + firsts[1:]],
-        [((cap, width), BF16)],
-        [pltpu.VMEM((back_rows, HEAD_DIM), F32)],
+        after=fetched[-1:],
+    )
+    half = len(z.downs) // 2
+    (before,) = call(
+        functools.partial(down_mine_kernel, z),
+        "down_mine",
+        [(a, VMEM) for a in [hidden] + down_blocks[:half]],
+        [((z.rows, out_width), F32)],
+        cost=pl.CostEstimate(
+            flops=z.rows * units * out_width, bytes_accessed=units * out_width, transcendentals=0
+        ),
     )
     parts = call(
         functools.partial(down_kernel, z),
         "down",
         [(tile_index, HBM)]
-        + [(a, VMEM) for a in [down_delta, hidden, swap(hidden, "tok", toks, 1)] + down_blocks],
-        [((2 * z.lane_slots, out_width // 2), BF16)] * cols,
+        + [(a, VMEM) for a in [down_delta, before, hidden, swap(hidden, "tok", toks, 1), from_core]]
+        + [(a, VMEM) for a in back[2::2] + down_blocks[half:]],
+        [((2 * z.lane_slots, out_width // 2), BF16)] * cols
+        + [((back_rows, 2 * HEAD_DIM), BF16)] * (chips - 1),
         [
             pltpu.VMEM((z.rows, units), BF16),
             pltpu.VMEM((z.rows, out_width), F32),
@@ -636,7 +714,16 @@
             dma,
         ],
     )
+    parts, across = parts[:cols], parts[cols:]
     parts = [parts[0]] + [swap(parts[s], "col", cols, s) for s in range(1, cols)]
+    across = [swap(rows, "tok", toks, 2 * s + 2) for s, rows in enumerate(across)]
+    (attended,) = call(
+        functools.partial(return_kernel, z),
+        "attended",
+        [(a, VMEM) for a in [back[0], from_core] + across],
+        [((cap, width), BF16)],
+        [pltpu.VMEM((back_rows, HEAD_DIM), F32)],
+    )
     (ffn_out,) = call(
         functools.partial(finish_kernel, z),
         "finish",

time: 58.4 us -> 53.2 us (0.911)
  waiting for transfers between devices: 13.4 us -> 6.26 us
  Pallas kernels: 26 us -> 27.6 us
    ppermute x16 -> x17, waiting for transfers between devices: 13.4 us -> 6.26 us  [swap(): return lax.ppermute(array, axis, [(i, i ^ distance) for i in range(size)])]
    pallas_call x13 -> x16, Pallas kernels: 26 us -> 27.6 us  [call(): pl.pallas_call(body, name=name, in_specs=[pl.BlockSpec(memory_space=s) fo...]
    ppermute x16 -> x17, starting transfers between devices: 16.7 us -> 17 us  [swap(): return lax.ppermute(array, axis, [(i, i ^ distance) for i in range(size)])]
  transfers between devices with their start and end apart: 16 -> 17, of which waited for: 7 -> 6; matrix products, arithmetic and copies ran while one was open for 1% -> 1% of each run, Pallas kernels for 23% -> 35%
where the time goes in v3:
time: 53.2 us; the launch traced here: 53 us
  Pallas kernels  27.6 us (52%)
  starting transfers between devices  17 us (32%)
  waiting for transfers between devices  6.26 us (12%)
  local copies, waits for them, and re-layouts  1.26 us (2%)
  between operations  0.8 us (2%)
    pallas_call x16, Pallas kernels, call(): pl.pallas_call(body, name=name, in_specs=[pl.BlockSpec(memory_space=s) fo...  27.6 us
    ppermute x17, starting transfers between devices, swap(): return lax.ppermute(array, axis, [(i, i ^ distance) for i in range(size)])  17 us
    ppermute x17, waiting for transfers between devices, swap(): return lax.ppermute(array, axis, [(i, i ^ distance) for i in range(size)])  6.26 us
    unnamed x2, local copies, waits for them, and re-layouts  1.26 us
  transfers between devices with their start and end apart: 17, of which 6 were waited for; matrix products, arithmetic and copies ran while one was open for 1% of the time, Pallas kernels for 35%

profile of v3, /device:TPU:0, one launch (start us, length us, event | category | flops | bytes accessed | tf_op | source)
XLA Modules:
  0.0 53.0 jit_solution(16327138494620943543)
XLA Ops:
  0.6 1.1 %pack.1 = (bf16[4,16,512]{2,1,0:T(8,128)(2,1)S(1)}, bf16[4,16,512]{2,1,0:T(8,128)(2,1)S(1)}, bf16[4,16,512]{2,1,0:T(8,128)(2,1)S(1)}, bf16[4,16,512]{2,1,0:T(8,128)(2,1)S(1)}) custom-call(bf16[2,10240]{1,0:T(2,128)(2,1)} %refs_0_.6, bf16[3,16,2048]{2,1,0:T(8,128)(2,1)} %refs_1_.6, bf16[2048,4096]{1,0:T(8,128)(2,1)} %refs_0_.11, bf16[2048,4096]{1,0:T(8,128)(2,1)} %refs_1_.11, ...), custom_call_target="tpu_custom_call" | custom-call | bytes 1024 | tf_op jit(solution)/shard_map/pack/pallas_call | solution.py:33
  2.3 2.6 %collective-permute-start.1 = (bf16[4,16,512]{2,1,0:T(8,128)(2,1)S(1)}, bf16[4,16,512]{2,1,0:T(8,128)(2,1)S(1)}, u32[]{:S(2)}, u32[]{:S(2)}) collective-permute-start(bf16[4,16,512]{2,1,0:T(8,128)(2,1)S(1)} %get-tuple-element.53), channel_id=1, source_target_pairs={{0,8},{4,12},{8,0},{12,4},{1,9},{5,13},{9,1},{13,5},{2,10},{6,14},... | collective-permute-start | bytes 196616 | tf_op jit(solution)/shard_map/ppermute | solution.py:483
  4.9 3.7 %fetch_early.1 = (f32[1,2048]{1,0:T(1,128)S(1)}, bf16[1,1,4,128,128]{4,3,2,1,0:T(8,128)(2,1)S(1)}, bf16[1,1,4,128,128]{4,3,2,1,0:T(8,128)(2,1)S(1)}, bf16[2048,5...) custom-call(bf16[2048,4096]{1,0:T(8,128)(2,1)} %refs_0_.11, ...), custom_call_target="tpu_custom_call" | custom-call | bytes 8388608 | tf_op jit(solution)/shard_map/fetch_early/pallas_call | solution.py:33
  8.9 1.6 %attend.1 = (bf16[24,1024]{1,0:T(8,128)(2,1)S(1)}, bf16[48,128]{1,0:T(8,128)(2,1)S(1)}, bf16[48,128]{1,0:T(8,128)(2,1)S(1)}, bf16[48,128]{1,0:T(8,128)(2,1)S(1)}...) custom-call(s32[3,1,4]{2,1,0:T(1,128)} %bitcast.7, s32[1,4]{1,0:T(1,128)} %bitcast.8, ...), custom_call_target="tpu_custom_call" | custom-call | bytes 1024 | tf_op jit(solution)/shard_map/attend/pallas_call | solution.py:33
  10.5 3.7 %collective-permute-start.5 = (bf16[24,1024]{1,0:T(8,128)(2,1)S(1)}, bf16[24,1024]{1,0:T(8,128)(2,1)S(1)}, u32[]{:S(2)}, u32[]{:S(2)}) collective-permute-start(bf16[24,1024]{1,0:T(8,128)(2,1)S(1)} %get-tuple-element.59.refs_3_.refs_4_), channel_id=1, source_target_pairs={{0,3},{1,2},{2,1},{3,0},{4,7},{5,6},{6,5},{7,4},{8,11},{9,10},{10,... | collective-permute-start | bytes 147464 | tf_op jit(solution)/shard_map/ppermute | solution.py:483
  14.3 0.7 %collective-permute-start.3 = (bf16[24,1024]{1,0:T(8,128)(2,1)S(1)}, bf16[24,1024]{1,0:T(8,128)(2,1)S(1)}, u32[]{:S(2)}, u32[]{:S(2)}) collective-permute-start(bf16[24,1024]{1,0:T(8,128)(2,1)S(1)} %get-tuple-element.59.refs_3_.refs_4_), channel_id=1, source_target_pairs={{0,1},{1,0},{2,3},{3,2},{4,5},{5,4},{6,7},{7,6},{8,9},{9,8},{10,11... | collective-permute-start | bytes 147464 | tf_op jit(solution)/shard_map/ppermute | solution.py:483
  15.0 4.2 %fetch_late.1 = (bf16[2048,512]{1,0:T(8,128)(2,1)S(1)}, bf16[2048,512]{1,0:T(8,128)(2,1)S(1)}, bf16[2048,512]{1,0:T(8,128)(2,1)S(1)}, bf16[2048,512]{1,0:T(8,128)(2,1)S(1)}, bf16[2048,512]{1,0:T(8,128)(2,1)S(1)}) custom-call(bf16[2048,4096]{1,0:T(8,128)(2,1)} %refs_0_.11, bf16[2048,4096]{1,0:T(8,128)(2,1)} %refs_1_.11, bf16[4096,2048]{1,0:T(8,128)(2,1)} %refs_2_.13, ...), custom_call_target="tpu_custom_call" | custom-call | bytes 10485760 | tf_op jit(solution)/shard_map/fetch_late/pallas_call | solution.py:33
  19.4 4.2 %project_first.1 = (bf16[48,2432]{1,0:T(8,128)(2,1)S(1)}, bf16[48,2176]{1,0:T(8,128)(2,1)S(1)}, bf16[48,2048]{1,0:T(8,128)(2,1)S(1)}, f32[48,8192]{1,0:T(8,128)S...) custom-call(s32[1,3,3,1,4]{4,3,2,1,0:T(1,128)} %bitcast.5, ...), custom_call_target="tpu_custom_call" | custom-call | bytes 1024 | tf_op jit(solution)/shard_map/project_first/pallas_call | solution.py:33
  23.7 1.6 %fetch_between.1.refs_2_.refs_13_ = bf16[2048,512]{1,0:T(8,128)(2,1)S(1)} custom-call(bf16[2048,4096]{1,0:T(8,128)(2,1)} %refs_0_.11, bf16[2048,4096]{1,0:T(8,128)(2,1)} %refs_1_.11, bf16[4096,2048]{1,0:T(8,128)(2,1)} %refs_2_.13, bf16[48,2432]{1,0:T(8,128)(2,1)S(1)} %get-tuple-element.71.refs_3_), custom_call_target="tpu_custom_call" | custom-call | bytes 2097152 | tf_op jit(solution)/shard_map/fetch_between/pallas_call | solution.py:33
  25.5 1.6 %collective-permute-start.7 = (bf16[48,2176]{1,0:T(8,128)(2,1)S(1)}, bf16[48,2176]{1,0:T(8,128)(2,1)S(1)}, u32[]{:S(2)}, u32[]{:S(2)}) collective-permute-start(bf16[48,2176]{1,0:T(8,128)(2,1)S(1)} %chip_sum_first.1.refs_14_.refs_0_), channel_id=1, source_target_pairs={{0,8},{4,12},{8,0},{12,4},{1,9},{5,13},{9,1},{13,5},{2,10},{6,14},... | collective-permute-start | bytes 626696 | tf_op jit(solution)/shard_map/ppermute | solution.py:483
  27.0 3.0 %project_next.1 = (bf16[48,1024]{1,0:T(8,128)(2,1)S(1)}, bf16[48,1024]{1,0:T(8,128)(2,1)S(1)}, bf16[48,1024]{1,0:T(8,128)(2,1)S(1)}, bf16[48,1024]{1,0:T(8,128)(...) custom-call(bf16[1,1,4,128,128]{4,3,2,1,0:T(8,128)(2,1)} %refs_0_.10, ...), custom_call_target="tpu_custom_call" | custom-call | flops 805306368 | bytes 16777216 | tf_op jit(solution)/shard_map/project_next/pallas_call | solution.py:33
  30.6 0.8 %collective-permute-done.8.refs_1_ = bf16[48,1024]{1,0:T(8,128)(2,1)S(1)} collective-permute-done((bf16[48,1024]{1,0:T(8,128)(2,1)S(1)}, bf16[48,1024]{1,0:T(8,128)(2,1)S(1)}, u32[]{:S(2)}, u32[]{:S(2)}) %collective-permute-start.8) | collective-permute-done | bytes 98336 | tf_op jit(solution)/shard_map/ppermute | solution.py:483
  31.5 0.6 %collective-permute-start.9 = (bf16[48,1024]{1,0:T(8,128)(2,1)S(1)}, bf16[48,1024]{1,0:T(8,128)(2,1)S(1)}, u32[]{:S(2)}, u32[]{:S(2)}) collective-permute-start(bf16[48,1024]{1,0:T(8,128)(2,1)S(1)} %chip_sum_next.2.refs_2_), channel_id=1, source_target_pairs={{0,8},{4,12},{8,0},{12,4},{1,9},{5,13},{9,1},{13,5},{2,10},{6,14},... | collective-permute-start | bytes 294920 | tf_op jit(solution)/shard_map/ppermute | solution.py:483
  32.1 1.6 %collective-permute-start.11 = (bf16[48,1024]{1,0:T(8,128)(2,1)S(1)}, bf16[48,1024]{1,0:T(8,128)(2,1)S(1)}, u32[]{:S(2)}, u32[]{:S(2)}) collective-permute-start(bf16[48,1024]{1,0:T(8,128)(2,1)S(1)} %chip_sum_next.3.refs_3_.refs_4_), channel_id=1, source_target_pairs={{0,8},{4,12},{8,0},{12,4},{1,9},{5,13},{9,1},{13,5},{2,10},{6,14},... | collective-permute-start | bytes 294920 | tf_op jit(solution)/shard_map/ppermute | solution.py:483
  33.6 4.1 %fetch_down.1 = (bf16[512,2048]{1,0:T(8,128)(2,1)S(1)}, bf16[512,2048]{1,0:T(8,128)(2,1)S(1)}, bf16[512,2048]{1,0:T(8,128)(2,1)S(1)}, bf16[512,2048]{1,0:T(8,128)(2,1)S(1)}, bf16[512,2048]{1,0:T(8,128)(2,1)S(1)}) custom-call(bf16[2048,4096]{1,0:T(8,128)(2,1)} %refs_0_.11, bf16[2048,4096]{1,0:T(8,128)(2,1)} %refs_1_.11, bf16[4096,2048]{1,0:T(8,128)(2,1)} %refs_2_.13, ...), custom_call_target="tpu_custom_call" | custom-call | bytes 10485760 | tf_op jit(solution)/shard_map/fetch_down/pallas_call | solution.py:33
  37.8 0.8 %collective-permute-done.11.refs_5_ = bf16[48,1024]{1,0:T(8,128)(2,1)S(1)} collective-permute-done((bf16[48,1024]{1,0:T(8,128)(2,1)S(1)}, bf16[48,1024]{1,0:T(8,128)(2,1)S(1)}, u32[]{:S(2)}, u32[]{:S(2)}) %collective-permute-start.11) | collective-permute-done | bytes 98336 | tf_op jit(solution)/shard_map/ppermute | solution.py:483
  38.8 1.6 %down_mine.1.refs_2_ = f32[48,2048]{1,0:T(8,128)S(1)} custom-call(bf16[48,2048]{1,0:T(8,128)(2,1)S(1)} %hidden.1.refs_0_.refs_3_, bf16[512,2048]{1,0:T(8,128)(2,1)S(1)} %get-tuple-element.87.refs_1_, bf16[512,2048]{1,0:T(8,128)(2,1)S(1)} %get-tuple-element.88.refs_2_, bf16[512,2048]{1,0:T(8,128)(2,1)S(1)} %get-tuple-element.89.refs_3_, ...), custom_call_target="tpu_custom_call" | custom-call | flops 402653184 | bytes 8388608 | tf_op jit(solution)/shard_map/down_mine/pallas_call | solution.py:33
  40.4 1.9 %down.1 = (bf16[24,1024]{1,0:T(8,128)(2,1)S(1)}, bf16[24,1024]{1,0:T(8,128)(2,1)S(1)}, bf16[24,1024]{1,0:T(8,128)(2,1)S(1)}, bf16[24,1024]{1,0:T(8,128)(2,1)S(1)}, bf16[48,256]{1,0:T(8,128)(2,1)S(1)}) custom-call(s32[1,3,3,1,4]{4,3,2,1,0:T(1,128)} %bitcast.6, bf16[1,1,4,128,128]{4,3,2,1,0:T(8,128)(2,1)S(1)} %get-tuple-element.81.refs_1_, ...), custom_call_target="tpu_custom_call" | custom-call | bytes 1024 | tf_op jit(solution)/shard_map/down/pallas_call | solution.py:33
  42.3 1.2 %collective-permute-start.14 = (bf16[24,1024]{1,0:T(8,128)(2,1)S(1)}, bf16[24,1024]{1,0:T(8,128)(2,1)S(1)}, u32[]{:S(2)}, u32[]{:S(2)}) collective-permute-start(bf16[24,1024]{1,0:T(8,128)(2,1)S(1)} %get-tuple-element.97), channel_id=1, source_target_pairs={{0,1},{1,0},{2,3},{3,2},{4,5},{5,4},{6,7},{7,6},{8,9},{9,8},{10,11... | collective-permute-start | bytes 147464 | tf_op jit(solution)/shard_map/ppermute | solution.py:483
  43.5 2.9 %collective-permute-start.15 = (bf16[24,1024]{1,0:T(8,128)(2,1)S(1)}, bf16[24,1024]{1,0:T(8,128)(2,1)S(1)}, u32[]{:S(2)}, u32[]{:S(2)}) collective-permute-start(bf16[24,1024]{1,0:T(8,128)(2,1)S(1)} %get-tuple-element.98), channel_id=1, source_target_pairs={{0,2},{1,3},{2,0},{3,1},{4,6},{5,7},{6,4},{7,5},{8,10},{9,11},{10,... | collective-permute-start | bytes 147464 | tf_op jit(solution)/shard_map/ppermute | solution.py:483
  47.3 3.3 %collective-permute-done.13.refs_2_ = bf16[48,256]{1,0:T(8,128)(2,1)S(1)} collective-permute-done((bf16[48,256]{1,0:T(8,128)(2,1)S(1)}, bf16[48,256]{1,0:T(8,128)(2,1)S(1)}, u32[]{:S(2)}, u32[]{:S(2)}) %collective-permute-start.13) | collective-permute-done | bytes 24608 | tf_op jit(solution)/shard_map/ppermute | solution.py:483
  50.7 0.6 %copy.14 = bf16[3,8192]{1,0:T(4,128)(2,1)} copy(bf16[3,8192]{1,0:T(4,128)(2,1)S(1)} %attended.1) | data formatting | bytes 98304
  51.4 0.9 %collective-permute-done.16.refs_3_ = bf16[24,1024]{1,0:T(8,128)(2,1)S(1)} collective-permute-done((bf16[24,1024]{1,0:T(8,128)(2,1)S(1)}, bf16[24,1024]{1,0:T(8,128)(2,1)S(1)}, u32[]{:S(2)}, u32[]{:S(2)}) %collective-permute-start.16) | collective-permute-done | bytes 49184 | tf_op jit(solution)/shard_map/ppermute | solution.py:483
  52.3 0.6 %copy.15 = bf16[12,2048]{1,0:T(8,128)(2,1)} copy(bf16[12,2048]{1,0:T(8,128)(2,1)S(1)} %finish.1) | data formatting | bytes 98304
  (28 shorter events, 3.2 us)
Async XLA Ops:
  1.8 6.9 %collective-permute-start = (bf16[4,16,512]{2,1,0:T(8,128)(2,1)S(1)}, bf16[4,16,512]{2,1,0:T(8,128)(2,1)S(1)}, u32[]{:S(2)}, u32[]{:S(2)}) collective-permute-start(bf16[4,16,512]{2,1,0:T(8,128)(2,1)S(1)} %get-tuple-element.52), channel_id=1, source_target_pairs={{0,4},{4,0},{8,12},{12,8},{1,5},{5,1},{9,13},{13,9},{2,6},{6,2},{1... | collective-permute-start | bytes 196616 | tf_op jit(solution)/shard_map/ppermute | solution.py:483
  2.3 6.4 %collective-permute-start.1 = (bf16[4,16,512]{2,1,0:T(8,128)(2,1)S(1)}, bf16[4,16,512]{2,1,0:T(8,128)(2,1)S(1)}, u32[]{:S(2)}, u32[]{:S(2)}) collective-permute-start(bf16[4,16,512]{2,1,0:T(8,128)(2,1)S(1)} %get-tuple-element.53), channel_id=1, source_target_pairs={{0,8},{4,12},{8,0},{12,4},{1,9},{5,13},{9,1},{13,5},{2,10},{6,14},... | collective-permute-start | bytes 196616 | tf_op jit(solution)/shard_map/ppermute | solution.py:483
  4.9 4.0 %collective-permute-start.2 = (bf16[4,16,512]{2,1,0:T(8,128)(2,1)S(1)}, bf16[4,16,512]{2,1,0:T(8,128)(2,1)S(1)}, u32[]{:S(2)}, u32[]{:S(2)}) collective-permute-start(bf16[4,16,512]{2,1,0:T(8,128)(2,1)S(1)} %get-tuple-element.54), channel_id=1, source_target_pairs={{0,12},{4,8},{8,4},{12,0},{1,13},{5,9},{9,5},{13,1},{2,14},{6,10},... | collective-permute-start | bytes 196616 | tf_op jit(solution)/shard_map/ppermute | solution.py:483
  10.5 8.6 %collective-permute-start.5 = (bf16[24,1024]{1,0:T(8,128)(2,1)S(1)}, bf16[24,1024]{1,0:T(8,128)(2,1)S(1)}, u32[]{:S(2)}, u32[]{:S(2)}) collective-permute-start(bf16[24,1024]{1,0:T(8,128)(2,1)S(1)} %get-tuple-element.59.refs_3_.refs_4_), channel_id=1, source_target_pairs={{0,3},{1,2},{2,1},{3,0},{4,7},{5,6},{6,5},{7,4},{8,11},{9,10},{10,... | collective-permute-start | bytes 147464 | tf_op jit(solution)/shard_map/ppermute | solution.py:483
  14.3 5.1 %collective-permute-start.4 = (bf16[24,1024]{1,0:T(8,128)(2,1)S(1)}, bf16[24,1024]{1,0:T(8,128)(2,1)S(1)}, u32[]{:S(2)}, u32[]{:S(2)}) collective-permute-start(bf16[24,1024]{1,0:T(8,128)(2,1)S(1)} %get-tuple-element.59.refs_3_.refs_4_), channel_id=1, source_target_pairs={{0,2},{1,3},{2,0},{3,1},{4,6},{5,7},{6,4},{7,5},{8,10},{9,11},{10,... | collective-permute-start | bytes 147464 | tf_op jit(solution)/shard_map/ppermute | solution.py:483
  14.3 5.1 %collective-permute-start.3 = (bf16[24,1024]{1,0:T(8,128)(2,1)S(1)}, bf16[24,1024]{1,0:T(8,128)(2,1)S(1)}, u32[]{:S(2)}, u32[]{:S(2)}) collective-permute-start(bf16[24,1024]{1,0:T(8,128)(2,1)S(1)} %get-tuple-element.59.refs_3_.refs_4_), channel_id=1, source_target_pairs={{0,1},{1,0},{2,3},{3,2},{4,5},{5,4},{6,7},{7,6},{8,9},{9,8},{10,11... | collective-permute-start | bytes 147464 | tf_op jit(solution)/shard_map/ppermute | solution.py:483
  23.6 1.7 %collective-permute-start.6 = (bf16[48,2432]{1,0:T(8,128)(2,1)S(1)}, bf16[48,2432]{1,0:T(8,128)(2,1)S(1)}, u32[]{:S(2)}, u32[]{:S(2)}) collective-permute-start(bf16[48,2432]{1,0:T(8,128)(2,1)S(1)} %get-tuple-element.71.refs_3_), channel_id=1, source_target_pairs={{0,4},{4,0},{8,12},{12,8},{1,5},{5,1},{9,13},{13,9},{2,6},{6,2},{1... | collective-permute-start | bytes 700424 | tf_op jit(solution)/shard_map/ppermute | solution.py:483
  25.5 13.1 %collective-permute-start.7 = (bf16[48,2176]{1,0:T(8,128)(2,1)S(1)}, bf16[48,2176]{1,0:T(8,128)(2,1)S(1)}, u32[]{:S(2)}, u32[]{:S(2)}) collective-permute-start(bf16[48,2176]{1,0:T(8,128)(2,1)S(1)} %chip_sum_first.1.refs_14_.refs_0_), channel_id=1, source_target_pairs={{0,8},{4,12},{8,0},{12,4},{1,9},{5,13},{9,1},{13,5},{2,10},{6,14},... | collective-permute-start | bytes 626696 | tf_op jit(solution)/shard_map/ppermute | solution.py:483
  30.1 1.4 %collective-permute-start.8 = (bf16[48,1024]{1,0:T(8,128)(2,1)S(1)}, bf16[48,1024]{1,0:T(8,128)(2,1)S(1)}, u32[]{:S(2)}, u32[]{:S(2)}) collective-permute-start(bf16[48,1024]{1,0:T(8,128)(2,1)S(1)} %get-tuple-element.83), channel_id=1, source_target_pairs={{0,4},{4,0},{8,12},{12,8},{1,5},{5,1},{9,13},{13,9},{2,6},{6,2},{1... | collective-permute-start | bytes 294920 | tf_op jit(solution)/shard_map/ppermute | solution.py:483
  30.3 1.7 %collective-permute-start.10 = (bf16[48,1024]{1,0:T(8,128)(2,1)S(1)}, bf16[48,1024]{1,0:T(8,128)(2,1)S(1)}, u32[]{:S(2)}, u32[]{:S(2)}) collective-permute-start(bf16[48,1024]{1,0:T(8,128)(2,1)S(1)} %get-tuple-element.85), channel_id=1, source_target_pairs={{0,4},{4,0},{8,12},{12,8},{1,5},{5,1},{9,13},{13,9},{2,6},{6,2},{1... | collective-permute-start | bytes 294920 | tf_op jit(solution)/shard_map/ppermute | solution.py:483
  31.5 6.3 %collective-permute-start.9 = (bf16[48,1024]{1,0:T(8,128)(2,1)S(1)}, bf16[48,1024]{1,0:T(8,128)(2,1)S(1)}, u32[]{:S(2)}, u32[]{:S(2)}) collective-permute-start(bf16[48,1024]{1,0:T(8,128)(2,1)S(1)} %chip_sum_next.2.refs_2_), channel_id=1, source_target_pairs={{0,8},{4,12},{8,0},{12,4},{1,9},{5,13},{9,1},{13,5},{2,10},{6,14},... | collective-permute-start | bytes 294920 | tf_op jit(solution)/shard_map/ppermute | solution.py:483
  32.1 6.4 %collective-permute-start.11 = (bf16[48,1024]{1,0:T(8,128)(2,1)S(1)}, bf16[48,1024]{1,0:T(8,128)(2,1)S(1)}, u32[]{:S(2)}, u32[]{:S(2)}) collective-permute-start(bf16[48,1024]{1,0:T(8,128)(2,1)S(1)} %chip_sum_next.3.refs_3_.refs_4_), channel_id=1, source_target_pairs={{0,8},{4,12},{8,0},{12,4},{1,9},{5,13},{9,1},{13,5},{2,10},{6,14},... | collective-permute-start | bytes 294920 | tf_op jit(solution)/shard_map/ppermute | solution.py:483
  38.7 1.6 %collective-permute-start.12 = (bf16[48,2048]{1,0:T(8,128)(2,1)S(1)}, bf16[48,2048]{1,0:T(8,128)(2,1)S(1)}, u32[]{:S(2)}, u32[]{:S(2)}) collective-permute-start(bf16[48,2048]{1,0:T(8,128)(2,1)S(1)} %hidden.1.refs_0_.refs_3_), channel_id=1, source_target_pairs={{0,4},{4,0},{8,12},{12,8},{1,5},{5,1},{9,13},{13,9},{2,6},{6,2},{1... | collective-permute-start | bytes 589832 | tf_op jit(solution)/shard_map/ppermute | solution.py:483
  42.3 9.1 %collective-permute-start.14 = (bf16[24,1024]{1,0:T(8,128)(2,1)S(1)}, bf16[24,1024]{1,0:T(8,128)(2,1)S(1)}, u32[]{:S(2)}, u32[]{:S(2)}) collective-permute-start(bf16[24,1024]{1,0:T(8,128)(2,1)S(1)} %get-tuple-element.97), channel_id=1, source_target_pairs={{0,1},{1,0},{2,3},{3,2},{4,5},{5,4},{6,7},{7,6},{8,9},{9,8},{10,11... | collective-permute-start | bytes 147464 | tf_op jit(solution)/shard_map/ppermute | solution.py:483
  43.5 7.9 %collective-permute-start.15 = (bf16[24,1024]{1,0:T(8,128)(2,1)S(1)}, bf16[24,1024]{1,0:T(8,128)(2,1)S(1)}, u32[]{:S(2)}, u32[]{:S(2)}) collective-permute-start(bf16[24,1024]{1,0:T(8,128)(2,1)S(1)} %get-tuple-element.98), channel_id=1, source_target_pairs={{0,2},{1,3},{2,0},{3,1},{4,6},{5,7},{6,4},{7,5},{8,10},{9,11},{10,... | collective-permute-start | bytes 147464 | tf_op jit(solution)/shard_map/ppermute | solution.py:483
  46.4 5.9 %collective-permute-start.16 = (bf16[24,1024]{1,0:T(8,128)(2,1)S(1)}, bf16[24,1024]{1,0:T(8,128)(2,1)S(1)}, u32[]{:S(2)}, u32[]{:S(2)}) collective-permute-start(bf16[24,1024]{1,0:T(8,128)(2,1)S(1)} %get-tuple-element.99), channel_id=1, source_target_pairs={{0,3},{1,2},{2,1},{3,0},{4,7},{5,6},{6,5},{7,4},{8,11},{9,10},{10,... | collective-permute-start | bytes 147464 | tf_op jit(solution)/shard_map/ppermute | solution.py:483
  46.7 3.8 %collective-permute-start.13 = (bf16[48,256]{1,0:T(8,128)(2,1)S(1)}, bf16[48,256]{1,0:T(8,128)(2,1)S(1)}, u32[]{:S(2)}, u32[]{:S(2)}) collective-permute-start(bf16[48,256]{1,0:T(8,128)(2,1)S(1)} %get-tuple-element.95), channel_id=1, source_target_pairs={{0,8},{4,12},{8,0},{12,4},{1,9},{5,13},{9,1},{13,5},{2,10},{6,14},... | collective-permute-start | bytes 73736 | tf_op jit(solution)/shard_map/ppermute | solution.py:483

commit v4 on v3

--- a/solution.py
+++ b/solution.py
@@ -12,7 +12,7 @@
 HEAD_DIM = 128
 GROUP = HEADS // KV_HEADS
 MIB = 1 << 20
-FETCH = (0, 4, 1, 5, 5, 1, 3, 5)
+FETCH = (0, 3, 1, 4, 5, 1, 2, 1, 6, 1)
 CUTS = (4, 6)
 BF16 = jnp.bfloat16
 F32 = jnp.float32
@@ -20,7 +20,7 @@
 HBM = pltpu.HBM
 
 
-def call(kernel, name, ins, outs, scratch=(), limit=8, cost=None, after=()):
+def call(kernel, name, ins, outs, scratch=(), limit=8, cost=None, after=(), out=VMEM):
     if cost is None:
         cost = pl.CostEstimate(flops=0, bytes_accessed=1024, transcendentals=0)
     count = len(ins)
@@ -34,8 +34,8 @@
             body,
             name=name,
             in_specs=[pl.BlockSpec(memory_space=s) for _, s in ins],
-            out_specs=[pl.BlockSpec(memory_space=VMEM) for _ in outs],
-            out_shape=[VMEM(shape, dtype) for shape, dtype in outs],
+            out_specs=[pl.BlockSpec(memory_space=out) for _ in outs],
+            out_shape=[out(shape, dtype) for shape, dtype in outs],
             scratch_shapes=list(scratch),
             cost_estimate=cost,
             compiler_params=pltpu.CompilerParams(vmem_limit_bytes=limit * MIB),
@@ -163,6 +163,7 @@
 
 def attend_kernel(z, ctx, jobs, list_hbm, count_hbm, *rest):
     weights, pieces, rest = rest[:3], rest[3 : 3 + z.toks], rest[3 + z.toks :]
+    pieces = pieces[:1] + pieces[-1:] + pieces[1:-1]
     send_ref, back_refs, rest = rest[0], rest[1 : 1 + z.toks], rest[1 + z.toks :]
     blocks, rest = rest[: len(jobs)], rest[len(jobs) :]
     cache, req, query, own_key, own_value, alive, mixed_all, list_ref, count_ref, table_sems, sems = rest
@@ -347,31 +348,18 @@
         send_ref[: ref.shape[0], lane : lane + HEAD_DIM] = ref[...]
 
 
-def next_project_kernel(z, jobs, delta_hbm, *rest):
-    count = sum(len(some) for some in z.blocks_of[1:])
-    here = sum(len(job) > 2 for job in jobs)
+def next_project_kernel(z, q, jobs, *rest):
     weights, (source, extra), rest = rest[:3], rest[3:5], rest[5:]
-    blocks, rest = rest[: count - here], rest[count - here :]
-    sums = 2 * (z.chunks - 1)
-    outs, (delta_ref, *fetched) = rest[:sums], rest[sums:-1]
-    copies = start_copies(
-        list(zip(weight_blocks(z, jobs, weights) + [delta_hbm], fetched + [delta_ref])), rest[-1]
-    )
-    blocks = list(blocks) + fetched[:here]
-    steps = []
-    for q in range(1, z.chunks):
-        refs = blocks[len(steps) : len(steps) + len(z.blocks_of[q])]
-        steps += project_steps(z, q, source, extra, refs, outs[2 * q - 2], outs[2 * q - 1])
+    blocks, rest = rest[: len(z.blocks_of[q])], rest[len(z.blocks_of[q]) :]
+    send_ref, keep_ref, *fetched, sems = rest
+    copies = start_copies(list(zip(weight_blocks(z, jobs, weights), fetched)), sems)
 
     @after_starts
     def _():
-        for step in steps[: count - here]:
+        for step in project_steps(z, q, source, extra, blocks, send_ref, keep_ref):
             step()
 
-    for n in range(here):
-        copies[n].wait()
-        after_starts(steps[count - here + n])
-    for copy in copies[here:]:
+    for copy in copies:
         copy.wait()
 
 
@@ -412,8 +400,14 @@
         total[:, lanes] = value
 
 
-def down_mine_kernel(z, mine, *rest):
-    down_products(z, True, mine, rest[:-1], rest[-1])
+def down_mine_kernel(z, jobs, *rest):
+    weights, mine, rest = rest[:3], rest[3], rest[4:]
+    blocks, rest = rest[: len(z.downs) // 2], rest[len(z.downs) // 2 :]
+    total, *fetched, sems = rest
+    copies = start_copies(list(zip(weight_blocks(z, jobs, weights), fetched)), sems)
+    after_starts(lambda: down_products(z, True, mine, blocks, total))
+    for copy in copies:
+        copy.wait()
 
 
 def down_kernel(z, index_hbm, delta_ref, before, mine, other, from_core, *rest):
@@ -447,36 +441,42 @@
         outs[s][...] = fold[...].astype(BF16)
 
 
-def finish_kernel(z, *refs):
-    parts, out_ref = refs[: z.cols], refs[z.cols]
-    total = sum(ref[...].astype(F32) for ref in parts)
-    half = total.shape[1]
-    out_ref[:, :half] = total[: z.lane_slots].astype(BF16)
-    out_ref[:, half:] = total[z.lane_slots :].astype(BF16)
-
-
-def return_kernel(z, own, from_core, *refs):
-    chips = z.toks // 2
-    parts, (out_ref, rows) = refs[: chips - 1], refs[chips - 1 :]
+def finish_kernel(z, own, from_core, *refs):
+    others = z.toks // 2 - 1
+    across, parts, rest = refs[:others], refs[others : others + z.cols], refs[others + z.cols :]
+    attended_hbm, out_hbm, attended, out, rows, sems = rest
     tok = lax.axis_index("tok")
     block = z.cap * z.group
     count = z.kvs * block
     tail = z.tail + HEAD_DIM
     for s in range(z.toks):
         if s == 0:
-            rows[...] = own[...].astype(F32)
+            rows[s] = own[...].astype(F32)
         elif s == 1:
-            rows[...] = from_core[:count, tail : tail + HEAD_DIM].astype(F32)
+            rows[s] = from_core[:count, tail : tail + HEAD_DIM].astype(F32)
         else:
             lane = s % 2 * HEAD_DIM
-            rows[...] = parts[s // 2 - 1][:, lane : lane + HEAD_DIM].astype(F32)
+            rows[s] = across[s // 2 - 1][:, lane : lane + HEAD_DIM].astype(F32)
         first = pl.multiple_of((tok ^ s) * z.heads * HEAD_DIM, HEAD_DIM)
         for j in range(z.kvs):
             for h in range(z.group):
                 to = first + (j * z.group + h) * HEAD_DIM
-                out_ref[:, pl.ds(to, HEAD_DIM)] = rows[
-                    pl.ds(j * block + h, z.cap, stride=z.group), :
+                attended[:, pl.ds(to, HEAD_DIM)] = rows[
+                    s, pl.ds(j * block + h, z.cap, stride=z.group), :
                 ].astype(BF16)
+    copies = start_copies([(attended, attended_hbm)], sems)
+
+    @after_starts
+    def _():
+        total = sum(ref[...].astype(F32) for ref in parts)
+        half = total.shape[1]
+        out[:, :half] = total[: z.lane_slots].astype(BF16)
+        out[:, half:] = total[z.lane_slots :].astype(BF16)
+
+    copy = pltpu.make_async_copy(out, out_hbm, sems.at[1])
+    copy.start()
+    for copy in copies + [copy]:
+        copy.wait()
 
 
 def swap(array, axis, size, distance):
@@ -519,7 +519,7 @@
     cuts = [0]
     for count in FETCH:
         cuts.append(cuts[-1] + count)
-    first, early, middle, late, beside, between, last, final = [jobs[a:b] for a, b in zip(cuts, cuts[1:])]
+    first, early, middle, late, beside, between, *lasts, final, ending = [jobs[a:b] for a, b in zip(cuts, cuts[1:])]
     weights = [(gate_weight, HBM), (up_weight, HBM), (down_weight, HBM)]
 
     def shapes(some):
@@ -562,7 +562,7 @@
     send, *rest = call(
         functools.partial(attend_kernel, z, ctx, middle),
         "attend",
-        [(route_list, HBM), (route_count, HBM)] + weights + [(p, VMEM) for p in pieces],
+        [(route_list, HBM), (route_count, HBM)] + weights + [(p, VMEM) for p in pieces[:1] + pieces[2:] + pieces[1:2]],
         [((z.kvs * z.lane_slots, z.group * HEAD_DIM), BF16)]
         + [((back_rows, HEAD_DIM), BF16)] * toks
         + shapes(middle),
@@ -638,26 +638,24 @@
             after=fetched[-1:],
         )
     ]
-    sizes = [2 * size for _, size in z.parts[1:]]
-    *sums, down_delta = call(
-        functools.partial(next_project_kernel, z, last),
-        "project_next",
-        [(down_delta, HBM)] + weights + [(a, VMEM) for a in [source, extra] + blocks[: used - len(z.blocks_of[0])]],
-        [((z.rows, size), BF16) for size in sizes for _ in range(2)]
-        + [(down_delta.shape, BF16)]
-        + shapes(last),
-        [dma((len(last) + 1,))],
-        cost=pl.CostEstimate(
-            flops=4 * z.rows * features * sum(sizes),
-            bytes_accessed=4 * features * sum(sizes),
-            transcendentals=0,
-        ),
-        after=totals[0][:1],
-    )
-    rest = sums[2 * len(sizes) :] + [down_delta]
-    down_delta, blocks = rest[0], blocks + rest[1:]
-    for q, size in enumerate(sizes):
-        sent, kept = sums[2 * q : 2 * q + 2]
+    for q, jobs in enumerate(lasts, 1):
+        size = 2 * z.parts[q][1]
+        place = sum(len(some) for some in z.blocks_of[1:q])
+        sent, kept, *fetched = call(
+            functools.partial(next_project_kernel, z, q, jobs),
+            "project_next",
+            weights
+            + [(a, VMEM) for a in [source, extra] + blocks[place : place + len(z.blocks_of[q])]],
+            [((z.rows, size), BF16)] * 2 + shapes(jobs),
+            [dma((len(jobs),))],
+            cost=pl.CostEstimate(
+                flops=4 * z.rows * features * size,
+                bytes_accessed=4 * features * size,
+                transcendentals=0,
+            ),
+            after=totals[0],
+        )
+        blocks += fetched
         other = swap(sent, "tok", toks, 1)
         totals.append(
             call(
@@ -671,16 +669,17 @@
         total + [swap(total[0], "tok", toks, 2 * s) for s in range(1, chips)]
         for total in totals
     ]
-    fetched = call(
-        functools.partial(fetch_kernel, z, final, [], 0),
+    down_delta, *fetched = call(
+        functools.partial(fetch_kernel, z, final, [down_delta], 0),
         "fetch_down",
-        weights,
-        shapes(final),
-        [dma((len(final),))],
+        weights + [(down_delta, HBM)],
+        [(down_delta.shape, BF16)] + shapes(final),
+        [dma((len(final) + 1,))],
         cost=traffic(final),
         after=totals[-1],
     )
-    down_blocks = (blocks + fetched)[-len(z.downs) :]
+    blocks += fetched
+    down_blocks = blocks[used - len(z.blocks_of[0]) :]
     (hidden,) = call(
         functools.partial(hidden_kernel, z, width),
         "hidden",
@@ -689,15 +688,17 @@
         after=fetched[-1:],
     )
     half = len(z.downs) // 2
-    (before,) = call(
-        functools.partial(down_mine_kernel, z),
+    before, *fetched = call(
+        functools.partial(down_mine_kernel, z, ending),
         "down_mine",
-        [(a, VMEM) for a in [hidden] + down_blocks[:half]],
-        [((z.rows, out_width), F32)],
+        weights + [(a, VMEM) for a in [hidden] + down_blocks[:half]],
+        [((z.rows, out_width), F32)] + shapes(ending),
+        [dma((max(1, len(ending)),))],
         cost=pl.CostEstimate(
             flops=z.rows * units * out_width, bytes_accessed=units * out_width, transcendentals=0
         ),
     )
+    down_blocks += fetched
     parts = call(
         functools.partial(down_kernel, z),
         "down",
@@ -717,18 +718,18 @@
     parts, across = parts[:cols], parts[cols:]
     parts = [parts[0]] + [swap(parts[s], "col", cols, s) for s in range(1, cols)]
     across = [swap(rows, "tok", toks, 2 * s + 2) for s, rows in enumerate(across)]
-    (attended,) = call(
-        functools.partial(return_kernel, z),
-        "attended",
-        [(a, VMEM) for a in [back[0], from_core] + across],
-        [((cap, width), BF16)],
-        [pltpu.VMEM((back_rows, HEAD_DIM), F32)],
-    )
-    (ffn_out,) = call(
+    attended, ffn_out = call(
         functools.partial(finish_kernel, z),
         "finish",
-        [(p, VMEM) for p in parts],
-        [((z.lane_slots, out_width), BF16)],
+        [(a, VMEM) for a in [back[0], from_core] + across + parts[::-1]],
+        [((cap, width), BF16), ((z.lane_slots, out_width), BF16)],
+        [
+            pltpu.VMEM((cap, width), BF16),
+            pltpu.VMEM((z.lane_slots, out_width), BF16),
+            pltpu.VMEM((toks, back_rows, HEAD_DIM), F32),
+            dma((2,)),
+        ],
+        out=HBM,
     )
     return attended, ffn_out
 

time: 53.2 us -> 52.1 us (0.979)
  local copies, waits for them, and re-layouts: 1.26 us -> 0 us
  Pallas kernels: 27.6 us -> 28.6 us
  waiting for transfers between devices: 6.26 us -> 5.32 us
    unnamed x2 -> x0, local copies, waits for them, and re-layouts: 1.26 us -> none
    pallas_call x16, Pallas kernels: 27.6 us -> 28.6 us  [call(): pl.pallas_call(body, name=name, in_specs=[pl.BlockSpec(memory_space=s) fo...]
    ppermute x17, waiting for transfers between devices: 6.26 us -> 5.32 us  [swap(): return lax.ppermute(array, axis, [(i, i ^ distance) for i in range(size)])]
  transfers between devices with their start and end apart: 17 -> 17, of which waited for: 6 -> 5; matrix products, arithmetic and copies ran while one was open for 1% -> 0% of each run, Pallas kernels for 35% -> 36%
where the time goes in v4:
time: 52.1 us; the launch traced here: 51.8 us
  Pallas kernels  28.6 us (55%)
  starting transfers between devices  17.1 us (33%)
  waiting for transfers between devices  5.32 us (10%)
  between operations  0.8 us (2%)
    pallas_call x16, Pallas kernels, call(): pl.pallas_call(body, name=name, in_specs=[pl.BlockSpec(memory_space=s) fo...  28.6 us
    ppermute x17, starting transfers between devices, swap(): return lax.ppermute(array, axis, [(i, i ^ distance) for i in range(size)])  17.1 us
    ppermute x17, waiting for transfers between devices, swap(): return lax.ppermute(array, axis, [(i, i ^ distance) for i in range(size)])  5.32 us
  transfers between devices with their start and end apart: 17, of which 5 were waited for; matrix products, arithmetic and copies ran while one was open for 0% of the time, Pallas kernels for 36%

profile of v4, /device:TPU:0, one launch (start us, length us, event | category | flops | bytes accessed | tf_op | source)
XLA Modules:
  0.0 51.8 jit_solution(16032947832140774409)
XLA Ops:
  0.6 1.1 %pack.1 = (bf16[4,16,512]{2,1,0:T(8,128)(2,1)S(1)}, bf16[4,16,512]{2,1,0:T(8,128)(2,1)S(1)}, bf16[4,16,512]{2,1,0:T(8,128)(2,1)S(1)}, bf16[4,16,512]{2,1,0:T(8,128)(2,1)S(1)}) custom-call(bf16[2,10240]{1,0:T(2,128)(2,1)} %refs_0_.8, bf16[3,16,2048]{2,1,0:T(8,128)(2,1)} %refs_1_.8, bf16[2048,4096]{1,0:T(8,128)(2,1)} %refs_0_.15, bf16[2048,4096]{1,0:T(8,128)(2,1)} %refs_1_.15, ...), custom_call_target="tpu_custom_call" | custom-call | bytes 1024 | tf_op jit(solution)/shard_map/pack/pallas_call | solution.py:33
  1.8 3.0 %collective-permute-start = (bf16[4,16,512]{2,1,0:T(8,128)(2,1)S(1)}, bf16[4,16,512]{2,1,0:T(8,128)(2,1)S(1)}, u32[]{:S(2)}, u32[]{:S(2)}) collective-permute-start(bf16[4,16,512]{2,1,0:T(8,128)(2,1)S(1)} %get-tuple-element.53), channel_id=1, source_target_pairs={{0,8},{4,12},{8,0},{12,4},{1,9},{5,13},{9,1},{13,5},{2,10},{6,14},... | collective-permute-start | bytes 196616 | tf_op jit(solution)/shard_map/ppermute | solution.py:483
  5.0 3.1 %fetch_early.1 = (f32[1,2048]{1,0:T(1,128)S(1)}, bf16[1,1,4,128,128]{4,3,2,1,0:T(8,128)(2,1)S(1)}, bf16[1,1,4,128,128]{4,3,2,1,0:T(8,128)(2,1)S(1)}, bf16[2048,5...) custom-call(bf16[2048,4096]{1,0:T(8,128)(2,1)} %refs_0_.15, ...), custom_call_target="tpu_custom_call" | custom-call | bytes 6291456 | tf_op jit(solution)/shard_map/fetch_early/pallas_call | solution.py:33
  8.1 0.8 %collective-permute-done.1.refs_7_ = bf16[4,16,512]{2,1,0:T(8,128)(2,1)S(1)} collective-permute-done((bf16[4,16,512]{2,1,0:T(8,128)(2,1)S(1)}, bf16[4,16,512]{2,1,0:T(8,128)(2,1)S(1)}, u32[]{:S(2)}, u32[]{:S(2)}) %collective-permute-start.1) | collective-permute-done | bytes 65568 | tf_op jit(solution)/shard_map/ppermute | solution.py:483
  8.9 1.6 %attend.1 = (bf16[24,1024]{1,0:T(8,128)(2,1)S(1)}, bf16[48,128]{1,0:T(8,128)(2,1)S(1)}, bf16[48,128]{1,0:T(8,128)(2,1)S(1)}, bf16[48,128]{1,0:T(8,128)(2,1)S(1)}...) custom-call(s32[3,1,4]{2,1,0:T(1,128)} %bitcast.7, s32[1,4]{1,0:T(1,128)} %bitcast.8, ...), custom_call_target="tpu_custom_call" | custom-call | bytes 1024 | tf_op jit(solution)/shard_map/attend/pallas_call | solution.py:33
  10.5 3.7 %collective-permute-start.5 = (bf16[24,1024]{1,0:T(8,128)(2,1)S(1)}, bf16[24,1024]{1,0:T(8,128)(2,1)S(1)}, u32[]{:S(2)}, u32[]{:S(2)}) collective-permute-start(bf16[24,1024]{1,0:T(8,128)(2,1)S(1)} %get-tuple-element.60.refs_3_.refs_4_), channel_id=1, source_target_pairs={{0,3},{1,2},{2,1},{3,0},{4,7},{5,6},{6,5},{7,4},{8,11},{9,10},{10,... | collective-permute-start | bytes 147464 | tf_op jit(solution)/shard_map/ppermute | solution.py:483
  14.3 0.7 %collective-permute-start.3 = (bf16[24,1024]{1,0:T(8,128)(2,1)S(1)}, bf16[24,1024]{1,0:T(8,128)(2,1)S(1)}, u32[]{:S(2)}, u32[]{:S(2)}) collective-permute-start(bf16[24,1024]{1,0:T(8,128)(2,1)S(1)} %get-tuple-element.60.refs_3_.refs_4_), channel_id=1, source_target_pairs={{0,1},{1,0},{2,3},{3,2},{4,5},{5,4},{6,7},{7,6},{8,9},{9,8},{10,11... | collective-permute-start | bytes 147464 | tf_op jit(solution)/shard_map/ppermute | solution.py:483
  15.0 3.5 %fetch_late.1 = (bf16[2048,512]{1,0:T(8,128)(2,1)S(1)}, bf16[2048,512]{1,0:T(8,128)(2,1)S(1)}, bf16[2048,512]{1,0:T(8,128)(2,1)S(1)}, bf16[2048,512]{1,0:T(8,128)(2,1)S(1)}) custom-call(bf16[2048,4096]{1,0:T(8,128)(2,1)} %refs_0_.15, bf16[2048,4096]{1,0:T(8,128)(2,1)} %refs_1_.15, bf16[4096,2048]{1,0:T(8,128)(2,1)} %refs_2_.17, ...), custom_call_target="tpu_custom_call" | custom-call | bytes 8388608 | tf_op jit(solution)/shard_map/fetch_late/pallas_call | solution.py:33
  19.2 4.2 %project_first.1 = (bf16[48,2432]{1,0:T(8,128)(2,1)S(1)}, bf16[48,2176]{1,0:T(8,128)(2,1)S(1)}, bf16[48,2048]{1,0:T(8,128)(2,1)S(1)}, f32[48,8192]{1,0:T(8,128)S...) custom-call(s32[1,3,3,1,4]{4,3,2,1,0:T(1,128)} %bitcast.5, ...), custom_call_target="tpu_custom_call" | custom-call | bytes 1024 | tf_op jit(solution)/shard_map/project_first/pallas_call | solution.py:33
  23.5 1.6 %fetch_between.1.refs_2_.refs_6_ = bf16[2048,512]{1,0:T(8,128)(2,1)S(1)} custom-call(bf16[2048,4096]{1,0:T(8,128)(2,1)} %refs_0_.15, bf16[2048,4096]{1,0:T(8,128)(2,1)} %refs_1_.15, bf16[4096,2048]{1,0:T(8,128)(2,1)} %refs_2_.17, bf16[48,2432]{1,0:T(8,128)(2,1)S(1)} %get-tuple-element.71.refs_3_), custom_call_target="tpu_custom_call" | custom-call | bytes 2097152 | tf_op jit(solution)/shard_map/fetch_between/pallas_call | solution.py:33
  25.3 1.2 %collective-permute-start.8 = (bf16[48,2176]{1,0:T(8,128)(2,1)S(1)}, bf16[48,2176]{1,0:T(8,128)(2,1)S(1)}, u32[]{:S(2)}, u32[]{:S(2)}) collective-permute-start(bf16[48,2176]{1,0:T(8,128)(2,1)S(1)} %chip_sum_first.1.refs_9_.refs_0_), channel_id=1, source_target_pairs={{0,8},{4,12},{8,0},{12,4},{1,9},{5,13},{9,1},{13,5},{2,10},{6,14},... | collective-permute-start | bytes 626696 | tf_op jit(solution)/shard_map/ppermute | solution.py:483
  26.5 2.3 %project_next.2 = (bf16[48,1024]{1,0:T(8,128)(2,1)S(1)}, bf16[48,1024]{1,0:T(8,128)(2,1)S(1)}, bf16[2048,512]{1,0:T(8,128)(2,1)S(1)}, bf16[2048,512]{1,0:T(8,128)(2,1)S(1)}) custom-call(bf16[2048,4096]{1,0:T(8,128)(2,1)} %refs_0_.15, bf16[2048,4096]{1,0:T(8,128)(2,1)} %refs_1_.15, bf16[4096,2048]{1,0:T(8,128)(2,1)} %refs_2_.17, ...), custom_call_target="tpu_custom_call" | custom-call | flops 402653184 | bytes 8388608 | tf_op jit(solution)/shard_map/project_next/pallas_call | solution.py:33
  28.8 1.6 %project_next.3 = (bf16[48,1024]{1,0:T(8,128)(2,1)S(1)}, bf16[48,1024]{1,0:T(8,128)(2,1)S(1)}, bf16[512,2048]{1,0:T(8,128)(2,1)S(1)}) custom-call(bf16[2048,4096]{1,0:T(8,128)(2,1)} %refs_0_.15, bf16[2048,4096]{1,0:T(8,128)(2,1)} %refs_1_.15, bf16[4096,2048]{1,0:T(8,128)(2,1)} %refs_2_.17, bf16[48,2048]{1,0:T(8,128)(2,1)S(1)} %get-tuple-element.72.refs_3_, ...), custom_call_target="tpu_custom_call" | custom-call | flops 402653184 | bytes 8388608 | tf_op jit(solution)/shard_map/project_next/pallas_call | solution.py:33
  31.0 0.8 %collective-permute-done.7.refs_1_ = bf16[48,1024]{1,0:T(8,128)(2,1)S(1)} collective-permute-done((bf16[48,1024]{1,0:T(8,128)(2,1)S(1)}, bf16[48,1024]{1,0:T(8,128)(2,1)S(1)}, u32[]{:S(2)}, u32[]{:S(2)}) %collective-permute-start.7) | collective-permute-done | bytes 98336 | tf_op jit(solution)/shard_map/ppermute | solution.py:483
  31.8 1.0 %collective-permute-start.11 = (bf16[48,1024]{1,0:T(8,128)(2,1)S(1)}, bf16[48,1024]{1,0:T(8,128)(2,1)S(1)}, u32[]{:S(2)}, u32[]{:S(2)}) collective-permute-start(bf16[48,1024]{1,0:T(8,128)(2,1)S(1)} %chip_sum_next.2.refs_4_), channel_id=1, source_target_pairs={{0,8},{4,12},{8,0},{12,4},{1,9},{5,13},{9,1},{13,5},{2,10},{6,14},... | collective-permute-start | bytes 294920 | tf_op jit(solution)/shard_map/ppermute | solution.py:483
  32.8 1.2 %collective-permute-start.10 = (bf16[48,1024]{1,0:T(8,128)(2,1)S(1)}, bf16[48,1024]{1,0:T(8,128)(2,1)S(1)}, u32[]{:S(2)}, u32[]{:S(2)}) collective-permute-start(bf16[48,1024]{1,0:T(8,128)(2,1)S(1)} %chip_sum_next.3.refs_2_), channel_id=1, source_target_pairs={{0,8},{4,12},{8,0},{12,4},{1,9},{5,13},{9,1},{13,5},{2,10},{6,14},... | collective-permute-start | bytes 294920 | tf_op jit(solution)/shard_map/ppermute | solution.py:483
  34.0 4.8 %fetch_down.1 = (bf16[1,1,4,128,128]{4,3,2,1,0:T(8,128)(2,1)S(1)}, bf16[512,2048]{1,0:T(8,128)(2,1)S(1)}, bf16[512,2048]{1,0:T(8,128)(2,1)S(1)}, bf16[512,2048]{...) custom-call(bf16[2048,4096]{1,0:T(8,128)(2,1)} %refs_0_.15, ...), custom_call_target="tpu_custom_call" | custom-call | bytes 12582912 | tf_op jit(solution)/shard_map/fetch_down/pallas_call | solution.py:33
  39.1 1.6 %down_mine.1 = (f32[48,2048]{1,0:T(8,128)S(1)}, bf16[512,2048]{1,0:T(8,128)(2,1)S(1)}) custom-call(bf16[2048,4096]{1,0:T(8,128)(2,1)} %refs_0_.15, bf16[2048,4096]{1,0:T(8,128)(2,1)} %refs_1_.15, bf16[4096,2048]{1,0:T(8,128)(2,1)} %refs_2_.17, bf16[48,2048]{1,0:T(8,128)(2,1)S(1)} %hidden.1.refs_3_, bf16[512,2048]{1,0:T(8,128)(2,1)S(1)} %get-tuple-element.88.refs_4_, ...), custom_call_target="tpu_custom_call" | custom-call | flops 402653184 | bytes 8388608 | tf_op jit(solution)/shard_map/down_mine/pallas_call | solution.py:33
  40.8 1.9 %down.1 = (bf16[24,1024]{1,0:T(8,128)(2,1)S(1)}, bf16[24,1024]{1,0:T(8,128)(2,1)S(1)}, bf16[24,1024]{1,0:T(8,128)(2,1)S(1)}, bf16[24,1024]{1,0:T(8,128)(2,1)S(1)}, bf16[48,256]{1,0:T(8,128)(2,1)S(1)}) custom-call(s32[1,3,3,1,4]{4,3,2,1,0:T(1,128)} %bitcast.6, bf16[1,1,4,128,128]{4,3,2,1,0:T(8,128)(2,1)S(1)} %get-tuple-element.84.refs_1_, ...), custom_call_target="tpu_custom_call" | custom-call | bytes 1024 | tf_op jit(solution)/shard_map/down/pallas_call | solution.py:33
  42.7 3.1 %collective-permute-start.14 = (bf16[24,1024]{1,0:T(8,128)(2,1)S(1)}, bf16[24,1024]{1,0:T(8,128)(2,1)S(1)}, u32[]{:S(2)}, u32[]{:S(2)}) collective-permute-start(bf16[24,1024]{1,0:T(8,128)(2,1)S(1)} %get-tuple-element.98), channel_id=1, source_target_pairs={{0,3},{1,2},{2,1},{3,0},{4,7},{5,6},{6,5},{7,4},{8,11},{9,10},{10,... | collective-permute-start | bytes 147464 | tf_op jit(solution)/shard_map/ppermute | solution.py:483
  45.8 1.3 %collective-permute-start.16 = (bf16[24,1024]{1,0:T(8,128)(2,1)S(1)}, bf16[24,1024]{1,0:T(8,128)(2,1)S(1)}, u32[]{:S(2)}, u32[]{:S(2)}) collective-permute-start(bf16[24,1024]{1,0:T(8,128)(2,1)S(1)} %get-tuple-element.100), channel_id=1, source_target_pairs={{0,1},{1,0},{2,3},{3,2},{4,5},{5,4},{6,7},{7,6},{8,9},{9,8},{10,11... | collective-permute-start | bytes 147464 | tf_op jit(solution)/shard_map/ppermute | solution.py:483
  47.1 0.9 %collective-permute-start.13 = (bf16[48,256]{1,0:T(8,128)(2,1)S(1)}, bf16[48,256]{1,0:T(8,128)(2,1)S(1)}, u32[]{:S(2)}, u32[]{:S(2)}) collective-permute-start(bf16[48,256]{1,0:T(8,128)(2,1)S(1)} %get-tuple-element.97), channel_id=1, source_target_pairs={{0,8},{4,12},{8,0},{12,4},{1,9},{5,13},{9,1},{13,5},{2,10},{6,14},... | collective-permute-start | bytes 73736 | tf_op jit(solution)/shard_map/ppermute | solution.py:483
  48.0 2.9 %collective-permute-done.13.refs_2_ = bf16[48,256]{1,0:T(8,128)(2,1)S(1)} collective-permute-done((bf16[48,256]{1,0:T(8,128)(2,1)S(1)}, bf16[48,256]{1,0:T(8,128)(2,1)S(1)}, u32[]{:S(2)}, u32[]{:S(2)}) %collective-permute-start.13) | collective-permute-done | bytes 24608 | tf_op jit(solution)/shard_map/ppermute | solution.py:483
  51.0 0.9 %finish.1 = (bf16[3,8192]{1,0:T(4,128)(2,1)}, bf16[12,2048]{1,0:T(8,128)(2,1)}) custom-call(bf16[48,128]{1,0:T(8,128)(2,1)S(1)} %get-tuple-element.57.refs_0_, bf16[48,2432]{1,0:T(8,128)(2,1)S(1)} %collective-permute-done.6.refs_1_.refs_5_, bf16[48,256]{1,0:T(8,128)(2,1)S(1)} %collective-permute-done.13.refs_2_, ...), custom_call_target="tpu_custom_call" | custom-call | bytes 1024 | tf_op jit(solution)/shard_map/finish/pallas_call | solution.py:33
  (26 shorter events, 2.1 us)
Async XLA Ops:
  1.8 6.3 %collective-permute-start = (bf16[4,16,512]{2,1,0:T(8,128)(2,1)S(1)}, bf16[4,16,512]{2,1,0:T(8,128)(2,1)S(1)}, u32[]{:S(2)}, u32[]{:S(2)}) collective-permute-start(bf16[4,16,512]{2,1,0:T(8,128)(2,1)S(1)} %get-tuple-element.53), channel_id=1, source_target_pairs={{0,8},{4,12},{8,0},{12,4},{1,9},{5,13},{9,1},{13,5},{2,10},{6,14},... | collective-permute-start | bytes 196616 | tf_op jit(solution)/shard_map/ppermute | solution.py:483
  4.8 4.1 %collective-permute-start.1 = (bf16[4,16,512]{2,1,0:T(8,128)(2,1)S(1)}, bf16[4,16,512]{2,1,0:T(8,128)(2,1)S(1)}, u32[]{:S(2)}, u32[]{:S(2)}) collective-permute-start(bf16[4,16,512]{2,1,0:T(8,128)(2,1)S(1)} %get-tuple-element.54), channel_id=1, source_target_pairs={{0,12},{4,8},{8,4},{12,0},{1,13},{5,9},{9,5},{13,1},{2,14},{6,10},... | collective-permute-start | bytes 196616 | tf_op jit(solution)/shard_map/ppermute | solution.py:483
  4.8 4.1 %collective-permute-start.2 = (bf16[4,16,512]{2,1,0:T(8,128)(2,1)S(1)}, bf16[4,16,512]{2,1,0:T(8,128)(2,1)S(1)}, u32[]{:S(2)}, u32[]{:S(2)}) collective-permute-start(bf16[4,16,512]{2,1,0:T(8,128)(2,1)S(1)} %get-tuple-element.55), channel_id=1, source_target_pairs={{0,4},{4,0},{8,12},{12,8},{1,5},{5,1},{9,13},{13,9},{2,6},{6,2},{1... | collective-permute-start | bytes 196616 | tf_op jit(solution)/shard_map/ppermute | solution.py:483
  10.5 8.0 %collective-permute-start.5 = (bf16[24,1024]{1,0:T(8,128)(2,1)S(1)}, bf16[24,1024]{1,0:T(8,128)(2,1)S(1)}, u32[]{:S(2)}, u32[]{:S(2)}) collective-permute-start(bf16[24,1024]{1,0:T(8,128)(2,1)S(1)} %get-tuple-element.60.refs_3_.refs_4_), channel_id=1, source_target_pairs={{0,3},{1,2},{2,1},{3,0},{4,7},{5,6},{6,5},{7,4},{8,11},{9,10},{10,... | collective-permute-start | bytes 147464 | tf_op jit(solution)/shard_map/ppermute | solution.py:483
  14.3 5.0 %collective-permute-start.4 = (bf16[24,1024]{1,0:T(8,128)(2,1)S(1)}, bf16[24,1024]{1,0:T(8,128)(2,1)S(1)}, u32[]{:S(2)}, u32[]{:S(2)}) collective-permute-start(bf16[24,1024]{1,0:T(8,128)(2,1)S(1)} %get-tuple-element.60.refs_3_.refs_4_), channel_id=1, source_target_pairs={{0,2},{1,3},{2,0},{3,1},{4,6},{5,7},{6,4},{7,5},{8,10},{9,11},{10,... | collective-permute-start | bytes 147464 | tf_op jit(solution)/shard_map/ppermute | solution.py:483
  14.3 5.0 %collective-permute-start.3 = (bf16[24,1024]{1,0:T(8,128)(2,1)S(1)}, bf16[24,1024]{1,0:T(8,128)(2,1)S(1)}, u32[]{:S(2)}, u32[]{:S(2)}) collective-permute-start(bf16[24,1024]{1,0:T(8,128)(2,1)S(1)} %get-tuple-element.60.refs_3_.refs_4_), channel_id=1, source_target_pairs={{0,1},{1,0},{2,3},{3,2},{4,5},{5,4},{6,7},{7,6},{8,9},{9,8},{10,11... | collective-permute-start | bytes 147464 | tf_op jit(solution)/shard_map/ppermute | solution.py:483
  23.4 1.7 %collective-permute-start.6 = (bf16[48,2432]{1,0:T(8,128)(2,1)S(1)}, bf16[48,2432]{1,0:T(8,128)(2,1)S(1)}, u32[]{:S(2)}, u32[]{:S(2)}) collective-permute-start(bf16[48,2432]{1,0:T(8,128)(2,1)S(1)} %get-tuple-element.71.refs_3_), channel_id=1, source_target_pairs={{0,4},{4,0},{8,12},{12,8},{1,5},{5,1},{9,13},{13,9},{2,6},{6,2},{1... | collective-permute-start | bytes 700424 | tf_op jit(solution)/shard_map/ppermute | solution.py:483
  25.3 13.6 %collective-permute-start.8 = (bf16[48,2176]{1,0:T(8,128)(2,1)S(1)}, bf16[48,2176]{1,0:T(8,128)(2,1)S(1)}, u32[]{:S(2)}, u32[]{:S(2)}) collective-permute-start(bf16[48,2176]{1,0:T(8,128)(2,1)S(1)} %chip_sum_first.1.refs_9_.refs_0_), channel_id=1, source_target_pairs={{0,8},{4,12},{8,0},{12,4},{1,9},{5,13},{9,1},{13,5},{2,10},{6,14},... | collective-permute-start | bytes 626696 | tf_op jit(solution)/shard_map/ppermute | solution.py:483
  30.4 1.4 %collective-permute-start.7 = (bf16[48,1024]{1,0:T(8,128)(2,1)S(1)}, bf16[48,1024]{1,0:T(8,128)(2,1)S(1)}, u32[]{:S(2)}, u32[]{:S(2)}) collective-permute-start(bf16[48,1024]{1,0:T(8,128)(2,1)S(1)} %get-tuple-element.83), channel_id=1, source_target_pairs={{0,4},{4,0},{8,12},{12,8},{1,5},{5,1},{9,13},{13,9},{2,6},{6,2},{1... | collective-permute-start | bytes 294920 | tf_op jit(solution)/shard_map/ppermute | solution.py:483
  30.7 2.1 %collective-permute-start.9 = (bf16[48,1024]{1,0:T(8,128)(2,1)S(1)}, bf16[48,1024]{1,0:T(8,128)(2,1)S(1)}, u32[]{:S(2)}, u32[]{:S(2)}) collective-permute-start(bf16[48,1024]{1,0:T(8,128)(2,1)S(1)} %get-tuple-element.86), channel_id=1, source_target_pairs={{0,4},{4,0},{8,12},{12,8},{1,5},{5,1},{9,13},{13,9},{2,6},{6,2},{1... | collective-permute-start | bytes 294920 | tf_op jit(solution)/shard_map/ppermute | solution.py:483
  31.8 7.0 %collective-permute-start.11 = (bf16[48,1024]{1,0:T(8,128)(2,1)S(1)}, bf16[48,1024]{1,0:T(8,128)(2,1)S(1)}, u32[]{:S(2)}, u32[]{:S(2)}) collective-permute-start(bf16[48,1024]{1,0:T(8,128)(2,1)S(1)} %chip_sum_next.2.refs_4_), channel_id=1, source_target_pairs={{0,8},{4,12},{8,0},{12,4},{1,9},{5,13},{9,1},{13,5},{2,10},{6,14},... | collective-permute-start | bytes 294920 | tf_op jit(solution)/shard_map/ppermute | solution.py:483
  32.8 6.1 %collective-permute-start.10 = (bf16[48,1024]{1,0:T(8,128)(2,1)S(1)}, bf16[48,1024]{1,0:T(8,128)(2,1)S(1)}, u32[]{:S(2)}, u32[]{:S(2)}) collective-permute-start(bf16[48,1024]{1,0:T(8,128)(2,1)S(1)} %chip_sum_next.3.refs_2_), channel_id=1, source_target_pairs={{0,8},{4,12},{8,0},{12,4},{1,9},{5,13},{9,1},{13,5},{2,10},{6,14},... | collective-permute-start | bytes 294920 | tf_op jit(solution)/shard_map/ppermute | solution.py:483
  39.1 1.7 %collective-permute-start.12 = (bf16[48,2048]{1,0:T(8,128)(2,1)S(1)}, bf16[48,2048]{1,0:T(8,128)(2,1)S(1)}, u32[]{:S(2)}, u32[]{:S(2)}) collective-permute-start(bf16[48,2048]{1,0:T(8,128)(2,1)S(1)} %hidden.1.refs_3_), channel_id=1, source_target_pairs={{0,4},{4,0},{8,12},{12,8},{1,5},{5,1},{9,13},{13,9},{2,6},{6,2},{1... | collective-permute-start | bytes 589832 | tf_op jit(solution)/shard_map/ppermute | solution.py:483
  42.7 8.3 %collective-permute-start.14 = (bf16[24,1024]{1,0:T(8,128)(2,1)S(1)}, bf16[24,1024]{1,0:T(8,128)(2,1)S(1)}, u32[]{:S(2)}, u32[]{:S(2)}) collective-permute-start(bf16[24,1024]{1,0:T(8,128)(2,1)S(1)} %get-tuple-element.98), channel_id=1, source_target_pairs={{0,3},{1,2},{2,1},{3,0},{4,7},{5,6},{6,5},{7,4},{8,11},{9,10},{10,... | collective-permute-start | bytes 147464 | tf_op jit(solution)/shard_map/ppermute | solution.py:483
  45.8 5.2 %collective-permute-start.15 = (bf16[24,1024]{1,0:T(8,128)(2,1)S(1)}, bf16[24,1024]{1,0:T(8,128)(2,1)S(1)}, u32[]{:S(2)}, u32[]{:S(2)}) collective-permute-start(bf16[24,1024]{1,0:T(8,128)(2,1)S(1)} %get-tuple-element.99), channel_id=1, source_target_pairs={{0,2},{1,3},{2,0},{3,1},{4,6},{5,7},{6,4},{7,5},{8,10},{9,11},{10,... | collective-permute-start | bytes 147464 | tf_op jit(solution)/shard_map/ppermute | solution.py:483
  45.8 5.2 %collective-permute-start.16 = (bf16[24,1024]{1,0:T(8,128)(2,1)S(1)}, bf16[24,1024]{1,0:T(8,128)(2,1)S(1)}, u32[]{:S(2)}, u32[]{:S(2)}) collective-permute-start(bf16[24,1024]{1,0:T(8,128)(2,1)S(1)} %get-tuple-element.100), channel_id=1, source_target_pairs={{0,1},{1,0},{2,3},{3,2},{4,5},{5,4},{6,7},{7,6},{8,9},{9,8},{10,11... | collective-permute-start | bytes 147464 | tf_op jit(solution)/shard_map/ppermute | solution.py:483
  47.1 3.8 %collective-permute-start.13 = (bf16[48,256]{1,0:T(8,128)(2,1)S(1)}, bf16[48,256]{1,0:T(8,128)(2,1)S(1)}, u32[]{:S(2)}, u32[]{:S(2)}) collective-permute-start(bf16[48,256]{1,0:T(8,128)(2,1)S(1)} %get-tuple-element.97), channel_id=1, source_target_pairs={{0,8},{4,12},{8,0},{12,4},{1,9},{5,13},{9,1},{13,5},{2,10},{6,14},... | collective-permute-start | bytes 73736 | tf_op jit(solution)/shard_map/ppermute | solution.py:483

commit v5 on v4

--- a/solution.py
+++ b/solution.py
@@ -12,8 +12,7 @@
 HEAD_DIM = 128
 GROUP = HEADS // KV_HEADS
 MIB = 1 << 20
-FETCH = (0, 3, 1, 4, 5, 1, 2, 1, 6, 1)
-CUTS = (4, 6)
+FETCH = (3, 1, 4)
 BF16 = jnp.bfloat16
 F32 = jnp.float32
 VMEM = pltpu.VMEM
@@ -47,21 +46,10 @@
     def __init__(self, toks, cols, cap, units):
         self.toks, self.cols, self.cap = toks, cols, cap
         half = units // 2
-        cuts = [half * n // 8 for n in CUTS]
-        self.parts = list(zip([0] + cuts, [b - a for a, b in zip([0] + cuts, cuts + [half])]))
-        self.chunks = len(self.parts)
-        self.step = min(512, min(size for _, size in self.parts))
-        self.blocks_of = [
-            [
-                (q, keep, m, first + at)
-                for keep in (False, True)
-                for m in range(2)
-                for at in range(0, size, self.step)
-            ]
-            for q, (first, size) in enumerate(self.parts)
-        ]
-        self.downs = [(mine, n * half // 4) for mine in (True, False) for n in range(4)]
-        self.tail = 2 * self.parts[0][1]
+        self.ups = [(0, half // 2), (half // 2, half // 2)]
+        self.tail = half
+        self.step = min(512, half // 4)
+        self.jobs = [(keep, at) for keep in (False, True) for at in range(0, half, half // 4)]
         self.heads = HEADS // toks
         self.kvs = max(1, self.heads // GROUP)
         self.group = self.heads // self.kvs
@@ -75,9 +63,8 @@
         return tok * self.heads // GROUP
 
 
-def pack_kernel(z, ctx, jobs, req_ref, cache_ref, *rest):
-    weights, outs, rest = rest[:3], rest[3 : 3 + z.toks], rest[3 + z.toks :]
-    blocks, (narrow, wide, rows, req_sem, sems, block_sems) = rest[: len(jobs)], rest[len(jobs) :]
+def pack_kernel(z, ctx, req_ref, cache_ref, *rest):
+    outs, (narrow, wide, rows, req_sem, sems) = rest[: z.toks], rest[z.toks :]
     tok = lax.axis_index("tok")
     width = z.kvs * HEAD_DIM
     pairs = KV_HEADS * HEAD_DIM
@@ -94,7 +81,6 @@
             )
             copy.start()
             copies.append(copy)
-    copies += start_copies(list(zip(weight_blocks(z, jobs, weights), blocks)), block_sems)
     fetch.wait()
 
     @after_starts
@@ -134,41 +120,36 @@
     pl.when(lax.axis_index("tok") >= 0)(compute)
 
 
-def weight_blocks(z, jobs, refs):
+def weight_blocks(jobs, gate_ref):
     core = lax.axis_index("tok") % 2
-    half = refs[0].shape[1] // 2
+    half = gate_ref.shape[1] // 2
     found = []
-    for job in jobs:
-        at = pl.multiple_of((core if job[-3 if len(job) > 2 else 0] else 1 - core) * half, half)
-        if len(job) > 2:
-            _, _, matrix, first = job
-            found.append(refs[matrix].at[:, pl.ds(at + first, z.step)])
-        else:
-            found.append(refs[2].at[pl.ds(at + job[1], half // 4), :])
+    for keep, first in jobs:
+        at = pl.multiple_of((core if keep else 1 - core) * half, half)
+        found.append(gate_ref.at[:, pl.ds(at + first, half // 4)])
     return found
 
 
-def fetch_kernel(z, jobs, whole, gain_size, *refs):
-    weights, rest = refs[:3], refs[3:]
+def fetch_kernel(jobs, whole, gain_size, gate_ref, *rest):
     sources, rest = list(rest[: len(whole)]), rest[len(whole) :]
     outs, sems = rest[:-1], rest[-1]
     if gain_size:
         tok = lax.axis_index("tok")
         at = pl.multiple_of(tok * gain_size, gain_size)
         sources[0] = sources[0].at[:, pl.ds(at, gain_size)]
-    sources += weight_blocks(z, jobs, weights)
+    sources += weight_blocks(jobs, gate_ref)
     for copy in start_copies(list(zip(sources, outs)), sems):
         copy.wait()
 
 
 def attend_kernel(z, ctx, jobs, list_hbm, count_hbm, *rest):
-    weights, pieces, rest = rest[:3], rest[3 : 3 + z.toks], rest[3 + z.toks :]
+    gate_ref, pieces, rest = rest[0], rest[1 : 1 + z.toks], rest[1 + z.toks :]
     pieces = pieces[:1] + pieces[-1:] + pieces[1:-1]
     send_ref, back_refs, rest = rest[0], rest[1 : 1 + z.toks], rest[1 + z.toks :]
     blocks, rest = rest[: len(jobs)], rest[len(jobs) :]
     cache, req, query, own_key, own_value, alive, mixed_all, list_ref, count_ref, table_sems, sems = rest
     tables = start_copies([(list_hbm, list_ref), (count_hbm, count_ref)], table_sems)
-    copies = start_copies(list(zip(weight_blocks(z, jobs, weights), blocks)), sems)
+    copies = start_copies(list(zip(weight_blocks(jobs, gate_ref), blocks)), sems)
 
     @after_starts
     def _():
@@ -271,54 +252,47 @@
         )
 
 
-def project_steps(z, chunk, source, extra, blocks, send_ref, keep_ref):
-    core = lax.axis_index("tok") % 2
-    units = extra.shape[1] // 2
-    first, size = z.parts[chunk]
-    steps = []
-    for n, (out_ref, side) in enumerate(((send_ref, 1 - core), (keep_ref, core))):
-        for m in range(2):
-            for p in range(size // z.step):
-                block = blocks[(2 * n + m) * (size // z.step) + p]
-                at = side * (units // 2) + m * units + first + p * z.step
-                to = m * size + p * z.step
-
-                def step(block=block, at=pl.multiple_of(at, HEAD_DIM), to=to, out_ref=out_ref):
-                    value = jnp.dot(source[...], block[...], preferred_element_type=F32)
-                    value += extra[:, pl.ds(at, z.step)]
-                    out_ref[:, to : to + z.step] = value.astype(BF16)
-
-                steps.append(step)
-    return steps
-
-
-def first_project_kernel(z, jobs, index_hbm, gain_ref, gate_delta, up_delta, *rest):
+def first_project_kernel(z, index_hbm, gain_ref, delta_ref, *rest):
     pieces, rest = rest[: z.cols], rest[z.cols :]
     odd_backs, rest = rest[: z.toks // 2], rest[z.toks // 2 :]
-    count = len(z.blocks_of[0])
-    weights, blocks, rest = rest[:3], rest[3 : 3 + count], rest[3 + count :]
-    send_ref, keep_ref, source, extra, *fetched = rest[: 4 + len(jobs)]
-    index_ref, index_sem, sems = rest[4 + len(jobs) :]
+    blocks, rest = rest[: len(z.jobs)], rest[len(z.jobs) :]
+    send_ref, keep_ref, source, extra, index_ref, index_sem = rest
     table = pltpu.make_async_copy(index_hbm, index_ref, index_sem)
     table.start()
-    copies = start_copies(list(zip(weight_blocks(z, jobs, weights), fetched)), sems)
-    units = extra.shape[1] // 2
 
     @after_starts
     def _():
         gather_rows(z, pieces, gain_ref, odd_backs, source, extra, send_ref, keep_ref)
 
     table.wait()
-
-    @after_starts
-    def _():
-        tile_terms(z, source, gate_delta, index_ref, 0, extra, 0)
-        tile_terms(z, source, up_delta, index_ref, 1, extra, units)
-        for step in project_steps(z, 0, source, extra, blocks, send_ref, keep_ref):
-            step()
-
-    for copy in copies:
-        copy.wait()
+    tile_terms(z, source, delta_ref, index_ref, 0, extra, 0)
+    core = lax.axis_index("tok") % 2
+    half = z.tail
+    for (keep, first), block in zip(z.jobs, blocks):
+        out_ref, side = (keep_ref, core) if keep else (send_ref, 1 - core)
+        for p in range(0, half // 4, z.step):
+            at = pl.multiple_of(side * half + first + p, HEAD_DIM)
+            value = jnp.dot(source[...], block[:, p : p + z.step], preferred_element_type=F32)
+            value += extra[:, pl.ds(at, z.step)]
+            out_ref[:, first + p : first + p + z.step] = value.astype(BF16)
+
+
+def up_kernel(z, part, source, extra, up_ref, send_ref, keep_ref):
+    core = lax.axis_index("tok") % 2
+    first, size = part
+    for out_ref, side in ((send_ref, 1 - core), (keep_ref, core)):
+        for p in range(0, size, z.step):
+            lanes = pl.ds(pl.multiple_of(side * z.tail + first + p, HEAD_DIM), z.step)
+            value = jnp.dot(source[...], up_ref[:, lanes], preferred_element_type=F32)
+            out_ref[:, p : p + z.step] = (value + extra[:, lanes]).astype(BF16)
+
+
+def up_tiles_kernel(z, index_hbm, delta_ref, source, extra, index_ref, index_sem):
+    table = pltpu.make_async_copy(index_hbm, index_ref, index_sem)
+    table.start()
+    extra[...] = jnp.zeros_like(extra)
+    table.wait()
+    tile_terms(z, source, delta_ref, index_ref, 1, extra, 0)
 
 
 def gather_rows(z, pieces, gain_ref, odd_backs, source, extra, send_ref, keep_ref):
@@ -348,21 +322,6 @@
         send_ref[: ref.shape[0], lane : lane + HEAD_DIM] = ref[...]
 
 
-def next_project_kernel(z, q, jobs, *rest):
-    weights, (source, extra), rest = rest[:3], rest[3:5], rest[5:]
-    blocks, rest = rest[: len(z.blocks_of[q])], rest[len(z.blocks_of[q]) :]
-    send_ref, keep_ref, *fetched, sems = rest
-    copies = start_copies(list(zip(weight_blocks(z, jobs, weights), fetched)), sems)
-
-    @after_starts
-    def _():
-        for step in project_steps(z, q, source, extra, blocks, send_ref, keep_ref):
-            step()
-
-    for copy in copies:
-        copy.wait()
-
-
 def add_kernel(z, mine, other, out_ref):
     size = mine.shape[1] // (2 * HEAD_DIM) * (2 * HEAD_DIM)
     out_ref[:, :size] = (mine[:, :size].astype(F32) + other[:, :size].astype(F32)).astype(BF16)
@@ -374,46 +333,41 @@
 
 def hidden_kernel(z, width, *refs):
     chips = z.toks // 2
-    out_ref = refs[-1]
-    squares = sum(ref[:, z.tail : z.tail + HEAD_DIM].astype(F32) for ref in refs[:chips])
+    gates, out_ref = refs[:chips], refs[-1]
+    squares = sum(ref[:, z.tail : z.tail + HEAD_DIM].astype(F32) for ref in gates)
     squares = jnp.sum(squares, axis=-1, keepdims=True)
     scale = lax.rsqrt(squares * (1.0 / width) + 1e-06)
-    for q, (first, size) in enumerate(z.parts):
-        parts = refs[q * chips : (q + 1) * chips]
+    for q, (first, size) in enumerate(z.ups):
+        ups = refs[(q + 1) * chips : (q + 2) * chips]
         step = min(size, 256)
         for at in range(0, size, step):
-            gate = sum(ref[:, at : at + step].astype(F32) for ref in parts) * scale
-            up = sum(ref[:, size + at : size + at + step].astype(F32) for ref in parts) * scale
-            out_ref[:, first + at : first + at + step] = (jax.nn.silu(gate) * up).astype(BF16)
-
-
-def down_products(z, mine, units_ref, weights, total, before=None):
-    width = total.shape[1]
-    places = [at for is_mine, at in z.downs if is_mine == mine]
+            lanes = slice(first + at, first + at + step)
+            gate = sum(ref[:, lanes].astype(F32) for ref in gates) * scale
+            up = sum(ref[:, at : at + step].astype(F32) for ref in ups) * scale
+            out_ref[:, lanes] = (jax.nn.silu(gate) * up).astype(BF16)
+
+
+def down_products(mine, units_ref, weight_ref, total, before=None):
+    core = lax.axis_index("tok") % 2
+    half, width = units_ref.shape[1], total.shape[1]
+    at = pl.multiple_of((core if mine else 1 - core) * half, half)
     step = min(width, 512)
     for to in range(0, width, step):
         lanes = slice(to, to + step)
-        value = jnp.zeros((z.rows, step), F32) if before is None else before[:, lanes]
-        for at, weight in zip(places, weights):
-            units = units_ref[:, at : at + weight.shape[0]]
-            value += jnp.dot(units, weight[:, lanes], preferred_element_type=F32)
-        total[:, lanes] = value
-
-
-def down_mine_kernel(z, jobs, *rest):
-    weights, mine, rest = rest[:3], rest[3], rest[4:]
-    blocks, rest = rest[: len(z.downs) // 2], rest[len(z.downs) // 2 :]
-    total, *fetched, sems = rest
-    copies = start_copies(list(zip(weight_blocks(z, jobs, weights), fetched)), sems)
-    after_starts(lambda: down_products(z, True, mine, blocks, total))
-    for copy in copies:
-        copy.wait()
+        value = jnp.dot(
+            units_ref[...], weight_ref[pl.ds(at, half), lanes], preferred_element_type=F32
+        )
+        total[:, lanes] = value if before is None else value + before[:, lanes]
+
+
+def down_mine_kernel(mine, weight, total):
+    down_products(True, mine, weight, total)
 
 
 def down_kernel(z, index_hbm, delta_ref, before, mine, other, from_core, *rest):
     others = z.toks // 2 - 1
     evens, rest = rest[:others], rest[others:]
-    weights, rest = rest[: len(z.downs) // 2], rest[len(z.downs) // 2 :]
+    weight, rest = rest[0], rest[1:]
     outs, backs, rest = rest[: z.cols], rest[z.cols : z.cols + others], rest[z.cols + others :]
     source, total, fold, index_ref, index_sem = rest
     table = pltpu.make_async_copy(index_hbm, index_ref, index_sem)
@@ -425,7 +379,7 @@
         half = mine.shape[1]
         source[:, pl.ds(pl.multiple_of(core * half, half), half)] = mine[...]
         source[:, pl.ds(pl.multiple_of((1 - core) * half, half), half)] = other[...]
-        down_products(z, False, other, weights, total, before)
+        down_products(False, other, weight, total, before)
 
     for s, back in enumerate(backs):
         back[:, :HEAD_DIM] = evens[s][...]
@@ -513,56 +467,55 @@
     tile_index = tile_index.transpose(0, 2, 4, 1, 3)
     dma = pltpu.SemaphoreType.DMA
 
-    jobs = [job for some in z.blocks_of for job in some]
-    used = len(jobs)
-    jobs += z.downs
     cuts = [0]
     for count in FETCH:
         cuts.append(cuts[-1] + count)
-    first, early, middle, late, beside, between, *lasts, final, ending = [jobs[a:b] for a, b in zip(cuts, cuts[1:])]
-    weights = [(gate_weight, HBM), (up_weight, HBM), (down_weight, HBM)]
+    early, middle, late = [z.jobs[a:b] for a, b in zip(cuts, cuts[1:])]
 
     def shapes(some):
-        up, down = (features, z.step), (units // 8, down_weight.shape[1])
-        return [(up if len(job) > 2 else down, BF16) for job in some]
+        return [((features, units // 8), BF16) for _ in some]
 
     def traffic(some):
         moved = sum(a * b * 2 for (a, b), _ in shapes(some))
         return pl.CostEstimate(flops=0, bytes_accessed=moved, transcendentals=0)
 
+    def product(share):
+        return pl.CostEstimate(
+            flops=int(2 * z.rows * features * units * share),
+            bytes_accessed=int(2 * features * units * share),
+            transcendentals=0,
+        )
+
     pieces = call(
-        functools.partial(pack_kernel, z, ctx, first),
+        functools.partial(pack_kernel, z, ctx),
         "pack",
-        [(request_rows, HBM), (key_cache, HBM)] + weights,
-        [(piece_shape, BF16)] * toks + shapes(first),
+        [(request_rows, HBM), (key_cache, HBM)],
+        [(piece_shape, BF16)] * toks,
         [
             pltpu.VMEM(request_rows.shape, BF16),
             pltpu.VMEM(request_rows.shape, F32),
             pltpu.VMEM((toks, 2 * z.req_rows, HEAD_DIM), F32),
             dma,
             dma((toks, 2)),
-            dma((max(1, len(first)),)),
         ],
     )
-    pieces, blocks = pieces[:toks], pieces[toks:]
     whole = [gain, gate_delta, up_delta]
-    gain, gate_delta, up_delta, *fetched = call(
-        functools.partial(fetch_kernel, z, early, whole, features),
+    gain, gate_delta, up_delta, *blocks = call(
+        functools.partial(fetch_kernel, early, whole, features),
         "fetch_early",
-        weights + [(a, HBM) for a in whole],
+        [(a, HBM) for a in [gate_weight] + whole],
         [((1, features), F32), (gate_delta.shape, BF16), (up_delta.shape, BF16)]
         + shapes(early),
         [dma((len(early) + 3,))],
         after=pieces[:1],
         cost=traffic(early),
     )
-    blocks += fetched
     pieces = [pieces[0]] + [swap(pieces[s], "tok", toks, s) for s in range(1, toks)]
     back_rows = z.kvs * cap * z.group
     send, *rest = call(
         functools.partial(attend_kernel, z, ctx, middle),
         "attend",
-        [(route_list, HBM), (route_count, HBM)] + weights + [(p, VMEM) for p in pieces[:1] + pieces[2:] + pieces[1:2]],
+        [(a, HBM) for a in [route_list, route_count, gate_weight]] + [(p, VMEM) for p in pieces[:1] + pieces[2:] + pieces[1:2]],
         [((z.kvs * z.lane_slots, z.group * HEAD_DIM), BF16)]
         + [((back_rows, HEAD_DIM), BF16)] * toks
         + shapes(middle),
@@ -584,9 +537,9 @@
     back = rest[:toks]
     blocks += rest[toks:]
     blocks += call(
-        functools.partial(fetch_kernel, z, late, [], 0),
+        functools.partial(fetch_kernel, late, [], 0),
         "fetch_late",
-        weights,
+        [(gate_weight, HBM)],
         shapes(late),
         [dma((len(late),))],
         after=[send],
@@ -595,73 +548,52 @@
     pieces = [send] + [swap(send, "col", cols, s) for s in range(1, cols)]
     out_width = down_weight.shape[1]
     table = pltpu.SMEM(tile_index.shape, jnp.int32)
-    sent, kept, source, extra, *fetched = call(
-        functools.partial(first_project_kernel, z, beside),
-        "project_first",
-        [
-            (tile_index, HBM),
-            (gain, VMEM),
-            (gate_delta, VMEM),
-            (up_delta, VMEM),
-        ]
-        + [(p, VMEM) for p in pieces + back[1::2]]
-        + weights
-        + [(p, VMEM) for p in blocks[: len(z.blocks_of[0])]],
+    sent, kept, source = call(
+        functools.partial(first_project_kernel, z),
+        "gate",
+        [(tile_index, HBM), (gain, VMEM), (gate_delta, VMEM)]
+        + [(p, VMEM) for p in pieces + back[1::2] + blocks],
         [
             ((z.rows, z.tail + (1 + chips) * HEAD_DIM), BF16),
             ((z.rows, z.tail + HEAD_DIM), BF16),
             ((z.rows, features), BF16),
-            ((z.rows, 2 * units), F32),
-        ]
-        + shapes(beside),
-        [table, dma, dma((len(beside),))],
-        after=blocks[-1:],
-    )
-    blocks = blocks[len(z.blocks_of[0]) :] + fetched
-    fetched = call(
-        functools.partial(fetch_kernel, z, between, [], 0),
-        "fetch_between",
-        weights,
-        shapes(between),
-        [dma((len(between),))],
-        cost=traffic(between),
-        after=[sent],
-    )
-    blocks += fetched
+        ],
+        [pltpu.VMEM((z.rows, units), F32), table, dma],
+        cost=product(1),
+    )
     from_core = swap(sent, "tok", toks, 1)
+    (extra,) = call(
+        functools.partial(up_tiles_kernel, z),
+        "up_tiles",
+        [(tile_index, HBM), (up_delta, VMEM), (source, VMEM)],
+        [((z.rows, units), F32)],
+        [table, dma],
+        cost=product(1 / 8),
+    )
     totals = [
         call(
             functools.partial(add_kernel, z),
             "chip_sum_first",
             [(kept, VMEM), (from_core, VMEM)],
             [((z.rows, z.tail + HEAD_DIM), BF16)],
-            after=fetched[-1:],
+            after=[extra],
         )
     ]
-    for q, jobs in enumerate(lasts, 1):
-        size = 2 * z.parts[q][1]
-        place = sum(len(some) for some in z.blocks_of[1:q])
-        sent, kept, *fetched = call(
-            functools.partial(next_project_kernel, z, q, jobs),
-            "project_next",
-            weights
-            + [(a, VMEM) for a in [source, extra] + blocks[place : place + len(z.blocks_of[q])]],
-            [((z.rows, size), BF16)] * 2 + shapes(jobs),
-            [dma((len(jobs),))],
-            cost=pl.CostEstimate(
-                flops=4 * z.rows * features * size,
-                bytes_accessed=4 * features * size,
-                transcendentals=0,
-            ),
+    for part in z.ups:
+        size = part[1]
+        sent, kept = call(
+            functools.partial(up_kernel, z, part),
+            "up",
+            [(a, VMEM) for a in [source, extra, up_weight]],
+            [((z.rows, size), BF16)] * 2,
+            cost=product(size / units * 2),
             after=totals[0],
         )
-        blocks += fetched
-        other = swap(sent, "tok", toks, 1)
         totals.append(
             call(
                 functools.partial(add_kernel, z),
                 "chip_sum_next",
-                [(kept, VMEM), (other, VMEM)],
+                [(kept, VMEM), (swap(sent, "tok", toks, 1), VMEM)],
                 [((z.rows, size), BF16)],
             )
         )
@@ -669,42 +601,27 @@
         total + [swap(total[0], "tok", toks, 2 * s) for s in range(1, chips)]
         for total in totals
     ]
-    down_delta, *fetched = call(
-        functools.partial(fetch_kernel, z, final, [down_delta], 0),
-        "fetch_down",
-        weights + [(down_delta, HBM)],
-        [(down_delta.shape, BF16)] + shapes(final),
-        [dma((len(final) + 1,))],
-        cost=traffic(final),
-        after=totals[-1],
-    )
-    blocks += fetched
-    down_blocks = blocks[used - len(z.blocks_of[0]) :]
     (hidden,) = call(
         functools.partial(hidden_kernel, z, width),
         "hidden",
         [(a, VMEM) for part in parts for a in part],
         [((z.rows, units // 2), BF16)],
-        after=fetched[-1:],
-    )
-    half = len(z.downs) // 2
-    before, *fetched = call(
-        functools.partial(down_mine_kernel, z, ending),
+    )
+    (before,) = call(
+        down_mine_kernel,
         "down_mine",
-        weights + [(a, VMEM) for a in [hidden] + down_blocks[:half]],
-        [((z.rows, out_width), F32)] + shapes(ending),
-        [dma((max(1, len(ending)),))],
+        [(hidden, VMEM), (down_weight, VMEM)],
+        [((z.rows, out_width), F32)],
         cost=pl.CostEstimate(
             flops=z.rows * units * out_width, bytes_accessed=units * out_width, transcendentals=0
         ),
     )
-    down_blocks += fetched
     parts = call(
         functools.partial(down_kernel, z),
         "down",
         [(tile_index, HBM)]
         + [(a, VMEM) for a in [down_delta, before, hidden, swap(hidden, "tok", toks, 1), from_core]]
-        + [(a, VMEM) for a in back[2::2] + down_blocks[half:]],
+        + [(a, VMEM) for a in back[2::2] + [down_weight]],
         [((2 * z.lane_slots, out_width // 2), BF16)] * cols
         + [((back_rows, 2 * HEAD_DIM), BF16)] * (chips - 1),
         [

time: 52.1 us -> 50.3 us (0.965)
  Pallas kernels: 28.6 us -> 22.4 us
  waiting for transfers between devices: 5.32 us -> 9.65 us
    pallas_call x16 -> x15, Pallas kernels: 28.6 us -> 22.4 us  [call(): pl.pallas_call(body, name=name, in_specs=[pl.BlockSpec(memory_space=s) fo...]
    ppermute x17, waiting for transfers between devices: 5.32 us -> 9.65 us  [swap(): return lax.ppermute(array, axis, [(i, i ^ distance) for i in range(size)])]
  transfers between devices with their start and end apart: 17 -> 17, of which waited for: 5 -> 7; matrix products, arithmetic and copies ran while one was open for 0% -> 0% of each run, Pallas kernels for 36% -> 25%
where the time goes in v5:
time: 50.3 us; the launch traced here: 50 us
  Pallas kernels  22.4 us (45%)
  starting transfers between devices  17.1 us (34%)
  waiting for transfers between devices  9.65 us (19%)
  between operations  0.88 us (2%)
    pallas_call x15, Pallas kernels, call(): pl.pallas_call(body, name=name, in_specs=[pl.BlockSpec(memory_space=s) fo...  22.4 us
    ppermute x17, starting transfers between devices, swap(): return lax.ppermute(array, axis, [(i, i ^ distance) for i in range(size)])  17.1 us
    ppermute x17, waiting for transfers between devices, swap(): return lax.ppermute(array, axis, [(i, i ^ distance) for i in range(size)])  9.65 us
  transfers between devices with their start and end apart: 17, of which 7 were waited for; matrix products, arithmetic and copies ran while one was open for 0% of the time, Pallas kernels for 25%

profile of v5, /device:TPU:0, one launch (start us, length us, event | category | flops | bytes accessed | tf_op | source)
XLA Modules:
  0.0 50.0 jit_solution(4257008677184310444)
XLA Ops:
  0.6 1.1 %pack.1 = (bf16[4,16,512]{2,1,0:T(8,128)(2,1)S(1)}, bf16[4,16,512]{2,1,0:T(8,128)(2,1)S(1)}, bf16[4,16,512]{2,1,0:T(8,128)(2,1)S(1)}, bf16[4,16,512]{2,1,0:T(8,128)(2,1)S(1)}) custom-call(bf16[2,10240]{1,0:T(2,128)(2,1)} %refs_0_.3, bf16[3,16,2048]{2,1,0:T(8,128)(2,1)} %refs_1_.3), custom_call_target="tpu_custom_call" | custom-call | bytes 1024 | tf_op jit(solution)/shard_map/pack/pallas_call | solution.py:32
  1.8 3.0 %collective-permute-start = (bf16[4,16,512]{2,1,0:T(8,128)(2,1)S(1)}, bf16[4,16,512]{2,1,0:T(8,128)(2,1)S(1)}, u32[]{:S(2)}, u32[]{:S(2)}) collective-permute-start(bf16[4,16,512]{2,1,0:T(8,128)(2,1)S(1)} %get-tuple-element.35), channel_id=1, source_target_pairs={{0,8},{4,12},{8,0},{12,4},{1,9},{5,13},{9,1},{13,5},{2,10},{6,14},... | collective-permute-start | bytes 196616 | tf_op jit(solution)/shard_map/ppermute | solution.py:437
  5.0 3.1 %fetch_early.1 = (f32[1,2048]{1,0:T(1,128)S(1)}, bf16[1,1,4,128,128]{4,3,2,1,0:T(8,128)(2,1)S(1)}, bf16[1,1,4,128,128]{4,3,2,1,0:T(8,128)(2,1)S(1)}, bf16[2048,5...) custom-call(bf16[2048,4096]{1,0:T(8,128)(2,1)} %refs_0_.5, f32[1,8192]{1,0:T(1,128)} %bitcast.11, ...), custom_call_target="tpu_custom_call" | custom-call | bytes 6291456 | tf_op jit(solution)/shard_map/fetch_early/pallas_call | solution.py:32
  8.1 0.8 %collective-permute-done.1.refs_5_ = bf16[4,16,512]{2,1,0:T(8,128)(2,1)S(1)} collective-permute-done((bf16[4,16,512]{2,1,0:T(8,128)(2,1)S(1)}, bf16[4,16,512]{2,1,0:T(8,128)(2,1)S(1)}, u32[]{:S(2)}, u32[]{:S(2)}) %collective-permute-start.1) | collective-permute-done | bytes 65568 | tf_op jit(solution)/shard_map/ppermute | solution.py:437
  8.9 1.6 %attend.1 = (bf16[24,1024]{1,0:T(8,128)(2,1)S(1)}, bf16[48,128]{1,0:T(8,128)(2,1)S(1)}, bf16[48,128]{1,0:T(8,128)(2,1)S(1)}, bf16[48,128]{1,0:T(8,128)(2,1)S(1)}...) custom-call(s32[3,1,4]{2,1,0:T(1,128)} %bitcast.12, s32[1,4]{1,0:T(1,128)} %bitcast.13, ...), custom_call_target="tpu_custom_call" | custom-call | bytes 1024 | tf_op jit(solution)/shard_map/attend/pallas_call | solution.py:32
  10.5 3.7 %collective-permute-start.5 = (bf16[24,1024]{1,0:T(8,128)(2,1)S(1)}, bf16[24,1024]{1,0:T(8,128)(2,1)S(1)}, u32[]{:S(2)}, u32[]{:S(2)}) collective-permute-start(bf16[24,1024]{1,0:T(8,128)(2,1)S(1)} %get-tuple-element.41.refs_1_.refs_3_), channel_id=1, source_target_pairs={{0,3},{1,2},{2,1},{3,0},{4,7},{5,6},{6,5},{7,4},{8,11},{9,10},{10,... | collective-permute-start | bytes 147464 | tf_op jit(solution)/shard_map/ppermute | solution.py:437
  14.2 0.7 %collective-permute-start.3 = (bf16[24,1024]{1,0:T(8,128)(2,1)S(1)}, bf16[24,1024]{1,0:T(8,128)(2,1)S(1)}, u32[]{:S(2)}, u32[]{:S(2)}) collective-permute-start(bf16[24,1024]{1,0:T(8,128)(2,1)S(1)} %get-tuple-element.41.refs_1_.refs_3_), channel_id=1, source_target_pairs={{0,1},{1,0},{2,3},{3,2},{4,5},{5,4},{6,7},{7,6},{8,9},{9,8},{10,11... | collective-permute-start | bytes 147464 | tf_op jit(solution)/shard_map/ppermute | solution.py:437
  15.0 3.7 %fetch_late.1 = (bf16[2048,512]{1,0:T(8,128)(2,1)S(1)}, bf16[2048,512]{1,0:T(8,128)(2,1)S(1)}, bf16[2048,512]{1,0:T(8,128)(2,1)S(1)}, bf16[2048,512]{1,0:T(8,128)(2,1)S(1)}) custom-call(bf16[2048,4096]{1,0:T(8,128)(2,1)} %refs_0_.5, bf16[24,1024]{1,0:T(8,128)(2,1)S(1)} %get-tuple-element.41.refs_1_.refs_3_), custom_call_target="tpu_custom_call" | custom-call | bytes 8388608 | tf_op jit(solution)/shard_map/fetch_late/pallas_call | solution.py:32
  19.2 4.0 %gate.1 = (bf16[48,2432]{1,0:T(8,128)(2,1)S(1)}, bf16[48,2176]{1,0:T(8,128)(2,1)S(1)}, bf16[48,2048]{1,0:T(8,128)(2,1)S(1)}) custom-call(s32[1,3,3,1,4]{4,3,2,1,0:T(1,128)} %bitcast.8, f32[1,2048]{1,0:T(1,128)S(1)} %get-tuple-element.38.refs_7_.refs_1_, bf16[1,1,4,128,128]{4,3,2,1,0:T(8,128)(2,1)S(1)} %get-tuple-element.40.refs_2_, ...), custom_call_target="tpu_custom_call" | custom-call | flops 805306368 | bytes 16777216 | tf_op jit(solution)/shard_map/gate/pallas_call | solution.py:32
  23.3 0.9 %up_tiles.1.refs_2_.refs_1_ = f32[48,4096]{1,0:T(8,128)S(1)} custom-call(s32[1,3,3,1,4]{4,3,2,1,0:T(1,128)} %bitcast.9, bf16[1,1,4,128,128]{4,3,2,1,0:T(8,128)(2,1)S(1)} %get-tuple-element.54.refs_1_, bf16[48,2048]{1,0:T(8,128)(2,1)S(1)} %get-tuple-element.55.refs_2_.refs_0_), custom_call_target="tpu_custom_call" | custom-call | flops 100663296 | bytes 2097152 | tf_op jit(solution)/shard_map/up_tiles/pallas_call | solution.py:32
  25.0 1.2 %collective-permute-start.7 = (bf16[48,2176]{1,0:T(8,128)(2,1)S(1)}, bf16[48,2176]{1,0:T(8,128)(2,1)S(1)}, u32[]{:S(2)}, u32[]{:S(2)}) collective-permute-start(bf16[48,2176]{1,0:T(8,128)(2,1)S(1)} %chip_sum_first.1.refs_3_.refs_0_), channel_id=1, source_target_pairs={{0,8},{4,12},{8,0},{12,4},{1,9},{5,13},{9,1},{13,5},{2,10},{6,14},... | collective-permute-start | bytes 626696 | tf_op jit(solution)/shard_map/ppermute | solution.py:437
  26.2 1.6 %up.3 = (bf16[48,1024]{1,0:T(8,128)(2,1)S(1)}, bf16[48,1024]{1,0:T(8,128)(2,1)S(1)}) custom-call(bf16[48,2048]{1,0:T(8,128)(2,1)S(1)} %get-tuple-element.55.refs_2_.refs_0_, f32[48,4096]{1,0:T(8,128)S(1)} %up_tiles.1.refs_2_.refs_1_, bf16[2048,4096]{1,0:T(8,128)(2,1)S(1)} %bitcast.5, bf16[48,2176]{1,0:T(8,128)(2,1)S(1)} %chip_sum_first.1.refs_3_.refs_0_), custom_call_target="tpu_custom_call" | custom-call | flops 402653184 | bytes 8388608 | tf_op jit(solution)/shard_map/up/pallas_call | solution.py:32
  27.9 1.6 %up.2 = (bf16[48,1024]{1,0:T(8,128)(2,1)S(1)}, bf16[48,1024]{1,0:T(8,128)(2,1)S(1)}) custom-call(bf16[48,2048]{1,0:T(8,128)(2,1)S(1)} %get-tuple-element.55.refs_2_.refs_0_, f32[48,4096]{1,0:T(8,128)S(1)} %up_tiles.1.refs_2_.refs_1_, bf16[2048,4096]{1,0:T(8,128)(2,1)S(1)} %bitcast.5, bf16[48,2176]{1,0:T(8,128)(2,1)S(1)} %chip_sum_first.1.refs_3_.refs_0_), custom_call_target="tpu_custom_call" | custom-call | flops 402653184 | bytes 8388608 | tf_op jit(solution)/shard_map/up/pallas_call | solution.py:32
  30.1 1.0 %collective-permute-start.11 = (bf16[48,1024]{1,0:T(8,128)(2,1)S(1)}, bf16[48,1024]{1,0:T(8,128)(2,1)S(1)}, u32[]{:S(2)}, u32[]{:S(2)}) collective-permute-start(bf16[48,1024]{1,0:T(8,128)(2,1)S(1)} %chip_sum_next.3.refs_4_), channel_id=1, source_target_pairs={{0,8},{4,12},{8,0},{12,4},{1,9},{5,13},{9,1},{13,5},{2,10},{6,14},... | collective-permute-start | bytes 294920 | tf_op jit(solution)/shard_map/ppermute | solution.py:437
  31.1 1.2 %collective-permute-start.9 = (bf16[48,1024]{1,0:T(8,128)(2,1)S(1)}, bf16[48,1024]{1,0:T(8,128)(2,1)S(1)}, u32[]{:S(2)}, u32[]{:S(2)}) collective-permute-start(bf16[48,1024]{1,0:T(8,128)(2,1)S(1)} %chip_sum_next.2.refs_2_), channel_id=1, source_target_pairs={{0,8},{4,12},{8,0},{12,4},{1,9},{5,13},{9,1},{13,5},{2,10},{6,14},... | collective-permute-start | bytes 294920 | tf_op jit(solution)/shard_map/ppermute | solution.py:437
  32.3 3.4 %collective-permute-done.11.refs_5_ = bf16[48,1024]{1,0:T(8,128)(2,1)S(1)} collective-permute-done((bf16[48,1024]{1,0:T(8,128)(2,1)S(1)}, bf16[48,1024]{1,0:T(8,128)(2,1)S(1)}, u32[]{:S(2)}, u32[]{:S(2)}) %collective-permute-start.11) | collective-permute-done | bytes 98336 | tf_op jit(solution)/shard_map/ppermute | solution.py:437
  35.7 1.3 %collective-permute-done.9.refs_3_ = bf16[48,1024]{1,0:T(8,128)(2,1)S(1)} collective-permute-done((bf16[48,1024]{1,0:T(8,128)(2,1)S(1)}, bf16[48,1024]{1,0:T(8,128)(2,1)S(1)}, u32[]{:S(2)}, u32[]{:S(2)}) %collective-permute-start.9) | collective-permute-done | bytes 98336 | tf_op jit(solution)/shard_map/ppermute | solution.py:437
  37.3 1.6 %down_mine.1.refs_2_ = f32[48,2048]{1,0:T(8,128)S(1)} custom-call(bf16[48,2048]{1,0:T(8,128)(2,1)S(1)} %hidden.1.refs_0_.refs_3_, bf16[4096,2048]{1,0:T(8,128)(2,1)S(1)} %bitcast.7), custom_call_target="tpu_custom_call" | custom-call | flops 402653184 | bytes 8388608 | tf_op jit(solution)/shard_map/down_mine/pallas_call | solution.py:32
  38.9 1.9 %down.1 = (bf16[24,1024]{1,0:T(8,128)(2,1)S(1)}, bf16[24,1024]{1,0:T(8,128)(2,1)S(1)}, bf16[24,1024]{1,0:T(8,128)(2,1)S(1)}, bf16[24,1024]{1,0:T(8,128)(2,1)S(1)}, bf16[48,256]{1,0:T(8,128)(2,1)S(1)}) custom-call(s32[1,3,3,1,4]{4,3,2,1,0:T(1,128)} %bitcast.10, bf16[1,1,4,128,128]{4,3,2,1,0:T(8,128)(2,1)S(1)} %copy-done, f32[48,2048]{1,0:T(8,128)S(1)} %down_mine.1.refs_2_, ...), custom_call_target="tpu_custom_call" | custom-call | bytes 1024 | tf_op jit(solution)/shard_map/down/pallas_call | solution.py:32
  40.8 3.2 %collective-permute-start.14 = (bf16[24,1024]{1,0:T(8,128)(2,1)S(1)}, bf16[24,1024]{1,0:T(8,128)(2,1)S(1)}, u32[]{:S(2)}, u32[]{:S(2)}) collective-permute-start(bf16[24,1024]{1,0:T(8,128)(2,1)S(1)} %get-tuple-element.62), channel_id=1, source_target_pairs={{0,3},{1,2},{2,1},{3,0},{4,7},{5,6},{6,5},{7,4},{8,11},{9,10},{10,... | collective-permute-start | bytes 147464 | tf_op jit(solution)/shard_map/ppermute | solution.py:437
  44.0 1.2 %collective-permute-start.16 = (bf16[24,1024]{1,0:T(8,128)(2,1)S(1)}, bf16[24,1024]{1,0:T(8,128)(2,1)S(1)}, u32[]{:S(2)}, u32[]{:S(2)}) collective-permute-start(bf16[24,1024]{1,0:T(8,128)(2,1)S(1)} %get-tuple-element.64), channel_id=1, source_target_pairs={{0,1},{1,0},{2,3},{3,2},{4,5},{5,4},{6,7},{7,6},{8,9},{9,8},{10,11... | collective-permute-start | bytes 147464 | tf_op jit(solution)/shard_map/ppermute | solution.py:437
  45.3 0.9 %collective-permute-start.13 = (bf16[48,256]{1,0:T(8,128)(2,1)S(1)}, bf16[48,256]{1,0:T(8,128)(2,1)S(1)}, u32[]{:S(2)}, u32[]{:S(2)}) collective-permute-start(bf16[48,256]{1,0:T(8,128)(2,1)S(1)} %get-tuple-element.61), channel_id=1, source_target_pairs={{0,8},{4,12},{8,0},{12,4},{1,9},{5,13},{9,1},{13,5},{2,10},{6,14},... | collective-permute-start | bytes 73736 | tf_op jit(solution)/shard_map/ppermute | solution.py:437
  46.2 2.9 %collective-permute-done.13.refs_2_ = bf16[48,256]{1,0:T(8,128)(2,1)S(1)} collective-permute-done((bf16[48,256]{1,0:T(8,128)(2,1)S(1)}, bf16[48,256]{1,0:T(8,128)(2,1)S(1)}, u32[]{:S(2)}, u32[]{:S(2)}) %collective-permute-start.13) | collective-permute-done | bytes 24608 | tf_op jit(solution)/shard_map/ppermute | solution.py:437
  49.2 0.9 %finish.1 = (bf16[3,8192]{1,0:T(4,128)(2,1)}, bf16[12,2048]{1,0:T(8,128)(2,1)}) custom-call(bf16[48,128]{1,0:T(8,128)(2,1)S(1)} %get-tuple-element.39.refs_0_, bf16[48,2432]{1,0:T(8,128)(2,1)S(1)} %collective-permute-done.6.refs_1_.refs_5_, bf16[48,256]{1,0:T(8,128)(2,1)S(1)} %collective-permute-done.13.refs_2_, ...), custom_call_target="tpu_custom_call" | custom-call | bytes 1024 | tf_op jit(solution)/shard_map/finish/pallas_call | solution.py:32
  (45 shorter events, 2.6 us)
Async XLA Ops:
  1.8 6.3 %collective-permute-start = (bf16[4,16,512]{2,1,0:T(8,128)(2,1)S(1)}, bf16[4,16,512]{2,1,0:T(8,128)(2,1)S(1)}, u32[]{:S(2)}, u32[]{:S(2)}) collective-permute-start(bf16[4,16,512]{2,1,0:T(8,128)(2,1)S(1)} %get-tuple-element.35), channel_id=1, source_target_pairs={{0,8},{4,12},{8,0},{12,4},{1,9},{5,13},{9,1},{13,5},{2,10},{6,14},... | collective-permute-start | bytes 196616 | tf_op jit(solution)/shard_map/ppermute | solution.py:437
  4.8 4.1 %collective-permute-start.1 = (bf16[4,16,512]{2,1,0:T(8,128)(2,1)S(1)}, bf16[4,16,512]{2,1,0:T(8,128)(2,1)S(1)}, u32[]{:S(2)}, u32[]{:S(2)}) collective-permute-start(bf16[4,16,512]{2,1,0:T(8,128)(2,1)S(1)} %get-tuple-element.36), channel_id=1, source_target_pairs={{0,12},{4,8},{8,4},{12,0},{1,13},{5,9},{9,5},{13,1},{2,14},{6,10},... | collective-permute-start | bytes 196616 | tf_op jit(solution)/shard_map/ppermute | solution.py:437
  4.8 4.1 %collective-permute-start.2 = (bf16[4,16,512]{2,1,0:T(8,128)(2,1)S(1)}, bf16[4,16,512]{2,1,0:T(8,128)(2,1)S(1)}, u32[]{:S(2)}, u32[]{:S(2)}) collective-permute-start(bf16[4,16,512]{2,1,0:T(8,128)(2,1)S(1)} %get-tuple-element.37), channel_id=1, source_target_pairs={{0,4},{4,0},{8,12},{12,8},{1,5},{5,1},{9,13},{13,9},{2,6},{6,2},{1... | collective-permute-start | bytes 196616 | tf_op jit(solution)/shard_map/ppermute | solution.py:437
  10.5 8.2 %collective-permute-start.5 = (bf16[24,1024]{1,0:T(8,128)(2,1)S(1)}, bf16[24,1024]{1,0:T(8,128)(2,1)S(1)}, u32[]{:S(2)}, u32[]{:S(2)}) collective-permute-start(bf16[24,1024]{1,0:T(8,128)(2,1)S(1)} %get-tuple-element.41.refs_1_.refs_3_), channel_id=1, source_target_pairs={{0,3},{1,2},{2,1},{3,0},{4,7},{5,6},{6,5},{7,4},{8,11},{9,10},{10,... | collective-permute-start | bytes 147464 | tf_op jit(solution)/shard_map/ppermute | solution.py:437
  14.2 5.0 %collective-permute-start.4 = (bf16[24,1024]{1,0:T(8,128)(2,1)S(1)}, bf16[24,1024]{1,0:T(8,128)(2,1)S(1)}, u32[]{:S(2)}, u32[]{:S(2)}) collective-permute-start(bf16[24,1024]{1,0:T(8,128)(2,1)S(1)} %get-tuple-element.41.refs_1_.refs_3_), channel_id=1, source_target_pairs={{0,2},{1,3},{2,0},{3,1},{4,6},{5,7},{6,4},{7,5},{8,10},{9,11},{10,... | collective-permute-start | bytes 147464 | tf_op jit(solution)/shard_map/ppermute | solution.py:437
  14.2 5.0 %collective-permute-start.3 = (bf16[24,1024]{1,0:T(8,128)(2,1)S(1)}, bf16[24,1024]{1,0:T(8,128)(2,1)S(1)}, u32[]{:S(2)}, u32[]{:S(2)}) collective-permute-start(bf16[24,1024]{1,0:T(8,128)(2,1)S(1)} %get-tuple-element.41.refs_1_.refs_3_), channel_id=1, source_target_pairs={{0,1},{1,0},{2,3},{3,2},{4,5},{5,4},{6,7},{7,6},{8,9},{9,8},{10,11... | collective-permute-start | bytes 147464 | tf_op jit(solution)/shard_map/ppermute | solution.py:437
  15.0 11.2 %slice-start = ((s8[16777216]{0:T(1024)(128)(4,1)}), s8[4194304]{0:T(1024)(128)(4,1)S(1)}, s32[]{:S(2)}) async-start(s8[16777216]{0:T(1024)(128)(4,1)} %bitcast.4), calls=%async_computation | async-start | bytes 8388608
  15.0 11.2 %slice-start.1 = ((s8[16777216]{0:T(1024)(128)(4,1)}), s8[4194304]{0:T(1024)(128)(4,1)S(1)}, s32[]{:S(2)}) async-start(s8[16777216]{0:T(1024)(128)(4,1)} %bitcast.4), calls=%async_computation.1 | async-start | bytes 8388608
  19.2 6.9 %slice-start.3 = ((s8[16777216]{0:T(1024)(128)(4,1)}), s8[4194304]{0:T(1024)(128)(4,1)S(1)}, s32[]{:S(2)}) async-start(s8[16777216]{0:T(1024)(128)(4,1)} %bitcast.4), calls=%async_computation.3 | async-start | bytes 8388608
  23.2 1.6 %collective-permute-start.6 = (bf16[48,2432]{1,0:T(8,128)(2,1)S(1)}, bf16[48,2432]{1,0:T(8,128)(2,1)S(1)}, u32[]{:S(2)}, u32[]{:S(2)}) collective-permute-start(bf16[48,2432]{1,0:T(8,128)(2,1)S(1)} %get-tuple-element.52), channel_id=1, source_target_pairs={{0,4},{4,0},{8,12},{12,8},{1,5},{5,1},{9,13},{13,9},{2,6},{6,2},{1... | collective-permute-start | bytes 700424 | tf_op jit(solution)/shard_map/ppermute | solution.py:437
  25.0 12.0 %collective-permute-start.7 = (bf16[48,2176]{1,0:T(8,128)(2,1)S(1)}, bf16[48,2176]{1,0:T(8,128)(2,1)S(1)}, u32[]{:S(2)}, u32[]{:S(2)}) collective-permute-start(bf16[48,2176]{1,0:T(8,128)(2,1)S(1)} %chip_sum_first.1.refs_3_.refs_0_), channel_id=1, source_target_pairs={{0,8},{4,12},{8,0},{12,4},{1,9},{5,13},{9,1},{13,5},{2,10},{6,14},... | collective-permute-start | bytes 626696 | tf_op jit(solution)/shard_map/ppermute | solution.py:437
  26.2 11.1 %slice-start.4 = ((s8[16777216]{0:T(1024)(128)(4,1)}), s8[4194304]{0:T(1024)(128)(4,1)S(1)}, s32[]{:S(2)}) async-start(s8[16777216]{0:T(1024)(128)(4,1)} %bitcast.6), calls=%async_computation.4 | async-start | bytes 8388608
  26.2 11.1 %slice-start.5 = ((s8[16777216]{0:T(1024)(128)(4,1)}), s8[4194304]{0:T(1024)(128)(4,1)S(1)}, s32[]{:S(2)}) async-start(s8[16777216]{0:T(1024)(128)(4,1)} %bitcast.6), calls=%async_computation.5 | async-start | bytes 8388608
  27.8 9.5 %slice-start.6 = ((s8[16777216]{0:T(1024)(128)(4,1)}), s8[4194304]{0:T(1024)(128)(4,1)S(1)}, s32[]{:S(2)}) async-start(s8[16777216]{0:T(1024)(128)(4,1)} %bitcast.6), calls=%async_computation.6 | async-start | bytes 8388608
  27.8 9.5 %slice-start.7 = ((s8[16777216]{0:T(1024)(128)(4,1)}), s8[4194304]{0:T(1024)(128)(4,1)S(1)}, s32[]{:S(2)}) async-start(s8[16777216]{0:T(1024)(128)(4,1)} %bitcast.6), calls=%async_computation.7 | async-start | bytes 8388608
  27.8 2.2 %collective-permute-start.10 = (bf16[48,1024]{1,0:T(8,128)(2,1)S(1)}, bf16[48,1024]{1,0:T(8,128)(2,1)S(1)}, u32[]{:S(2)}, u32[]{:S(2)}) collective-permute-start(bf16[48,1024]{1,0:T(8,128)(2,1)S(1)} %get-tuple-element.59), channel_id=1, source_target_pairs={{0,4},{4,0},{8,12},{12,8},{1,5},{5,1},{9,13},{13,9},{2,6},{6,2},{1... | collective-permute-start | bytes 294920 | tf_op jit(solution)/shard_map/ppermute | solution.py:437
  29.5 1.5 %collective-permute-start.8 = (bf16[48,1024]{1,0:T(8,128)(2,1)S(1)}, bf16[48,1024]{1,0:T(8,128)(2,1)S(1)}, u32[]{:S(2)}, u32[]{:S(2)}) collective-permute-start(bf16[48,1024]{1,0:T(8,128)(2,1)S(1)} %get-tuple-element.57), channel_id=1, source_target_pairs={{0,4},{4,0},{8,12},{12,8},{1,5},{5,1},{9,13},{13,9},{2,6},{6,2},{1... | collective-permute-start | bytes 294920 | tf_op jit(solution)/shard_map/ppermute | solution.py:437
  30.1 5.6 %collective-permute-start.11 = (bf16[48,1024]{1,0:T(8,128)(2,1)S(1)}, bf16[48,1024]{1,0:T(8,128)(2,1)S(1)}, u32[]{:S(2)}, u32[]{:S(2)}) collective-permute-start(bf16[48,1024]{1,0:T(8,128)(2,1)S(1)} %chip_sum_next.3.refs_4_), channel_id=1, source_target_pairs={{0,8},{4,12},{8,0},{12,4},{1,9},{5,13},{9,1},{13,5},{2,10},{6,14},... | collective-permute-start | bytes 294920 | tf_op jit(solution)/shard_map/ppermute | solution.py:437
  31.1 5.9 %collective-permute-start.9 = (bf16[48,1024]{1,0:T(8,128)(2,1)S(1)}, bf16[48,1024]{1,0:T(8,128)(2,1)S(1)}, u32[]{:S(2)}, u32[]{:S(2)}) collective-permute-start(bf16[48,1024]{1,0:T(8,128)(2,1)S(1)} %chip_sum_next.2.refs_2_), channel_id=1, source_target_pairs={{0,8},{4,12},{8,0},{12,4},{1,9},{5,13},{9,1},{13,5},{2,10},{6,14},... | collective-permute-start | bytes 294920 | tf_op jit(solution)/shard_map/ppermute | solution.py:437
  37.2 1.7 %collective-permute-start.12 = (bf16[48,2048]{1,0:T(8,128)(2,1)S(1)}, bf16[48,2048]{1,0:T(8,128)(2,1)S(1)}, u32[]{:S(2)}, u32[]{:S(2)}) collective-permute-start(bf16[48,2048]{1,0:T(8,128)(2,1)S(1)} %hidden.1.refs_0_.refs_3_), channel_id=1, source_target_pairs={{0,4},{4,0},{8,12},{12,8},{1,5},{5,1},{9,13},{13,9},{2,6},{6,2},{1... | collective-permute-start | bytes 589832 | tf_op jit(solution)/shard_map/ppermute | solution.py:437
  40.8 8.3 %collective-permute-start.14 = (bf16[24,1024]{1,0:T(8,128)(2,1)S(1)}, bf16[24,1024]{1,0:T(8,128)(2,1)S(1)}, u32[]{:S(2)}, u32[]{:S(2)}) collective-permute-start(bf16[24,1024]{1,0:T(8,128)(2,1)S(1)} %get-tuple-element.62), channel_id=1, source_target_pairs={{0,3},{1,2},{2,1},{3,0},{4,7},{5,6},{6,5},{7,4},{8,11},{9,10},{10,... | collective-permute-start | bytes 147464 | tf_op jit(solution)/shard_map/ppermute | solution.py:437
  44.0 5.1 %collective-permute-start.15 = (bf16[24,1024]{1,0:T(8,128)(2,1)S(1)}, bf16[24,1024]{1,0:T(8,128)(2,1)S(1)}, u32[]{:S(2)}, u32[]{:S(2)}) collective-permute-start(bf16[24,1024]{1,0:T(8,128)(2,1)S(1)} %get-tuple-element.63), channel_id=1, source_target_pairs={{0,2},{1,3},{2,0},{3,1},{4,6},{5,7},{6,4},{7,5},{8,10},{9,11},{10,... | collective-permute-start | bytes 147464 | tf_op jit(solution)/shard_map/ppermute | solution.py:437
  44.0 5.1 %collective-permute-start.16 = (bf16[24,1024]{1,0:T(8,128)(2,1)S(1)}, bf16[24,1024]{1,0:T(8,128)(2,1)S(1)}, u32[]{:S(2)}, u32[]{:S(2)}) collective-permute-start(bf16[24,1024]{1,0:T(8,128)(2,1)S(1)} %get-tuple-element.64), channel_id=1, source_target_pairs={{0,1},{1,0},{2,3},{3,2},{4,5},{5,4},{6,7},{7,6},{8,9},{9,8},{10,11... | collective-permute-start | bytes 147464 | tf_op jit(solution)/shard_map/ppermute | solution.py:437
  45.3 3.8 %collective-permute-start.13 = (bf16[48,256]{1,0:T(8,128)(2,1)S(1)}, bf16[48,256]{1,0:T(8,128)(2,1)S(1)}, u32[]{:S(2)}, u32[]{:S(2)}) collective-permute-start(bf16[48,256]{1,0:T(8,128)(2,1)S(1)} %get-tuple-element.61), channel_id=1, source_target_pairs={{0,8},{4,12},{8,0},{12,4},{1,9},{5,13},{9,1},{13,5},{2,10},{6,14},... | collective-permute-start | bytes 73736 | tf_op jit(solution)/shard_map/ppermute | solution.py:437
  (2 other events, 8.7 us)

commit v6 on v5

--- a/solution.py
+++ b/solution.py
@@ -12,7 +12,7 @@
 HEAD_DIM = 128
 GROUP = HEADS // KV_HEADS
 MIB = 1 << 20
-FETCH = (3, 1, 4)
+FETCH = (1, 1, 6)
 BF16 = jnp.bfloat16
 F32 = jnp.float32
 VMEM = pltpu.VMEM
@@ -49,7 +49,7 @@
         self.ups = [(0, half // 2), (half // 2, half // 2)]
         self.tail = half
         self.step = min(512, half // 4)
-        self.jobs = [(keep, at) for keep in (False, True) for at in range(0, half, half // 4)]
+        self.jobs = [(mine, at) for mine in (True, False) for at in range(0, half, half // 4)]
         self.heads = HEADS // toks
         self.kvs = max(1, self.heads // GROUP)
         self.group = self.heads // self.kvs
@@ -120,36 +120,50 @@
     pl.when(lax.axis_index("tok") >= 0)(compute)
 
 
-def weight_blocks(jobs, gate_ref):
+def weight_blocks(jobs, down_ref):
     core = lax.axis_index("tok") % 2
-    half = gate_ref.shape[1] // 2
+    half = down_ref.shape[0] // 2
     found = []
-    for keep, first in jobs:
-        at = pl.multiple_of((core if keep else 1 - core) * half, half)
-        found.append(gate_ref.at[:, pl.ds(at + first, half // 4)])
+    for mine, first in jobs:
+        at = pl.multiple_of((core if mine else 1 - core) * half, half)
+        found.append(down_ref.at[pl.ds(at + first, half // 4), :])
     return found
 
 
-def fetch_kernel(jobs, whole, gain_size, gate_ref, *rest):
-    sources, rest = list(rest[: len(whole)]), rest[len(whole) :]
+def fetch_kernel(jobs, down_ref, delta_hbm, *rest):
     outs, sems = rest[:-1], rest[-1]
-    if gain_size:
-        tok = lax.axis_index("tok")
-        at = pl.multiple_of(tok * gain_size, gain_size)
-        sources[0] = sources[0].at[:, pl.ds(at, gain_size)]
-    sources += weight_blocks(jobs, gate_ref)
-    for copy in start_copies(list(zip(sources, outs)), sems):
+    for copy in start_copies(list(zip([delta_hbm] + weight_blocks(jobs, down_ref), outs)), sems):
         copy.wait()
 
 
-def attend_kernel(z, ctx, jobs, list_hbm, count_hbm, *rest):
-    gate_ref, pieces, rest = rest[0], rest[1 : 1 + z.toks], rest[1 + z.toks :]
+def first_fetch_kernel(z, list_hbm, count_hbm, gain_ref, gate_delta, up_delta, _, *rest):
+    place_ref, *outs = rest[:-4]
+    list_ref, count_ref, table_sems, sems = rest[-4:]
+    tables = start_copies([(list_hbm, list_ref), (count_hbm, count_ref)], table_sems)
+    features = outs[0].shape[1]
+    at = pl.multiple_of(lax.axis_index("tok") * features, features)
+    sources = [gain_ref.at[:, pl.ds(at, features)], gate_delta, up_delta]
+    copies = start_copies(list(zip(sources, outs)), sems)
+    for table in tables:
+        table.wait()
+
+    @after_starts
+    def _():
+        for g in range(z.toks):
+            for k in range(z.cap):
+                row = jnp.where(k < count_ref[0, g], list_ref[k, 0, g], -1)
+                at = (g * z.cap + k) * z.group
+                place_ref[at : at + z.group, :] = jnp.full((z.group, HEAD_DIM), row, jnp.int32)
+
+    for copy in copies:
+        copy.wait()
+
+
+def attend_kernel(z, ctx, place_ref, _, *rest):
+    pieces, rest = rest[: z.toks], rest[z.toks :]
     pieces = pieces[:1] + pieces[-1:] + pieces[1:-1]
     send_ref, back_refs, rest = rest[0], rest[1 : 1 + z.toks], rest[1 + z.toks :]
-    blocks, rest = rest[: len(jobs)], rest[len(jobs) :]
-    cache, req, query, own_key, own_value, alive, mixed_all, list_ref, count_ref, table_sems, sems = rest
-    tables = start_copies([(list_hbm, list_ref), (count_hbm, count_ref)], table_sems)
-    copies = start_copies(list(zip(weight_blocks(jobs, gate_ref), blocks)), sems)
+    cache, req, mixed_all = rest
 
     @after_starts
     def _():
@@ -161,27 +175,20 @@
             for p in range(z.pieces):
                 at, lane = z.cap + p // z.blocks, p % z.blocks * HEAD_DIM
                 r, part = p * 16 // z.req_rows, p * 16 % z.req_rows
-                req[source * 2 + r, part : part + 16, :] = pieces[s][
-                    at, :, lane : lane + HEAD_DIM
-                ].astype(F32)
-        for table in tables:
-            table.wait()
-        for g in range(z.toks):
-            for k in range(z.cap):
-                live = (k < count_ref[0, g]).astype(F32)
-                rows = req[list_ref[k, 0, g]] * live
-                at = (g * z.cap + k) * z.group
-                for j in range(z.kvs):
-                    query[j, at : at + z.group, :] = rows[j * z.group : (j + 1) * z.group, :]
-                    key, value = z.heads + j, z.heads + z.kvs + j
-                    own_key[j, at : at + z.group, :] = jnp.broadcast_to(
-                        rows[key : key + 1, :], (z.group, HEAD_DIM)
-                    )
-                    own_value[j, at : at + z.group, :] = jnp.broadcast_to(
-                        rows[value : value + 1, :], (z.group, HEAD_DIM)
-                    )
-                alive[at : at + z.group, :] = jnp.full((z.group, HEAD_DIM), live, F32)
+                req[source * 2 + r, part : part + 16, :] = pieces[s][at, :, lane : lane + HEAD_DIM]
         many, keys = z.lane_slots * z.group, z.toks * cache_rows
+        held = 2 * z.toks * z.req_rows
+        requests = req[...].reshape(held, HEAD_DIM)
+        first = place_ref[:, :1]
+        alive = (first >= 0).astype(F32)
+        first = first * z.req_rows
+        head = lax.broadcasted_iota(jnp.int32, (many, 1), 0) % z.group
+        column = lax.broadcasted_iota(jnp.int32, (many, held), 1)
+
+        def rows_at(at):
+            pick = (column == first + at).astype(F32).astype(BF16)
+            return jnp.dot(pick, requests, preferred_element_type=F32)
+
         row_slot = lax.broadcasted_iota(jnp.int32, (many, keys), 0) // z.group
         key_slot = lax.broadcasted_iota(jnp.int32, (many, keys), 1) // ctx
         same = row_slot == key_slot
@@ -190,16 +197,18 @@
             cached_keys = cache[:, :, j * HEAD_DIM : (j + 1) * HEAD_DIM].reshape(keys, HEAD_DIM)
             at = (z.kvs + j) * HEAD_DIM
             cached_values = cache[:, :, at : at + HEAD_DIM].reshape(keys, HEAD_DIM)
+            query = rows_at(head + j * z.group)
+            own_key, own_value = rows_at(z.heads + j), rows_at(z.heads + z.kvs + j)
             past = (
                 lax.dot_general(
-                    query[j].astype(BF16),
+                    query.astype(BF16),
                     cached_keys,
                     (((1,), (1,)), ((), ())),
                     preferred_element_type=F32,
                 )
                 * scale
             )
-            own = jnp.sum(query[j] * own_key[j], axis=-1, keepdims=True) * scale
+            own = jnp.sum(query * own_key, axis=-1, keepdims=True) * scale
             top = jnp.maximum(jnp.max(jnp.where(same, past, -jnp.inf), axis=-1, keepdims=True), own)
             past_exp = jnp.where(same, jnp.exp(jnp.where(same, past - top, 0.0)), 0.0)
             own_exp = jnp.exp(own - top)
@@ -207,7 +216,7 @@
             weights = (past_exp / total).astype(BF16)
             own_weight = (own_exp / total).astype(BF16).astype(F32)
             mixed = jnp.dot(weights, cached_values, preferred_element_type=F32)
-            mixed = (mixed + own_weight * own_value[j]) * alive[...]
+            mixed = (mixed + own_weight * own_value) * alive
             mixed_all[j * many : (j + 1) * many, :] = mixed.astype(BF16).astype(F32)
         block = z.cap * z.group
         for s in range(z.toks):
@@ -220,9 +229,6 @@
                 pl.ds(h, count, stride=z.group), :
             ].astype(BF16)
 
-    for copy in copies:
-        copy.wait()
-
 
 def halves(value):
     high = value.astype(BF16).astype(F32)
@@ -255,36 +261,47 @@
 def first_project_kernel(z, index_hbm, gain_ref, delta_ref, *rest):
     pieces, rest = rest[: z.cols], rest[z.cols :]
     odd_backs, rest = rest[: z.toks // 2], rest[z.toks // 2 :]
-    blocks, rest = rest[: len(z.jobs)], rest[len(z.jobs) :]
-    send_ref, keep_ref, source, extra, index_ref, index_sem = rest
+    weight, rest = rest[0], rest[1:]
+    send_ref, keep_ref, source, extra, stack, index_ref, index_sem = rest
     table = pltpu.make_async_copy(index_hbm, index_ref, index_sem)
     table.start()
 
     @after_starts
     def _():
-        gather_rows(z, pieces, gain_ref, odd_backs, source, extra, send_ref, keep_ref)
+        gather_rows(z, pieces, gain_ref, odd_backs, stack, source, send_ref, keep_ref)
+
+    core = lax.axis_index("tok") % 2
+    half = z.tail
+
+    @after_starts
+    def _():
+        for at in range(0, 2 * half, z.step):
+            lanes = slice(at, at + z.step)
+            extra[:, lanes] = jnp.dot(source[...], weight[:, lanes], preferred_element_type=F32)
 
     table.wait()
     tile_terms(z, source, delta_ref, index_ref, 0, extra, 0)
-    core = lax.axis_index("tok") % 2
-    half = z.tail
-    for (keep, first), block in zip(z.jobs, blocks):
-        out_ref, side = (keep_ref, core) if keep else (send_ref, 1 - core)
-        for p in range(0, half // 4, z.step):
-            at = pl.multiple_of(side * half + first + p, HEAD_DIM)
-            value = jnp.dot(source[...], block[:, p : p + z.step], preferred_element_type=F32)
-            value += extra[:, pl.ds(at, z.step)]
-            out_ref[:, first + p : first + p + z.step] = value.astype(BF16)
-
-
-def up_kernel(z, part, source, extra, up_ref, send_ref, keep_ref):
-    core = lax.axis_index("tok") % 2
-    first, size = part
     for out_ref, side in ((send_ref, 1 - core), (keep_ref, core)):
-        for p in range(0, size, z.step):
-            lanes = pl.ds(pl.multiple_of(side * z.tail + first + p, HEAD_DIM), z.step)
-            value = jnp.dot(source[...], up_ref[:, lanes], preferred_element_type=F32)
-            out_ref[:, p : p + z.step] = (value + extra[:, lanes]).astype(BF16)
+        for p in range(0, half, z.step):
+            at = pl.multiple_of(side * half + p, HEAD_DIM)
+            out_ref[:, p : p + z.step] = extra[:, pl.ds(at, z.step)].astype(BF16)
+
+
+def up_kernel(z, part, jobs, source, extra, up_ref, down_ref, send_ref, keep_ref, *rest):
+    copies = start_copies(list(zip(weight_blocks(jobs, down_ref), rest[:-1])), rest[-1])
+
+    @after_starts
+    def _():
+        core = lax.axis_index("tok") % 2
+        first, size = part
+        for out_ref, side in ((send_ref, 1 - core), (keep_ref, core)):
+            for p in range(0, size, z.step):
+                lanes = pl.ds(pl.multiple_of(side * z.tail + first + p, HEAD_DIM), z.step)
+                value = jnp.dot(source[...], up_ref[:, lanes], preferred_element_type=F32)
+                out_ref[:, p : p + z.step] = (value + extra[:, lanes]).astype(BF16)
+
+    for copy in copies:
+        copy.wait()
 
 
 def up_tiles_kernel(z, index_hbm, delta_ref, source, extra, index_ref, index_sem):
@@ -295,21 +312,25 @@
     tile_terms(z, source, delta_ref, index_ref, 1, extra, 0)
 
 
-def gather_rows(z, pieces, gain_ref, odd_backs, source, extra, send_ref, keep_ref):
+def gather_rows(z, pieces, gain_ref, odd_backs, stack, source, send_ref, keep_ref):
     col = lax.axis_index("col")
-    extra[...] = jnp.zeros_like(extra)
     count = z.kvs * z.lane_slots
     wide = z.group * HEAD_DIM
-    slot = slot_of_row(z, col, (z.rows, count))
+    deep = stack.shape[0] // z.cols
+    for s in range(z.cols):
+        piece = pieces[s][...].astype(F32)
+        if deep > count:
+            piece = jnp.concatenate([piece, jnp.zeros((deep - count, wide), F32)], axis=0)
+        stack[s * deep : (s + 1) * deep, :] = piece.astype(BF16)
+    shape = (z.rows, z.cols * deep)
+    slot = slot_of_row(z, col, shape)
     lane_of, owner = slot // z.cap % z.cols, slot // (z.cols * z.cap)
-    column = lax.broadcasted_iota(jnp.int32, (z.rows, count), 1)
+    column = lax.broadcasted_iota(jnp.int32, shape, 1)
+    first = (lane_of ^ col) * deep + owner * z.cap + slot % z.cap
     squares = jnp.zeros((z.rows, 1), F32)
     for j in range(z.kvs):
-        place = j * z.lane_slots + owner * z.cap + slot % z.cap
-        found = jnp.zeros((z.rows, wide), F32)
-        for s in range(z.cols):
-            pick = ((lane_of == (col ^ s)) & (column == place)).astype(F32).astype(BF16)
-            found += jnp.dot(pick, pieces[s][...], preferred_element_type=F32)
+        pick = (column == first + j * z.lane_slots).astype(F32).astype(BF16)
+        found = jnp.dot(pick, stack[...], preferred_element_type=F32)
         squares += jnp.sum(found * found, axis=-1, keepdims=True)
         lanes = slice(j * wide, (j + 1) * wide)
         source[:, lanes] = (found * gain_ref[:, lanes]).astype(BF16)
@@ -347,27 +368,27 @@
             out_ref[:, lanes] = (jax.nn.silu(gate) * up).astype(BF16)
 
 
-def down_products(mine, units_ref, weight_ref, total, before=None):
-    core = lax.axis_index("tok") % 2
-    half, width = units_ref.shape[1], total.shape[1]
-    at = pl.multiple_of((core if mine else 1 - core) * half, half)
+def down_products(units_ref, blocks, total, before=None):
+    width = total.shape[1]
+    deep = blocks[0].shape[0]
     step = min(width, 512)
     for to in range(0, width, step):
         lanes = slice(to, to + step)
-        value = jnp.dot(
-            units_ref[...], weight_ref[pl.ds(at, half), lanes], preferred_element_type=F32
-        )
-        total[:, lanes] = value if before is None else value + before[:, lanes]
-
-
-def down_mine_kernel(mine, weight, total):
-    down_products(True, mine, weight, total)
+        value = jnp.zeros((total.shape[0], step), F32) if before is None else before[:, lanes]
+        for n, block in enumerate(blocks):
+            units = units_ref[:, n * deep : (n + 1) * deep]
+            value += jnp.dot(units, block[:, lanes], preferred_element_type=F32)
+        total[:, lanes] = value
+
+
+def down_mine_kernel(mine, *rest):
+    down_products(mine, rest[:-1], rest[-1])
 
 
 def down_kernel(z, index_hbm, delta_ref, before, mine, other, from_core, *rest):
     others = z.toks // 2 - 1
     evens, rest = rest[:others], rest[others:]
-    weight, rest = rest[0], rest[1:]
+    blocks, rest = rest[: len(z.jobs) // 2], rest[len(z.jobs) // 2 :]
     outs, backs, rest = rest[: z.cols], rest[z.cols : z.cols + others], rest[z.cols + others :]
     source, total, fold, index_ref, index_sem = rest
     table = pltpu.make_async_copy(index_hbm, index_ref, index_sem)
@@ -379,7 +400,7 @@
         half = mine.shape[1]
         source[:, pl.ds(pl.multiple_of(core * half, half), half)] = mine[...]
         source[:, pl.ds(pl.multiple_of((1 - core) * half, half), half)] = other[...]
-        down_products(False, other, weight, total, before)
+        down_products(other, blocks, total, before)
 
     for s, back in enumerate(backs):
         back[:, :HEAD_DIM] = evens[s][...]
@@ -470,10 +491,10 @@
     cuts = [0]
     for count in FETCH:
         cuts.append(cuts[-1] + count)
-    early, middle, late = [z.jobs[a:b] for a, b in zip(cuts, cuts[1:])]
+    *beside, final = [z.jobs[a:b] for a, b in zip(cuts, cuts[1:])]
 
     def shapes(some):
-        return [((features, units // 8), BF16) for _ in some]
+        return [((units // 8, down_weight.shape[1]), BF16) for _ in some]
 
     def traffic(some):
         moved = sum(a * b * 2 for (a, b), _ in shapes(some))
@@ -498,52 +519,38 @@
             dma,
             dma((toks, 2)),
         ],
-    )
-    whole = [gain, gate_delta, up_delta]
-    gain, gate_delta, up_delta, *blocks = call(
-        functools.partial(fetch_kernel, early, whole, features),
+        cost=product(1),
+    )
+    place, gain, gate_delta, up_delta = call(
+        functools.partial(first_fetch_kernel, z),
         "fetch_early",
-        [(a, HBM) for a in [gate_weight] + whole],
-        [((1, features), F32), (gate_delta.shape, BF16), (up_delta.shape, BF16)]
-        + shapes(early),
-        [dma((len(early) + 3,))],
-        after=pieces[:1],
-        cost=traffic(early),
-    )
-    pieces = [pieces[0]] + [swap(pieces[s], "tok", toks, s) for s in range(1, toks)]
-    back_rows = z.kvs * cap * z.group
-    send, *rest = call(
-        functools.partial(attend_kernel, z, ctx, middle),
-        "attend",
-        [(a, HBM) for a in [route_list, route_count, gate_weight]] + [(p, VMEM) for p in pieces[:1] + pieces[2:] + pieces[1:2]],
-        [((z.kvs * z.lane_slots, z.group * HEAD_DIM), BF16)]
-        + [((back_rows, HEAD_DIM), BF16)] * toks
-        + shapes(middle),
+        [(a, HBM) for a in [route_list, route_count, gain, gate_delta, up_delta, gate_weight]],
+        [((many, HEAD_DIM), jnp.int32), ((1, features), F32)]
+        + [(gate_delta.shape, BF16), (up_delta.shape, BF16)],
         [
-            pltpu.VMEM((toks, cache_rows, lanes), BF16),
-            pltpu.VMEM((2 * toks, z.req_rows, HEAD_DIM), F32),
-            pltpu.VMEM((z.kvs, many, HEAD_DIM), F32),
-            pltpu.VMEM((z.kvs, many, HEAD_DIM), F32),
-            pltpu.VMEM((z.kvs, many, HEAD_DIM), F32),
-            pltpu.VMEM((many, HEAD_DIM), F32),
-            pltpu.VMEM((z.kvs * many, HEAD_DIM), F32),
             pltpu.SMEM(route_list.shape, jnp.int32),
             pltpu.SMEM(route_count.shape, jnp.int32),
             dma((2,)),
-            dma((max(1, len(middle)),)),
+            dma((3,)),
         ],
+        cost=traffic([]),
+        after=pieces[:1],
+    )
+    pieces = [pieces[0]] + [swap(pieces[s], "tok", toks, s) for s in range(1, toks)]
+    back_rows = z.kvs * cap * z.group
+    send, *back = call(
+        functools.partial(attend_kernel, z, ctx),
+        "attend",
+        [(place, VMEM), (gate_weight, HBM)] + [(p, VMEM) for p in pieces[:1] + pieces[2:] + pieces[1:2]],
+        [((z.kvs * z.lane_slots, z.group * HEAD_DIM), BF16)]
+        + [((back_rows, HEAD_DIM), BF16)] * toks,
+        [
+            pltpu.VMEM((toks, cache_rows, lanes), BF16),
+            pltpu.VMEM((2 * toks, z.req_rows, HEAD_DIM), BF16),
+            pltpu.VMEM((z.kvs * many, HEAD_DIM), F32),
+        ],
+        cost=product(1),
         after=[gain],
-    )
-    back = rest[:toks]
-    blocks += rest[toks:]
-    blocks += call(
-        functools.partial(fetch_kernel, late, [], 0),
-        "fetch_late",
-        [(gate_weight, HBM)],
-        shapes(late),
-        [dma((len(late),))],
-        after=[send],
-        cost=traffic(late),
     )
     pieces = [send] + [swap(send, "col", cols, s) for s in range(1, cols)]
     out_width = down_weight.shape[1]
@@ -552,13 +559,18 @@
         functools.partial(first_project_kernel, z),
         "gate",
         [(tile_index, HBM), (gain, VMEM), (gate_delta, VMEM)]
-        + [(p, VMEM) for p in pieces + back[1::2] + blocks],
+        + [(p, VMEM) for p in pieces + back[1::2] + [gate_weight]],
         [
             ((z.rows, z.tail + (1 + chips) * HEAD_DIM), BF16),
             ((z.rows, z.tail + HEAD_DIM), BF16),
             ((z.rows, features), BF16),
         ],
-        [pltpu.VMEM((z.rows, units), F32), table, dma],
+        [
+            pltpu.VMEM((z.rows, units), F32),
+            pltpu.VMEM((cols * -(-z.kvs * z.lane_slots // 16) * 16, z.group * HEAD_DIM), BF16),
+            table,
+            dma,
+        ],
         cost=product(1),
     )
     from_core = swap(sent, "tok", toks, 1)
@@ -579,16 +591,19 @@
             after=[extra],
         )
     ]
-    for part in z.ups:
+    blocks = []
+    for part, jobs in zip(z.ups, beside):
         size = part[1]
-        sent, kept = call(
-            functools.partial(up_kernel, z, part),
+        sent, kept, *fetched = call(
+            functools.partial(up_kernel, z, part, jobs),
             "up",
-            [(a, VMEM) for a in [source, extra, up_weight]],
-            [((z.rows, size), BF16)] * 2,
+            [(a, VMEM) for a in [source, extra, up_weight]] + [(down_weight, HBM)],
+            [((z.rows, size), BF16)] * 2 + shapes(jobs),
+            [dma((len(jobs),))],
             cost=product(size / units * 2),
             after=totals[0],
         )
+        blocks += fetched
         totals.append(
             call(
                 functools.partial(add_kernel, z),
@@ -601,16 +616,28 @@
         total + [swap(total[0], "tok", toks, 2 * s) for s in range(1, chips)]
         for total in totals
     ]
+    down_delta, *fetched = call(
+        functools.partial(fetch_kernel, final),
+        "fetch_down",
+        [(down_weight, HBM), (down_delta, HBM)],
+        [(down_delta.shape, BF16)] + shapes(final),
+        [dma((len(final) + 1,))],
+        cost=traffic(final),
+        after=totals[-1],
+    )
+    blocks += fetched
+    half = len(blocks) // 2
     (hidden,) = call(
         functools.partial(hidden_kernel, z, width),
         "hidden",
         [(a, VMEM) for part in parts for a in part],
         [((z.rows, units // 2), BF16)],
+        after=fetched[-1:],
     )
     (before,) = call(
         down_mine_kernel,
         "down_mine",
-        [(hidden, VMEM), (down_weight, VMEM)],
+        [(a, VMEM) for a in [hidden] + blocks[:half]],
         [((z.rows, out_width), F32)],
         cost=pl.CostEstimate(
             flops=z.rows * units * out_width, bytes_accessed=units * out_width, transcendentals=0
@@ -621,7 +648,7 @@
         "down",
         [(tile_index, HBM)]
         + [(a, VMEM) for a in [down_delta, before, hidden, swap(hidden, "tok", toks, 1), from_core]]
-        + [(a, VMEM) for a in back[2::2] + [down_weight]],
+        + [(a, VMEM) for a in back[2::2] + blocks[half:]],
         [((2 * z.lane_slots, out_width // 2), BF16)] * cols
         + [((back_rows, 2 * HEAD_DIM), BF16)] * (chips - 1),
         [

time: 50.3 us -> 49.3 us (0.980)
  Pallas kernels: 22.4 us -> 20.7 us
  waiting for transfers between devices: 9.65 us -> 10.3 us
    pallas_call x15, Pallas kernels: 22.4 us -> 20.7 us  [call(): pl.pallas_call(body, name=name, in_specs=[pl.BlockSpec(memory_space=s) fo...]
    ppermute x17, waiting for transfers between devices: 9.65 us -> 10.3 us  [swap(): return lax.ppermute(array, axis, [(i, i ^ distance) for i in range(size)])]
  transfers between devices with their start and end apart: 17 -> 17, of which waited for: 7 -> 6; matrix products, arithmetic and copies ran while one was open for 0% -> 0% of each run, Pallas kernels for 25% -> 24%
where the time goes in v6:
time: 49.3 us; the launch traced here: 49 us
  Pallas kernels  20.7 us (42%)
  starting transfers between devices  17.1 us (35%)
  waiting for transfers between devices  10.3 us (21%)
  between operations  0.85 us (2%)
    pallas_call x15, Pallas kernels, call(): pl.pallas_call(body, name=name, in_specs=[pl.BlockSpec(memory_space=s) fo...  20.7 us
    ppermute x17, starting transfers between devices, swap(): return lax.ppermute(array, axis, [(i, i ^ distance) for i in range(size)])  17.1 us
    ppermute x17, waiting for transfers between devices, swap(): return lax.ppermute(array, axis, [(i, i ^ distance) for i in range(size)])  10.3 us
  transfers between devices with their start and end apart: 17, of which 6 were waited for; matrix products, arithmetic and copies ran while one was open for 0% of the time, Pallas kernels for 24%

profile of v6, /device:TPU:0, one launch (start us, length us, event | category | flops | bytes accessed | tf_op | source)
XLA Modules:
  0.0 49.0 jit_solution(616484463932409462)
XLA Ops:
  0.6 1.1 %pack.1 = (bf16[4,16,512]{2,1,0:T(8,128)(2,1)S(1)}, bf16[4,16,512]{2,1,0:T(8,128)(2,1)S(1)}, bf16[4,16,512]{2,1,0:T(8,128)(2,1)S(1)}, bf16[4,16,512]{2,1,0:T(8,128)(2,1)S(1)}) custom-call(bf16[2,10240]{1,0:T(2,128)(2,1)} %refs_0_.2, bf16[3,16,2048]{2,1,0:T(8,128)(2,1)} %refs_1_.3), custom_call_target="tpu_custom_call" | custom-call | flops 805306368 | bytes 16777216 | tf_op jit(solution)/shard_map/pack/pallas_call | solution.py:32
  1.8 3.0 %collective-permute-start = (bf16[4,16,512]{2,1,0:T(8,128)(2,1)S(1)}, bf16[4,16,512]{2,1,0:T(8,128)(2,1)S(1)}, u32[]{:S(2)}, u32[]{:S(2)}) collective-permute-start(bf16[4,16,512]{2,1,0:T(8,128)(2,1)S(1)} %get-tuple-element.38), channel_id=1, source_target_pairs={{0,8},{4,12},{8,0},{12,4},{1,9},{5,13},{9,1},{13,5},{2,10},{6,14},... | collective-permute-start | bytes 196616 | tf_op jit(solution)/shard_map/ppermute | solution.py:458
  5.0 1.2 %fetch_early.1 = (s32[96,128]{1,0:T(8,128)S(1)}, f32[1,2048]{1,0:T(1,128)S(1)}, bf16[1,1,4,128,128]{4,3,2,1,0:T(8,128)(2,1)S(1)}, bf16[1,1,4,128,128]{4,3,2,1,0:T(8,128)(2,1)S(1)}) custom-call(s32[3,1,4]{2,1,0:T(1,128)} %bitcast.12, s32[1,4]{1,0:T(1,128)} %bitcast.13, f32[1,8192]{1,0:T(1,128)} %bitcast.11, bf16[1,1,4,128,128]{4,3,2,1,0:T(8,128)(2,1)} %refs_3_.3, ...), custom_call_target="tpu_custom_call" | custom-call | tf_op jit(solution)/shard_map/fetch_early/pallas_call | solution.py:32
  6.1 0.9 %collective-permute-done.refs_3_ = bf16[4,16,512]{2,1,0:T(8,128)(2,1)S(1)} collective-permute-done((bf16[4,16,512]{2,1,0:T(8,128)(2,1)S(1)}, bf16[4,16,512]{2,1,0:T(8,128)(2,1)S(1)}, u32[]{:S(2)}, u32[]{:S(2)}) %collective-permute-start) | collective-permute-done | bytes 65568 | tf_op jit(solution)/shard_map/ppermute | solution.py:458
  7.0 1.9 %collective-permute-done.1.refs_4_ = bf16[4,16,512]{2,1,0:T(8,128)(2,1)S(1)} collective-permute-done((bf16[4,16,512]{2,1,0:T(8,128)(2,1)S(1)}, bf16[4,16,512]{2,1,0:T(8,128)(2,1)S(1)}, u32[]{:S(2)}, u32[]{:S(2)}) %collective-permute-start.1) | collective-permute-done | bytes 65568 | tf_op jit(solution)/shard_map/ppermute | solution.py:458
  8.9 1.2 %attend.1 = (bf16[24,1024]{1,0:T(8,128)(2,1)S(1)}, bf16[48,128]{1,0:T(8,128)(2,1)S(1)}, bf16[48,128]{1,0:T(8,128)(2,1)S(1)}, bf16[48,128]{1,0:T(8,128)(2,1)S(1)}, bf16[48,128]{1,0:T(8,128)(2,1)S(1)}) custom-call(s32[96,128]{1,0:T(8,128)S(1)} %get-tuple-element.37.refs_0_, bf16[2048,4096]{1,0:T(8,128)(2,1)} %refs_9_.1, ...), custom_call_target="tpu_custom_call" | custom-call | flops 805306368 | bytes 16777216 | tf_op jit(solution)/shard_map/attend/pallas_call | solution.py:32
  10.1 3.7 %collective-permute-start.5 = (bf16[24,1024]{1,0:T(8,128)(2,1)S(1)}, bf16[24,1024]{1,0:T(8,128)(2,1)S(1)}, u32[]{:S(2)}, u32[]{:S(2)}) collective-permute-start(bf16[24,1024]{1,0:T(8,128)(2,1)S(1)} %get-tuple-element.44.refs_3_), channel_id=1, source_target_pairs={{0,3},{1,2},{2,1},{3,0},{4,7},{5,6},{6,5},{7,4},{8,11},{9,10},{10,... | collective-permute-start | bytes 147464 | tf_op jit(solution)/shard_map/ppermute | solution.py:458
  14.5 1.8 %collective-permute-done.5.refs_6_ = bf16[24,1024]{1,0:T(8,128)(2,1)S(1)} collective-permute-done((bf16[24,1024]{1,0:T(8,128)(2,1)S(1)}, bf16[24,1024]{1,0:T(8,128)(2,1)S(1)}, u32[]{:S(2)}, u32[]{:S(2)}) %collective-permute-start.5) | collective-permute-done | bytes 49184 | tf_op jit(solution)/shard_map/ppermute | solution.py:458
  16.3 2.5 %collective-permute-done.4.refs_5_ = bf16[24,1024]{1,0:T(8,128)(2,1)S(1)} collective-permute-done((bf16[24,1024]{1,0:T(8,128)(2,1)S(1)}, bf16[24,1024]{1,0:T(8,128)(2,1)S(1)}, u32[]{:S(2)}, u32[]{:S(2)}) %collective-permute-start.4) | collective-permute-done | bytes 49184 | tf_op jit(solution)/shard_map/ppermute | solution.py:458
  18.8 3.6 %gate.1 = (bf16[48,2432]{1,0:T(8,128)(2,1)S(1)}, bf16[48,2176]{1,0:T(8,128)(2,1)S(1)}, bf16[48,2048]{1,0:T(8,128)(2,1)S(1)}) custom-call(s32[1,3,3,1,4]{4,3,2,1,0:T(1,128)} %bitcast.8, f32[1,2048]{1,0:T(1,128)S(1)} %get-tuple-element.41.refs_6_.refs_1_, bf16[1,1,4,128,128]{4,3,2,1,0:T(8,128)(2,1)S(1)} %get-tuple-element.43.refs_2_, ...), custom_call_target="tpu_custom_call" | custom-call | flops 805306368 | bytes 16777216 | tf_op jit(solution)/shard_map/gate/pallas_call | solution.py:32
  22.6 0.9 %up_tiles.1.refs_2_.refs_1_ = f32[48,4096]{1,0:T(8,128)S(1)} custom-call(s32[1,3,3,1,4]{4,3,2,1,0:T(1,128)} %bitcast.9, bf16[1,1,4,128,128]{4,3,2,1,0:T(8,128)(2,1)S(1)} %get-tuple-element.49.refs_1_, bf16[48,2048]{1,0:T(8,128)(2,1)S(1)} %get-tuple-element.48.refs_2_.refs_0_), custom_call_target="tpu_custom_call" | custom-call | flops 100663296 | bytes 2097152 | tf_op jit(solution)/shard_map/up_tiles/pallas_call | solution.py:32
  24.2 1.0 %collective-permute-start.8 = (bf16[48,2176]{1,0:T(8,128)(2,1)S(1)}, bf16[48,2176]{1,0:T(8,128)(2,1)S(1)}, u32[]{:S(2)}, u32[]{:S(2)}) collective-permute-start(bf16[48,2176]{1,0:T(8,128)(2,1)S(1)} %chip_sum_first.1.refs_4_.refs_0_), channel_id=1, source_target_pairs={{0,8},{4,12},{8,0},{12,4},{1,9},{5,13},{9,1},{13,5},{2,10},{6,14},... | collective-permute-start | bytes 626696 | tf_op jit(solution)/shard_map/ppermute | solution.py:458
  25.2 1.6 %up.3 = (bf16[48,1024]{1,0:T(8,128)(2,1)S(1)}, bf16[48,1024]{1,0:T(8,128)(2,1)S(1)}, bf16[512,2048]{1,0:T(8,128)(2,1)S(1)}) custom-call(bf16[48,2048]{1,0:T(8,128)(2,1)S(1)} %get-tuple-element.48.refs_2_.refs_0_, f32[48,4096]{1,0:T(8,128)S(1)} %up_tiles.1.refs_2_.refs_1_, bf16[2048,4096]{1,0:T(8,128)(2,1)S(1)} %bitcast.7, bf16[4096,2048]{1,0:T(8,128)(2,1)} %refs_3_.5, ...), custom_call_target="tpu_custom_call" | custom-call | flops 402653184 | bytes 8388608 | tf_op jit(solution)/shard_map/up/pallas_call | solution.py:32
  26.9 1.6 %up.2 = (bf16[48,1024]{1,0:T(8,128)(2,1)S(1)}, bf16[48,1024]{1,0:T(8,128)(2,1)S(1)}, bf16[512,2048]{1,0:T(8,128)(2,1)S(1)}) custom-call(bf16[48,2048]{1,0:T(8,128)(2,1)S(1)} %get-tuple-element.48.refs_2_.refs_0_, f32[48,4096]{1,0:T(8,128)S(1)} %up_tiles.1.refs_2_.refs_1_, bf16[2048,4096]{1,0:T(8,128)(2,1)S(1)} %bitcast.7, bf16[4096,2048]{1,0:T(8,128)(2,1)} %refs_3_.5, ...), custom_call_target="tpu_custom_call" | custom-call | flops 402653184 | bytes 8388608 | tf_op jit(solution)/shard_map/up/pallas_call | solution.py:32
  29.1 1.2 %collective-permute-start.10 = (bf16[48,1024]{1,0:T(8,128)(2,1)S(1)}, bf16[48,1024]{1,0:T(8,128)(2,1)S(1)}, u32[]{:S(2)}, u32[]{:S(2)}) collective-permute-start(bf16[48,1024]{1,0:T(8,128)(2,1)S(1)} %chip_sum_next.3.refs_2_), channel_id=1, source_target_pairs={{0,8},{4,12},{8,0},{12,4},{1,9},{5,13},{9,1},{13,5},{2,10},{6,14},... | collective-permute-start | bytes 294920 | tf_op jit(solution)/shard_map/ppermute | solution.py:458
  30.3 1.0 %collective-permute-start.11 = (bf16[48,1024]{1,0:T(8,128)(2,1)S(1)}, bf16[48,1024]{1,0:T(8,128)(2,1)S(1)}, u32[]{:S(2)}, u32[]{:S(2)}) collective-permute-start(bf16[48,1024]{1,0:T(8,128)(2,1)S(1)} %chip_sum_next.2.refs_2_.refs_4_), channel_id=1, source_target_pairs={{0,8},{4,12},{8,0},{12,4},{1,9},{5,13},{9,1},{13,5},{2,10},{6,14},... | collective-permute-start | bytes 294920 | tf_op jit(solution)/shard_map/ppermute | solution.py:458
  31.3 4.8 %fetch_down.1 = (bf16[1,1,4,128,128]{4,3,2,1,0:T(8,128)(2,1)S(1)}, bf16[512,2048]{1,0:T(8,128)(2,1)S(1)}, bf16[512,2048]{1,0:T(8,128)(2,1)S(1)}, bf16[512,2048]{...) custom-call(bf16[4096,2048]{1,0:T(8,128)(2,1)} %refs_3_.5, ...), custom_call_target="tpu_custom_call" | custom-call | bytes 12582912 | tf_op jit(solution)/shard_map/fetch_down/pallas_call | solution.py:32
  36.4 1.6 %down_mine.1.refs_2_ = f32[48,2048]{1,0:T(8,128)S(1)} custom-call(bf16[48,2048]{1,0:T(8,128)(2,1)S(1)} %hidden.1.refs_0_.refs_3_, bf16[512,2048]{1,0:T(8,128)(2,1)S(1)} %get-tuple-element.57.refs_1_, bf16[512,2048]{1,0:T(8,128)(2,1)S(1)} %get-tuple-element.58.refs_2_, bf16[512,2048]{1,0:T(8,128)(2,1)S(1)} %get-tuple-element.59.refs_3_, ...), custom_call_target="tpu_custom_call" | custom-call | flops 402653184 | bytes 8388608 | tf_op jit(solution)/shard_map/down_mine/pallas_call | solution.py:32
  38.0 1.9 %down.1 = (bf16[24,1024]{1,0:T(8,128)(2,1)S(1)}, bf16[24,1024]{1,0:T(8,128)(2,1)S(1)}, bf16[24,1024]{1,0:T(8,128)(2,1)S(1)}, bf16[24,1024]{1,0:T(8,128)(2,1)S(1)}, bf16[48,256]{1,0:T(8,128)(2,1)S(1)}) custom-call(s32[1,3,3,1,4]{4,3,2,1,0:T(1,128)} %bitcast.10, bf16[1,1,4,128,128]{4,3,2,1,0:T(8,128)(2,1)S(1)} %get-tuple-element.53.refs_1_, ...), custom_call_target="tpu_custom_call" | custom-call | bytes 1024 | tf_op jit(solution)/shard_map/down/pallas_call | solution.py:32
  39.9 2.2 %collective-permute-start.14 = (bf16[24,1024]{1,0:T(8,128)(2,1)S(1)}, bf16[24,1024]{1,0:T(8,128)(2,1)S(1)}, u32[]{:S(2)}, u32[]{:S(2)}) collective-permute-start(bf16[24,1024]{1,0:T(8,128)(2,1)S(1)} %get-tuple-element.66), channel_id=1, source_target_pairs={{0,3},{1,2},{2,1},{3,0},{4,7},{5,6},{6,5},{7,4},{8,11},{9,10},{10,... | collective-permute-start | bytes 147464 | tf_op jit(solution)/shard_map/ppermute | solution.py:458
  42.6 1.8 %collective-permute-start.16 = (bf16[24,1024]{1,0:T(8,128)(2,1)S(1)}, bf16[24,1024]{1,0:T(8,128)(2,1)S(1)}, u32[]{:S(2)}, u32[]{:S(2)}) collective-permute-start(bf16[24,1024]{1,0:T(8,128)(2,1)S(1)} %get-tuple-element.68), channel_id=1, source_target_pairs={{0,1},{1,0},{2,3},{3,2},{4,5},{5,4},{6,7},{7,6},{8,9},{9,8},{10,11... | collective-permute-start | bytes 147464 | tf_op jit(solution)/shard_map/ppermute | solution.py:458
  44.3 1.1 %collective-permute-start.13 = (bf16[48,256]{1,0:T(8,128)(2,1)S(1)}, bf16[48,256]{1,0:T(8,128)(2,1)S(1)}, u32[]{:S(2)}, u32[]{:S(2)}) collective-permute-start(bf16[48,256]{1,0:T(8,128)(2,1)S(1)} %get-tuple-element.65), channel_id=1, source_target_pairs={{0,8},{4,12},{8,0},{12,4},{1,9},{5,13},{9,1},{13,5},{2,10},{6,14},... | collective-permute-start | bytes 73736 | tf_op jit(solution)/shard_map/ppermute | solution.py:458
  45.4 2.7 %collective-permute-done.13.refs_2_ = bf16[48,256]{1,0:T(8,128)(2,1)S(1)} collective-permute-done((bf16[48,256]{1,0:T(8,128)(2,1)S(1)}, bf16[48,256]{1,0:T(8,128)(2,1)S(1)}, u32[]{:S(2)}, u32[]{:S(2)}) %collective-permute-start.13) | collective-permute-done | bytes 24608 | tf_op jit(solution)/shard_map/ppermute | solution.py:458
  48.2 0.9 %finish.1 = (bf16[3,8192]{1,0:T(4,128)(2,1)}, bf16[12,2048]{1,0:T(8,128)(2,1)}) custom-call(bf16[48,128]{1,0:T(8,128)(2,1)S(1)} %get-tuple-element.42.refs_0_, bf16[48,2432]{1,0:T(8,128)(2,1)S(1)} %collective-permute-done.6.refs_1_.refs_5_, bf16[48,256]{1,0:T(8,128)(2,1)S(1)} %collective-permute-done.13.refs_2_, ...), custom_call_target="tpu_custom_call" | custom-call | bytes 1024 | tf_op jit(solution)/shard_map/finish/pallas_call | solution.py:32
  (43 shorter events, 3.2 us)
Async XLA Ops:
  1.8 5.2 %collective-permute-start = (bf16[4,16,512]{2,1,0:T(8,128)(2,1)S(1)}, bf16[4,16,512]{2,1,0:T(8,128)(2,1)S(1)}, u32[]{:S(2)}, u32[]{:S(2)}) collective-permute-start(bf16[4,16,512]{2,1,0:T(8,128)(2,1)S(1)} %get-tuple-element.38), channel_id=1, source_target_pairs={{0,8},{4,12},{8,0},{12,4},{1,9},{5,13},{9,1},{13,5},{2,10},{6,14},... | collective-permute-start | bytes 196616 | tf_op jit(solution)/shard_map/ppermute | solution.py:458
  4.8 4.1 %collective-permute-start.1 = (bf16[4,16,512]{2,1,0:T(8,128)(2,1)S(1)}, bf16[4,16,512]{2,1,0:T(8,128)(2,1)S(1)}, u32[]{:S(2)}, u32[]{:S(2)}) collective-permute-start(bf16[4,16,512]{2,1,0:T(8,128)(2,1)S(1)} %get-tuple-element.39), channel_id=1, source_target_pairs={{0,12},{4,8},{8,4},{12,0},{1,13},{5,9},{9,5},{13,1},{2,14},{6,10},... | collective-permute-start | bytes 196616 | tf_op jit(solution)/shard_map/ppermute | solution.py:458
  4.8 4.1 %collective-permute-start.2 = (bf16[4,16,512]{2,1,0:T(8,128)(2,1)S(1)}, bf16[4,16,512]{2,1,0:T(8,128)(2,1)S(1)}, u32[]{:S(2)}, u32[]{:S(2)}) collective-permute-start(bf16[4,16,512]{2,1,0:T(8,128)(2,1)S(1)} %get-tuple-element.40), channel_id=1, source_target_pairs={{0,4},{4,0},{8,12},{12,8},{1,5},{5,1},{9,13},{13,9},{2,6},{6,2},{1... | collective-permute-start | bytes 196616 | tf_op jit(solution)/shard_map/ppermute | solution.py:458
  5.0 13.8 %slice-start = ((s8[16777216]{0:T(1024)(128)(4,1)}), s8[4194304]{0:T(1024)(128)(4,1)S(1)}, s32[]{:S(2)}) async-start(s8[16777216]{0:T(1024)(128)(4,1)} %bitcast.4), calls=%async_computation | async-start | bytes 8388608
  5.0 13.8 %slice-start.1 = ((s8[16777216]{0:T(1024)(128)(4,1)}), s8[4194304]{0:T(1024)(128)(4,1)S(1)}, s32[]{:S(2)}) async-start(s8[16777216]{0:T(1024)(128)(4,1)} %bitcast.4), calls=%async_computation.1 | async-start | bytes 8388608
  5.0 13.8 %slice-start.2 = ((s8[16777216]{0:T(1024)(128)(4,1)}), s8[4194304]{0:T(1024)(128)(4,1)S(1)}, s32[]{:S(2)}) async-start(s8[16777216]{0:T(1024)(128)(4,1)} %bitcast.4), calls=%async_computation.2 | async-start | bytes 8388608
  8.9 9.9 %slice-start.3 = ((s8[16777216]{0:T(1024)(128)(4,1)}), s8[4194304]{0:T(1024)(128)(4,1)S(1)}, s32[]{:S(2)}) async-start(s8[16777216]{0:T(1024)(128)(4,1)} %bitcast.4), calls=%async_computation.3 | async-start | bytes 8388608
  8.9 16.3 %slice-start.4 = ((s8[16777216]{0:T(1024)(128)(4,1)}), s8[4194304]{0:T(1024)(128)(4,1)S(1)}, s32[]{:S(2)}) async-start(s8[16777216]{0:T(1024)(128)(4,1)} %bitcast.6), calls=%async_computation.4 | async-start | bytes 8388608
  8.9 16.3 %slice-start.5 = ((s8[16777216]{0:T(1024)(128)(4,1)}), s8[4194304]{0:T(1024)(128)(4,1)S(1)}, s32[]{:S(2)}) async-start(s8[16777216]{0:T(1024)(128)(4,1)} %bitcast.6), calls=%async_computation.5 | async-start | bytes 8388608
  10.1 6.2 %collective-permute-start.5 = (bf16[24,1024]{1,0:T(8,128)(2,1)S(1)}, bf16[24,1024]{1,0:T(8,128)(2,1)S(1)}, u32[]{:S(2)}, u32[]{:S(2)}) collective-permute-start(bf16[24,1024]{1,0:T(8,128)(2,1)S(1)} %get-tuple-element.44.refs_3_), channel_id=1, source_target_pairs={{0,3},{1,2},{2,1},{3,0},{4,7},{5,6},{6,5},{7,4},{8,11},{9,10},{10,... | collective-permute-start | bytes 147464 | tf_op jit(solution)/shard_map/ppermute | solution.py:458
  13.8 5.0 %collective-permute-start.4 = (bf16[24,1024]{1,0:T(8,128)(2,1)S(1)}, bf16[24,1024]{1,0:T(8,128)(2,1)S(1)}, u32[]{:S(2)}, u32[]{:S(2)}) collective-permute-start(bf16[24,1024]{1,0:T(8,128)(2,1)S(1)} %get-tuple-element.44.refs_3_), channel_id=1, source_target_pairs={{0,2},{1,3},{2,0},{3,1},{4,6},{5,7},{6,4},{7,5},{8,10},{9,11},{10,... | collective-permute-start | bytes 147464 | tf_op jit(solution)/shard_map/ppermute | solution.py:458
  13.8 5.0 %collective-permute-start.3 = (bf16[24,1024]{1,0:T(8,128)(2,1)S(1)}, bf16[24,1024]{1,0:T(8,128)(2,1)S(1)}, u32[]{:S(2)}, u32[]{:S(2)}) collective-permute-start(bf16[24,1024]{1,0:T(8,128)(2,1)S(1)} %get-tuple-element.44.refs_3_), channel_id=1, source_target_pairs={{0,1},{1,0},{2,3},{3,2},{4,5},{5,4},{6,7},{7,6},{8,9},{9,8},{10,11... | collective-permute-start | bytes 147464 | tf_op jit(solution)/shard_map/ppermute | solution.py:458
  18.8 6.4 %slice-start.6 = ((s8[16777216]{0:T(1024)(128)(4,1)}), s8[4194304]{0:T(1024)(128)(4,1)S(1)}, s32[]{:S(2)}) async-start(s8[16777216]{0:T(1024)(128)(4,1)} %bitcast.6), calls=%async_computation.6 | async-start | bytes 8388608
  22.5 1.6 %collective-permute-start.6 = (bf16[48,2432]{1,0:T(8,128)(2,1)S(1)}, bf16[48,2432]{1,0:T(8,128)(2,1)S(1)}, u32[]{:S(2)}, u32[]{:S(2)}) collective-permute-start(bf16[48,2432]{1,0:T(8,128)(2,1)S(1)} %get-tuple-element.47), channel_id=1, source_target_pairs={{0,4},{4,0},{8,12},{12,8},{1,5},{5,1},{9,13},{13,9},{2,6},{6,2},{1... | collective-permute-start | bytes 700424 | tf_op jit(solution)/shard_map/ppermute | solution.py:458
  24.2 11.9 %collective-permute-start.8 = (bf16[48,2176]{1,0:T(8,128)(2,1)S(1)}, bf16[48,2176]{1,0:T(8,128)(2,1)S(1)}, u32[]{:S(2)}, u32[]{:S(2)}) collective-permute-start(bf16[48,2176]{1,0:T(8,128)(2,1)S(1)} %chip_sum_first.1.refs_4_.refs_0_), channel_id=1, source_target_pairs={{0,8},{4,12},{8,0},{12,4},{1,9},{5,13},{9,1},{13,5},{2,10},{6,14},... | collective-permute-start | bytes 626696 | tf_op jit(solution)/shard_map/ppermute | solution.py:458
  26.8 2.3 %collective-permute-start.9 = (bf16[48,1024]{1,0:T(8,128)(2,1)S(1)}, bf16[48,1024]{1,0:T(8,128)(2,1)S(1)}, u32[]{:S(2)}, u32[]{:S(2)}) collective-permute-start(bf16[48,1024]{1,0:T(8,128)(2,1)S(1)} %get-tuple-element.55), channel_id=1, source_target_pairs={{0,4},{4,0},{8,12},{12,8},{1,5},{5,1},{9,13},{13,9},{2,6},{6,2},{1... | collective-permute-start | bytes 294920 | tf_op jit(solution)/shard_map/ppermute | solution.py:458
  28.5 1.8 %collective-permute-start.7 = (bf16[48,1024]{1,0:T(8,128)(2,1)S(1)}, bf16[48,1024]{1,0:T(8,128)(2,1)S(1)}, u32[]{:S(2)}, u32[]{:S(2)}) collective-permute-start(bf16[48,1024]{1,0:T(8,128)(2,1)S(1)} %get-tuple-element.52), channel_id=1, source_target_pairs={{0,4},{4,0},{8,12},{12,8},{1,5},{5,1},{9,13},{13,9},{2,6},{6,2},{1... | collective-permute-start | bytes 294920 | tf_op jit(solution)/shard_map/ppermute | solution.py:458
  29.1 7.0 %collective-permute-start.10 = (bf16[48,1024]{1,0:T(8,128)(2,1)S(1)}, bf16[48,1024]{1,0:T(8,128)(2,1)S(1)}, u32[]{:S(2)}, u32[]{:S(2)}) collective-permute-start(bf16[48,1024]{1,0:T(8,128)(2,1)S(1)} %chip_sum_next.3.refs_2_), channel_id=1, source_target_pairs={{0,8},{4,12},{8,0},{12,4},{1,9},{5,13},{9,1},{13,5},{2,10},{6,14},... | collective-permute-start | bytes 294920 | tf_op jit(solution)/shard_map/ppermute | solution.py:458
  30.3 5.8 %collective-permute-start.11 = (bf16[48,1024]{1,0:T(8,128)(2,1)S(1)}, bf16[48,1024]{1,0:T(8,128)(2,1)S(1)}, u32[]{:S(2)}, u32[]{:S(2)}) collective-permute-start(bf16[48,1024]{1,0:T(8,128)(2,1)S(1)} %chip_sum_next.2.refs_2_.refs_4_), channel_id=1, source_target_pairs={{0,8},{4,12},{8,0},{12,4},{1,9},{5,13},{9,1},{13,5},{2,10},{6,14},... | collective-permute-start | bytes 294920 | tf_op jit(solution)/shard_map/ppermute | solution.py:458
  36.3 1.7 %collective-permute-start.12 = (bf16[48,2048]{1,0:T(8,128)(2,1)S(1)}, bf16[48,2048]{1,0:T(8,128)(2,1)S(1)}, u32[]{:S(2)}, u32[]{:S(2)}) collective-permute-start(bf16[48,2048]{1,0:T(8,128)(2,1)S(1)} %hidden.1.refs_0_.refs_3_), channel_id=1, source_target_pairs={{0,4},{4,0},{8,12},{12,8},{1,5},{5,1},{9,13},{13,9},{2,6},{6,2},{1... | collective-permute-start | bytes 589832 | tf_op jit(solution)/shard_map/ppermute | solution.py:458
  39.9 8.3 %collective-permute-start.14 = (bf16[24,1024]{1,0:T(8,128)(2,1)S(1)}, bf16[24,1024]{1,0:T(8,128)(2,1)S(1)}, u32[]{:S(2)}, u32[]{:S(2)}) collective-permute-start(bf16[24,1024]{1,0:T(8,128)(2,1)S(1)} %get-tuple-element.66), channel_id=1, source_target_pairs={{0,3},{1,2},{2,1},{3,0},{4,7},{5,6},{6,5},{7,4},{8,11},{9,10},{10,... | collective-permute-start | bytes 147464 | tf_op jit(solution)/shard_map/ppermute | solution.py:458
  42.1 6.1 %collective-permute-start.15 = (bf16[24,1024]{1,0:T(8,128)(2,1)S(1)}, bf16[24,1024]{1,0:T(8,128)(2,1)S(1)}, u32[]{:S(2)}, u32[]{:S(2)}) collective-permute-start(bf16[24,1024]{1,0:T(8,128)(2,1)S(1)} %get-tuple-element.67), channel_id=1, source_target_pairs={{0,2},{1,3},{2,0},{3,1},{4,6},{5,7},{6,4},{7,5},{8,10},{9,11},{10,... | collective-permute-start | bytes 147464 | tf_op jit(solution)/shard_map/ppermute | solution.py:458
  42.6 5.6 %collective-permute-start.16 = (bf16[24,1024]{1,0:T(8,128)(2,1)S(1)}, bf16[24,1024]{1,0:T(8,128)(2,1)S(1)}, u32[]{:S(2)}, u32[]{:S(2)}) collective-permute-start(bf16[24,1024]{1,0:T(8,128)(2,1)S(1)} %get-tuple-element.68), channel_id=1, source_target_pairs={{0,1},{1,0},{2,3},{3,2},{4,5},{5,4},{6,7},{7,6},{8,9},{9,8},{10,11... | collective-permute-start | bytes 147464 | tf_op jit(solution)/shard_map/ppermute | solution.py:458
  44.3 3.8 %collective-permute-start.13 = (bf16[48,256]{1,0:T(8,128)(2,1)S(1)}, bf16[48,256]{1,0:T(8,128)(2,1)S(1)}, u32[]{:S(2)}, u32[]{:S(2)}) collective-permute-start(bf16[48,256]{1,0:T(8,128)(2,1)S(1)} %get-tuple-element.65), channel_id=1, source_target_pairs={{0,8},{4,12},{8,0},{12,4},{1,9},{5,13},{9,1},{13,5},{2,10},{6,14},... | collective-permute-start | bytes 73736 | tf_op jit(solution)/shard_map/ppermute | solution.py:458
  (1 other events, 6.4 us)

commit v7 on v6

--- a/solution.py
+++ b/solution.py
@@ -12,7 +12,7 @@
 HEAD_DIM = 128
 GROUP = HEADS // KV_HEADS
 MIB = 1 << 20
-FETCH = (1, 1, 6)
+FETCH = (1, 1, 5, 1)
 BF16 = jnp.bfloat16
 F32 = jnp.float32
 VMEM = pltpu.VMEM
@@ -381,8 +381,12 @@
         total[:, lanes] = value
 
 
-def down_mine_kernel(mine, *rest):
-    down_products(mine, rest[:-1], rest[-1])
+def down_mine_kernel(z, jobs, down_ref, mine, *rest):
+    blocks, (total, *fetched, sems) = rest[: len(z.jobs) // 2], rest[len(z.jobs) // 2 :]
+    copies = start_copies(list(zip(weight_blocks(jobs, down_ref), fetched)), sems)
+    after_starts(lambda: down_products(mine, blocks, total))
+    for copy in copies:
+        copy.wait()
 
 
 def down_kernel(z, index_hbm, delta_ref, before, mine, other, from_core, *rest):
@@ -491,7 +495,7 @@
     cuts = [0]
     for count in FETCH:
         cuts.append(cuts[-1] + count)
-    *beside, final = [z.jobs[a:b] for a, b in zip(cuts, cuts[1:])]
+    *beside, final, ending = [z.jobs[a:b] for a, b in zip(cuts, cuts[1:])]
 
     def shapes(some):
         return [((units // 8, down_weight.shape[1]), BF16) for _ in some]
@@ -626,7 +630,7 @@
         after=totals[-1],
     )
     blocks += fetched
-    half = len(blocks) // 2
+    half = len(z.jobs) // 2
     (hidden,) = call(
         functools.partial(hidden_kernel, z, width),
         "hidden",
@@ -634,15 +638,17 @@
         [((z.rows, units // 2), BF16)],
         after=fetched[-1:],
     )
-    (before,) = call(
-        down_mine_kernel,
+    before, *fetched = call(
+        functools.partial(down_mine_kernel, z, ending),
         "down_mine",
-        [(a, VMEM) for a in [hidden] + blocks[:half]],
-        [((z.rows, out_width), F32)],
+        [(down_weight, HBM)] + [(a, VMEM) for a in [hidden] + blocks[:half]],
+        [((z.rows, out_width), F32)] + shapes(ending),
+        [dma((len(ending),))],
         cost=pl.CostEstimate(
             flops=z.rows * units * out_width, bytes_accessed=units * out_width, transcendentals=0
         ),
     )
+    blocks += fetched
     parts = call(
         functools.partial(down_kernel, z),
         "down",

time: 49.3 us -> 49.3 us (level)
  Pallas kernels: 20.7 us -> 20.2 us
  waiting for transfers between devices: 10.3 us -> 10.8 us
    pallas_call x15, Pallas kernels: 20.7 us -> 20.2 us  [call(): pl.pallas_call(body, name=name, in_specs=[pl.BlockSpec(memory_space=s) fo...]
    ppermute x17, waiting for transfers between devices: 10.3 us -> 10.8 us  [swap(): return lax.ppermute(array, axis, [(i, i ^ distance) for i in range(size)])]
  transfers between devices with their start and end apart: 17 -> 17, of which waited for: 6 -> 7; matrix products, arithmetic and copies ran while one was open for 0% -> 0% of each run, Pallas kernels for 24% -> 23%
where the time goes in v7:
time: 49.3 us; the launch traced here: 49 us
  Pallas kernels  20.2 us (41%)
  starting transfers between devices  17.1 us (35%)
  waiting for transfers between devices  10.8 us (22%)
  between operations  0.84 us (2%)
    pallas_call x15, Pallas kernels, call(): pl.pallas_call(body, name=name, in_specs=[pl.BlockSpec(memory_space=s) fo...  20.2 us
    ppermute x17, starting transfers between devices, swap(): return lax.ppermute(array, axis, [(i, i ^ distance) for i in range(size)])  17.1 us
    ppermute x17, waiting for transfers between devices, swap(): return lax.ppermute(array, axis, [(i, i ^ distance) for i in range(size)])  10.8 us
  transfers between devices with their start and end apart: 17, of which 7 were waited for; matrix products, arithmetic and copies ran while one was open for 0% of the time, Pallas kernels for 23%

profile of v7, /device:TPU:0, one launch (start us, length us, event | category | flops | bytes accessed | tf_op | source)
XLA Modules:
  0.0 49.0 jit_solution(3932686777013913139)
XLA Ops:
  0.6 1.1 %pack.1 = (bf16[4,16,512]{2,1,0:T(8,128)(2,1)S(1)}, bf16[4,16,512]{2,1,0:T(8,128)(2,1)S(1)}, bf16[4,16,512]{2,1,0:T(8,128)(2,1)S(1)}, bf16[4,16,512]{2,1,0:T(8,128)(2,1)S(1)}) custom-call(bf16[2,10240]{1,0:T(2,128)(2,1)} %refs_0_.3, bf16[3,16,2048]{2,1,0:T(8,128)(2,1)} %refs_1_.3), custom_call_target="tpu_custom_call" | custom-call | flops 805306368 | bytes 16777216 | tf_op jit(solution)/shard_map/pack/pallas_call | solution.py:32
  1.8 3.0 %collective-permute-start = (bf16[4,16,512]{2,1,0:T(8,128)(2,1)S(1)}, bf16[4,16,512]{2,1,0:T(8,128)(2,1)S(1)}, u32[]{:S(2)}, u32[]{:S(2)}) collective-permute-start(bf16[4,16,512]{2,1,0:T(8,128)(2,1)S(1)} %get-tuple-element.39), channel_id=1, source_target_pairs={{0,8},{4,12},{8,0},{12,4},{1,9},{5,13},{9,1},{13,5},{2,10},{6,14},... | collective-permute-start | bytes 196616 | tf_op jit(solution)/shard_map/ppermute | solution.py:462
  5.0 1.2 %fetch_early.1 = (s32[96,128]{1,0:T(8,128)S(1)}, f32[1,2048]{1,0:T(1,128)S(1)}, bf16[1,1,4,128,128]{4,3,2,1,0:T(8,128)(2,1)S(1)}, bf16[1,1,4,128,128]{4,3,2,1,0:T(8,128)(2,1)S(1)}) custom-call(s32[3,1,4]{2,1,0:T(1,128)} %bitcast.12, s32[1,4]{1,0:T(1,128)} %bitcast.13, f32[1,8192]{1,0:T(1,128)} %bitcast.11, bf16[1,1,4,128,128]{4,3,2,1,0:T(8,128)(2,1)} %refs_3_.3, ...), custom_call_target="tpu_custom_call" | custom-call | tf_op jit(solution)/shard_map/fetch_early/pallas_call | solution.py:32
  6.1 0.9 %collective-permute-done.refs_3_ = bf16[4,16,512]{2,1,0:T(8,128)(2,1)S(1)} collective-permute-done((bf16[4,16,512]{2,1,0:T(8,128)(2,1)S(1)}, bf16[4,16,512]{2,1,0:T(8,128)(2,1)S(1)}, u32[]{:S(2)}, u32[]{:S(2)}) %collective-permute-start) | collective-permute-done | bytes 65568 | tf_op jit(solution)/shard_map/ppermute | solution.py:462
  7.0 1.9 %collective-permute-done.1.refs_4_ = bf16[4,16,512]{2,1,0:T(8,128)(2,1)S(1)} collective-permute-done((bf16[4,16,512]{2,1,0:T(8,128)(2,1)S(1)}, bf16[4,16,512]{2,1,0:T(8,128)(2,1)S(1)}, u32[]{:S(2)}, u32[]{:S(2)}) %collective-permute-start.1) | collective-permute-done | bytes 65568 | tf_op jit(solution)/shard_map/ppermute | solution.py:462
  8.9 1.2 %attend.1 = (bf16[24,1024]{1,0:T(8,128)(2,1)S(1)}, bf16[48,128]{1,0:T(8,128)(2,1)S(1)}, bf16[48,128]{1,0:T(8,128)(2,1)S(1)}, bf16[48,128]{1,0:T(8,128)(2,1)S(1)}, bf16[48,128]{1,0:T(8,128)(2,1)S(1)}) custom-call(s32[96,128]{1,0:T(8,128)S(1)} %get-tuple-element.38.refs_0_, bf16[2048,4096]{1,0:T(8,128)(2,1)} %refs_9_.1, ...), custom_call_target="tpu_custom_call" | custom-call | flops 805306368 | bytes 16777216 | tf_op jit(solution)/shard_map/attend/pallas_call | solution.py:32
  10.1 3.7 %collective-permute-start.5 = (bf16[24,1024]{1,0:T(8,128)(2,1)S(1)}, bf16[24,1024]{1,0:T(8,128)(2,1)S(1)}, u32[]{:S(2)}, u32[]{:S(2)}) collective-permute-start(bf16[24,1024]{1,0:T(8,128)(2,1)S(1)} %get-tuple-element.45.refs_3_), channel_id=1, source_target_pairs={{0,3},{1,2},{2,1},{3,0},{4,7},{5,6},{6,5},{7,4},{8,11},{9,10},{10,... | collective-permute-start | bytes 147464 | tf_op jit(solution)/shard_map/ppermute | solution.py:462
  14.5 1.8 %collective-permute-done.5.refs_6_ = bf16[24,1024]{1,0:T(8,128)(2,1)S(1)} collective-permute-done((bf16[24,1024]{1,0:T(8,128)(2,1)S(1)}, bf16[24,1024]{1,0:T(8,128)(2,1)S(1)}, u32[]{:S(2)}, u32[]{:S(2)}) %collective-permute-start.5) | collective-permute-done | bytes 49184 | tf_op jit(solution)/shard_map/ppermute | solution.py:462
  16.3 2.5 %collective-permute-done.4.refs_5_ = bf16[24,1024]{1,0:T(8,128)(2,1)S(1)} collective-permute-done((bf16[24,1024]{1,0:T(8,128)(2,1)S(1)}, bf16[24,1024]{1,0:T(8,128)(2,1)S(1)}, u32[]{:S(2)}, u32[]{:S(2)}) %collective-permute-start.4) | collective-permute-done | bytes 49184 | tf_op jit(solution)/shard_map/ppermute | solution.py:462
  18.8 3.6 %gate.1 = (bf16[48,2432]{1,0:T(8,128)(2,1)S(1)}, bf16[48,2176]{1,0:T(8,128)(2,1)S(1)}, bf16[48,2048]{1,0:T(8,128)(2,1)S(1)}) custom-call(s32[1,3,3,1,4]{4,3,2,1,0:T(1,128)} %bitcast.8, f32[1,2048]{1,0:T(1,128)S(1)} %get-tuple-element.42.refs_6_.refs_1_, bf16[1,1,4,128,128]{4,3,2,1,0:T(8,128)(2,1)S(1)} %get-tuple-element.44.refs_2_, ...), custom_call_target="tpu_custom_call" | custom-call | flops 805306368 | bytes 16777216 | tf_op jit(solution)/shard_map/gate/pallas_call | solution.py:32
  22.6 0.9 %up_tiles.1.refs_2_.refs_1_ = f32[48,4096]{1,0:T(8,128)S(1)} custom-call(s32[1,3,3,1,4]{4,3,2,1,0:T(1,128)} %bitcast.9, bf16[1,1,4,128,128]{4,3,2,1,0:T(8,128)(2,1)S(1)} %get-tuple-element.50.refs_1_, bf16[48,2048]{1,0:T(8,128)(2,1)S(1)} %get-tuple-element.49.refs_2_.refs_0_), custom_call_target="tpu_custom_call" | custom-call | flops 100663296 | bytes 2097152 | tf_op jit(solution)/shard_map/up_tiles/pallas_call | solution.py:32
  24.2 1.0 %collective-permute-start.8 = (bf16[48,2176]{1,0:T(8,128)(2,1)S(1)}, bf16[48,2176]{1,0:T(8,128)(2,1)S(1)}, u32[]{:S(2)}, u32[]{:S(2)}) collective-permute-start(bf16[48,2176]{1,0:T(8,128)(2,1)S(1)} %chip_sum_first.1.refs_4_.refs_0_), channel_id=1, source_target_pairs={{0,8},{4,12},{8,0},{12,4},{1,9},{5,13},{9,1},{13,5},{2,10},{6,14},... | collective-permute-start | bytes 626696 | tf_op jit(solution)/shard_map/ppermute | solution.py:462
  25.2 1.6 %up.3 = (bf16[48,1024]{1,0:T(8,128)(2,1)S(1)}, bf16[48,1024]{1,0:T(8,128)(2,1)S(1)}, bf16[512,2048]{1,0:T(8,128)(2,1)S(1)}) custom-call(bf16[48,2048]{1,0:T(8,128)(2,1)S(1)} %get-tuple-element.49.refs_2_.refs_0_, f32[48,4096]{1,0:T(8,128)S(1)} %up_tiles.1.refs_2_.refs_1_, bf16[2048,4096]{1,0:T(8,128)(2,1)S(1)} %bitcast.7, bf16[4096,2048]{1,0:T(8,128)(2,1)} %refs_0_.5, ...), custom_call_target="tpu_custom_call" | custom-call | flops 402653184 | bytes 8388608 | tf_op jit(solution)/shard_map/up/pallas_call | solution.py:32
  26.9 1.6 %up.2 = (bf16[48,1024]{1,0:T(8,128)(2,1)S(1)}, bf16[48,1024]{1,0:T(8,128)(2,1)S(1)}, bf16[512,2048]{1,0:T(8,128)(2,1)S(1)}) custom-call(bf16[48,2048]{1,0:T(8,128)(2,1)S(1)} %get-tuple-element.49.refs_2_.refs_0_, f32[48,4096]{1,0:T(8,128)S(1)} %up_tiles.1.refs_2_.refs_1_, bf16[2048,4096]{1,0:T(8,128)(2,1)S(1)} %bitcast.7, bf16[4096,2048]{1,0:T(8,128)(2,1)} %refs_0_.5, ...), custom_call_target="tpu_custom_call" | custom-call | flops 402653184 | bytes 8388608 | tf_op jit(solution)/shard_map/up/pallas_call | solution.py:32
  29.1 1.2 %collective-permute-start.10 = (bf16[48,1024]{1,0:T(8,128)(2,1)S(1)}, bf16[48,1024]{1,0:T(8,128)(2,1)S(1)}, u32[]{:S(2)}, u32[]{:S(2)}) collective-permute-start(bf16[48,1024]{1,0:T(8,128)(2,1)S(1)} %chip_sum_next.3.refs_2_), channel_id=1, source_target_pairs={{0,8},{4,12},{8,0},{12,4},{1,9},{5,13},{9,1},{13,5},{2,10},{6,14},... | collective-permute-start | bytes 294920 | tf_op jit(solution)/shard_map/ppermute | solution.py:462
  30.3 1.0 %collective-permute-start.11 = (bf16[48,1024]{1,0:T(8,128)(2,1)S(1)}, bf16[48,1024]{1,0:T(8,128)(2,1)S(1)}, u32[]{:S(2)}, u32[]{:S(2)}) collective-permute-start(bf16[48,1024]{1,0:T(8,128)(2,1)S(1)} %chip_sum_next.2.refs_2_.refs_4_), channel_id=1, source_target_pairs={{0,8},{4,12},{8,0},{12,4},{1,9},{5,13},{9,1},{13,5},{2,10},{6,14},... | collective-permute-start | bytes 294920 | tf_op jit(solution)/shard_map/ppermute | solution.py:462
  31.3 4.2 %fetch_down.1 = (bf16[1,1,4,128,128]{4,3,2,1,0:T(8,128)(2,1)S(1)}, bf16[512,2048]{1,0:T(8,128)(2,1)S(1)}, bf16[512,2048]{1,0:T(8,128)(2,1)S(1)}, bf16[512,2048]{...) custom-call(bf16[4096,2048]{1,0:T(8,128)(2,1)} %refs_0_.5, ...), custom_call_target="tpu_custom_call" | custom-call | bytes 10485760 | tf_op jit(solution)/shard_map/fetch_down/pallas_call | solution.py:32
  36.3 1.6 %down_mine.1 = (f32[48,2048]{1,0:T(8,128)S(1)}, bf16[512,2048]{1,0:T(8,128)(2,1)S(1)}) custom-call(bf16[4096,2048]{1,0:T(8,128)(2,1)} %refs_0_.5, bf16[48,2048]{1,0:T(8,128)(2,1)S(1)} %hidden.1.refs_1_.refs_3_, bf16[512,2048]{1,0:T(8,128)(2,1)S(1)} %get-tuple-element.58.refs_2_, bf16[512,2048]{1,0:T(8,128)(2,1)S(1)} %get-tuple-element.59.refs_3_, ...), custom_call_target="tpu_custom_call" | custom-call | flops 402653184 | bytes 8388608 | tf_op jit(solution)/shard_map/down_mine/pallas_call | solution.py:32
  37.9 1.9 %down.1 = (bf16[24,1024]{1,0:T(8,128)(2,1)S(1)}, bf16[24,1024]{1,0:T(8,128)(2,1)S(1)}, bf16[24,1024]{1,0:T(8,128)(2,1)S(1)}, bf16[24,1024]{1,0:T(8,128)(2,1)S(1)}, bf16[48,256]{1,0:T(8,128)(2,1)S(1)}) custom-call(s32[1,3,3,1,4]{4,3,2,1,0:T(1,128)} %bitcast.10, bf16[1,1,4,128,128]{4,3,2,1,0:T(8,128)(2,1)S(1)} %get-tuple-element.54.refs_1_, ...), custom_call_target="tpu_custom_call" | custom-call | bytes 1024 | tf_op jit(solution)/shard_map/down/pallas_call | solution.py:32
  39.8 2.1 %collective-permute-start.14 = (bf16[24,1024]{1,0:T(8,128)(2,1)S(1)}, bf16[24,1024]{1,0:T(8,128)(2,1)S(1)}, u32[]{:S(2)}, u32[]{:S(2)}) collective-permute-start(bf16[24,1024]{1,0:T(8,128)(2,1)S(1)} %get-tuple-element.68), channel_id=1, source_target_pairs={{0,3},{1,2},{2,1},{3,0},{4,7},{5,6},{6,5},{7,4},{8,11},{9,10},{10,... | collective-permute-start | bytes 147464 | tf_op jit(solution)/shard_map/ppermute | solution.py:462
  42.5 1.8 %collective-permute-start.16 = (bf16[24,1024]{1,0:T(8,128)(2,1)S(1)}, bf16[24,1024]{1,0:T(8,128)(2,1)S(1)}, u32[]{:S(2)}, u32[]{:S(2)}) collective-permute-start(bf16[24,1024]{1,0:T(8,128)(2,1)S(1)} %get-tuple-element.70), channel_id=1, source_target_pairs={{0,1},{1,0},{2,3},{3,2},{4,5},{5,4},{6,7},{7,6},{8,9},{9,8},{10,11... | collective-permute-start | bytes 147464 | tf_op jit(solution)/shard_map/ppermute | solution.py:462
  44.3 1.1 %collective-permute-start.13 = (bf16[48,256]{1,0:T(8,128)(2,1)S(1)}, bf16[48,256]{1,0:T(8,128)(2,1)S(1)}, u32[]{:S(2)}, u32[]{:S(2)}) collective-permute-start(bf16[48,256]{1,0:T(8,128)(2,1)S(1)} %get-tuple-element.67), channel_id=1, source_target_pairs={{0,8},{4,12},{8,0},{12,4},{1,9},{5,13},{9,1},{13,5},{2,10},{6,14},... | collective-permute-start | bytes 73736 | tf_op jit(solution)/shard_map/ppermute | solution.py:462
  45.4 2.7 %collective-permute-done.13.refs_2_ = bf16[48,256]{1,0:T(8,128)(2,1)S(1)} collective-permute-done((bf16[48,256]{1,0:T(8,128)(2,1)S(1)}, bf16[48,256]{1,0:T(8,128)(2,1)S(1)}, u32[]{:S(2)}, u32[]{:S(2)}) %collective-permute-start.13) | collective-permute-done | bytes 24608 | tf_op jit(solution)/shard_map/ppermute | solution.py:462
  48.1 0.9 %finish.1 = (bf16[3,8192]{1,0:T(4,128)(2,1)}, bf16[12,2048]{1,0:T(8,128)(2,1)}) custom-call(bf16[48,128]{1,0:T(8,128)(2,1)S(1)} %get-tuple-element.43.refs_0_, bf16[48,2432]{1,0:T(8,128)(2,1)S(1)} %collective-permute-done.6.refs_1_.refs_5_, bf16[48,256]{1,0:T(8,128)(2,1)S(1)} %collective-permute-done.13.refs_2_, ...), custom_call_target="tpu_custom_call" | custom-call | bytes 1024 | tf_op jit(solution)/shard_map/finish/pallas_call | solution.py:32
  (43 shorter events, 3.7 us)
Async XLA Ops:
  1.8 5.2 %collective-permute-start = (bf16[4,16,512]{2,1,0:T(8,128)(2,1)S(1)}, bf16[4,16,512]{2,1,0:T(8,128)(2,1)S(1)}, u32[]{:S(2)}, u32[]{:S(2)}) collective-permute-start(bf16[4,16,512]{2,1,0:T(8,128)(2,1)S(1)} %get-tuple-element.39), channel_id=1, source_target_pairs={{0,8},{4,12},{8,0},{12,4},{1,9},{5,13},{9,1},{13,5},{2,10},{6,14},... | collective-permute-start | bytes 196616 | tf_op jit(solution)/shard_map/ppermute | solution.py:462
  4.8 4.1 %collective-permute-start.1 = (bf16[4,16,512]{2,1,0:T(8,128)(2,1)S(1)}, bf16[4,16,512]{2,1,0:T(8,128)(2,1)S(1)}, u32[]{:S(2)}, u32[]{:S(2)}) collective-permute-start(bf16[4,16,512]{2,1,0:T(8,128)(2,1)S(1)} %get-tuple-element.40), channel_id=1, source_target_pairs={{0,12},{4,8},{8,4},{12,0},{1,13},{5,9},{9,5},{13,1},{2,14},{6,10},... | collective-permute-start | bytes 196616 | tf_op jit(solution)/shard_map/ppermute | solution.py:462
  4.8 4.1 %collective-permute-start.2 = (bf16[4,16,512]{2,1,0:T(8,128)(2,1)S(1)}, bf16[4,16,512]{2,1,0:T(8,128)(2,1)S(1)}, u32[]{:S(2)}, u32[]{:S(2)}) collective-permute-start(bf16[4,16,512]{2,1,0:T(8,128)(2,1)S(1)} %get-tuple-element.41), channel_id=1, source_target_pairs={{0,4},{4,0},{8,12},{12,8},{1,5},{5,1},{9,13},{13,9},{2,6},{6,2},{1... | collective-permute-start | bytes 196616 | tf_op jit(solution)/shard_map/ppermute | solution.py:462
  5.0 13.8 %slice-start = ((s8[16777216]{0:T(1024)(128)(4,1)}), s8[4194304]{0:T(1024)(128)(4,1)S(1)}, s32[]{:S(2)}) async-start(s8[16777216]{0:T(1024)(128)(4,1)} %bitcast.4), calls=%async_computation | async-start | bytes 8388608
  5.0 13.8 %slice-start.1 = ((s8[16777216]{0:T(1024)(128)(4,1)}), s8[4194304]{0:T(1024)(128)(4,1)S(1)}, s32[]{:S(2)}) async-start(s8[16777216]{0:T(1024)(128)(4,1)} %bitcast.4), calls=%async_computation.1 | async-start | bytes 8388608
  5.0 13.8 %slice-start.2 = ((s8[16777216]{0:T(1024)(128)(4,1)}), s8[4194304]{0:T(1024)(128)(4,1)S(1)}, s32[]{:S(2)}) async-start(s8[16777216]{0:T(1024)(128)(4,1)} %bitcast.4), calls=%async_computation.2 | async-start | bytes 8388608
  8.9 9.9 %slice-start.3 = ((s8[16777216]{0:T(1024)(128)(4,1)}), s8[4194304]{0:T(1024)(128)(4,1)S(1)}, s32[]{:S(2)}) async-start(s8[16777216]{0:T(1024)(128)(4,1)} %bitcast.4), calls=%async_computation.3 | async-start | bytes 8388608
  8.9 16.3 %slice-start.4 = ((s8[16777216]{0:T(1024)(128)(4,1)}), s8[4194304]{0:T(1024)(128)(4,1)S(1)}, s32[]{:S(2)}) async-start(s8[16777216]{0:T(1024)(128)(4,1)} %bitcast.6), calls=%async_computation.4 | async-start | bytes 8388608
  8.9 16.3 %slice-start.5 = ((s8[16777216]{0:T(1024)(128)(4,1)}), s8[4194304]{0:T(1024)(128)(4,1)S(1)}, s32[]{:S(2)}) async-start(s8[16777216]{0:T(1024)(128)(4,1)} %bitcast.6), calls=%async_computation.5 | async-start | bytes 8388608
  10.1 6.2 %collective-permute-start.5 = (bf16[24,1024]{1,0:T(8,128)(2,1)S(1)}, bf16[24,1024]{1,0:T(8,128)(2,1)S(1)}, u32[]{:S(2)}, u32[]{:S(2)}) collective-permute-start(bf16[24,1024]{1,0:T(8,128)(2,1)S(1)} %get-tuple-element.45.refs_3_), channel_id=1, source_target_pairs={{0,3},{1,2},{2,1},{3,0},{4,7},{5,6},{6,5},{7,4},{8,11},{9,10},{10,... | collective-permute-start | bytes 147464 | tf_op jit(solution)/shard_map/ppermute | solution.py:462
  13.8 5.0 %collective-permute-start.4 = (bf16[24,1024]{1,0:T(8,128)(2,1)S(1)}, bf16[24,1024]{1,0:T(8,128)(2,1)S(1)}, u32[]{:S(2)}, u32[]{:S(2)}) collective-permute-start(bf16[24,1024]{1,0:T(8,128)(2,1)S(1)} %get-tuple-element.45.refs_3_), channel_id=1, source_target_pairs={{0,2},{1,3},{2,0},{3,1},{4,6},{5,7},{6,4},{7,5},{8,10},{9,11},{10,... | collective-permute-start | bytes 147464 | tf_op jit(solution)/shard_map/ppermute | solution.py:462
  13.8 5.0 %collective-permute-start.3 = (bf16[24,1024]{1,0:T(8,128)(2,1)S(1)}, bf16[24,1024]{1,0:T(8,128)(2,1)S(1)}, u32[]{:S(2)}, u32[]{:S(2)}) collective-permute-start(bf16[24,1024]{1,0:T(8,128)(2,1)S(1)} %get-tuple-element.45.refs_3_), channel_id=1, source_target_pairs={{0,1},{1,0},{2,3},{3,2},{4,5},{5,4},{6,7},{7,6},{8,9},{9,8},{10,11... | collective-permute-start | bytes 147464 | tf_op jit(solution)/shard_map/ppermute | solution.py:462
  18.8 6.4 %slice-start.6 = ((s8[16777216]{0:T(1024)(128)(4,1)}), s8[4194304]{0:T(1024)(128)(4,1)S(1)}, s32[]{:S(2)}) async-start(s8[16777216]{0:T(1024)(128)(4,1)} %bitcast.6), calls=%async_computation.6 | async-start | bytes 8388608
  22.5 1.6 %collective-permute-start.6 = (bf16[48,2432]{1,0:T(8,128)(2,1)S(1)}, bf16[48,2432]{1,0:T(8,128)(2,1)S(1)}, u32[]{:S(2)}, u32[]{:S(2)}) collective-permute-start(bf16[48,2432]{1,0:T(8,128)(2,1)S(1)} %get-tuple-element.48), channel_id=1, source_target_pairs={{0,4},{4,0},{8,12},{12,8},{1,5},{5,1},{9,13},{13,9},{2,6},{6,2},{1... | collective-permute-start | bytes 700424 | tf_op jit(solution)/shard_map/ppermute | solution.py:462
  24.2 11.8 %collective-permute-start.8 = (bf16[48,2176]{1,0:T(8,128)(2,1)S(1)}, bf16[48,2176]{1,0:T(8,128)(2,1)S(1)}, u32[]{:S(2)}, u32[]{:S(2)}) collective-permute-start(bf16[48,2176]{1,0:T(8,128)(2,1)S(1)} %chip_sum_first.1.refs_4_.refs_0_), channel_id=1, source_target_pairs={{0,8},{4,12},{8,0},{12,4},{1,9},{5,13},{9,1},{13,5},{2,10},{6,14},... | collective-permute-start | bytes 626696 | tf_op jit(solution)/shard_map/ppermute | solution.py:462
  26.8 2.3 %collective-permute-start.9 = (bf16[48,1024]{1,0:T(8,128)(2,1)S(1)}, bf16[48,1024]{1,0:T(8,128)(2,1)S(1)}, u32[]{:S(2)}, u32[]{:S(2)}) collective-permute-start(bf16[48,1024]{1,0:T(8,128)(2,1)S(1)} %get-tuple-element.56), channel_id=1, source_target_pairs={{0,4},{4,0},{8,12},{12,8},{1,5},{5,1},{9,13},{13,9},{2,6},{6,2},{1... | collective-permute-start | bytes 294920 | tf_op jit(solution)/shard_map/ppermute | solution.py:462
  28.5 1.8 %collective-permute-start.7 = (bf16[48,1024]{1,0:T(8,128)(2,1)S(1)}, bf16[48,1024]{1,0:T(8,128)(2,1)S(1)}, u32[]{:S(2)}, u32[]{:S(2)}) collective-permute-start(bf16[48,1024]{1,0:T(8,128)(2,1)S(1)} %get-tuple-element.53), channel_id=1, source_target_pairs={{0,4},{4,0},{8,12},{12,8},{1,5},{5,1},{9,13},{13,9},{2,6},{6,2},{1... | collective-permute-start | bytes 294920 | tf_op jit(solution)/shard_map/ppermute | solution.py:462
  29.1 6.4 %collective-permute-start.10 = (bf16[48,1024]{1,0:T(8,128)(2,1)S(1)}, bf16[48,1024]{1,0:T(8,128)(2,1)S(1)}, u32[]{:S(2)}, u32[]{:S(2)}) collective-permute-start(bf16[48,1024]{1,0:T(8,128)(2,1)S(1)} %chip_sum_next.3.refs_2_), channel_id=1, source_target_pairs={{0,8},{4,12},{8,0},{12,4},{1,9},{5,13},{9,1},{13,5},{2,10},{6,14},... | collective-permute-start | bytes 294920 | tf_op jit(solution)/shard_map/ppermute | solution.py:462
  30.3 5.7 %collective-permute-start.11 = (bf16[48,1024]{1,0:T(8,128)(2,1)S(1)}, bf16[48,1024]{1,0:T(8,128)(2,1)S(1)}, u32[]{:S(2)}, u32[]{:S(2)}) collective-permute-start(bf16[48,1024]{1,0:T(8,128)(2,1)S(1)} %chip_sum_next.2.refs_2_.refs_4_), channel_id=1, source_target_pairs={{0,8},{4,12},{8,0},{12,4},{1,9},{5,13},{9,1},{13,5},{2,10},{6,14},... | collective-permute-start | bytes 294920 | tf_op jit(solution)/shard_map/ppermute | solution.py:462
  36.2 1.7 %collective-permute-start.12 = (bf16[48,2048]{1,0:T(8,128)(2,1)S(1)}, bf16[48,2048]{1,0:T(8,128)(2,1)S(1)}, u32[]{:S(2)}, u32[]{:S(2)}) collective-permute-start(bf16[48,2048]{1,0:T(8,128)(2,1)S(1)} %hidden.1.refs_1_.refs_3_), channel_id=1, source_target_pairs={{0,4},{4,0},{8,12},{12,8},{1,5},{5,1},{9,13},{13,9},{2,6},{6,2},{1... | collective-permute-start | bytes 589832 | tf_op jit(solution)/shard_map/ppermute | solution.py:462
  39.8 8.3 %collective-permute-start.14 = (bf16[24,1024]{1,0:T(8,128)(2,1)S(1)}, bf16[24,1024]{1,0:T(8,128)(2,1)S(1)}, u32[]{:S(2)}, u32[]{:S(2)}) collective-permute-start(bf16[24,1024]{1,0:T(8,128)(2,1)S(1)} %get-tuple-element.68), channel_id=1, source_target_pairs={{0,3},{1,2},{2,1},{3,0},{4,7},{5,6},{6,5},{7,4},{8,11},{9,10},{10,... | collective-permute-start | bytes 147464 | tf_op jit(solution)/shard_map/ppermute | solution.py:462
  42.0 6.1 %collective-permute-start.15 = (bf16[24,1024]{1,0:T(8,128)(2,1)S(1)}, bf16[24,1024]{1,0:T(8,128)(2,1)S(1)}, u32[]{:S(2)}, u32[]{:S(2)}) collective-permute-start(bf16[24,1024]{1,0:T(8,128)(2,1)S(1)} %get-tuple-element.69), channel_id=1, source_target_pairs={{0,2},{1,3},{2,0},{3,1},{4,6},{5,7},{6,4},{7,5},{8,10},{9,11},{10,... | collective-permute-start | bytes 147464 | tf_op jit(solution)/shard_map/ppermute | solution.py:462
  42.5 5.6 %collective-permute-start.16 = (bf16[24,1024]{1,0:T(8,128)(2,1)S(1)}, bf16[24,1024]{1,0:T(8,128)(2,1)S(1)}, u32[]{:S(2)}, u32[]{:S(2)}) collective-permute-start(bf16[24,1024]{1,0:T(8,128)(2,1)S(1)} %get-tuple-element.70), channel_id=1, source_target_pairs={{0,1},{1,0},{2,3},{3,2},{4,5},{5,4},{6,7},{7,6},{8,9},{9,8},{10,11... | collective-permute-start | bytes 147464 | tf_op jit(solution)/shard_map/ppermute | solution.py:462
  44.3 3.8 %collective-permute-start.13 = (bf16[48,256]{1,0:T(8,128)(2,1)S(1)}, bf16[48,256]{1,0:T(8,128)(2,1)S(1)}, u32[]{:S(2)}, u32[]{:S(2)}) collective-permute-start(bf16[48,256]{1,0:T(8,128)(2,1)S(1)} %get-tuple-element.67), channel_id=1, source_target_pairs={{0,8},{4,12},{8,0},{12,4},{1,9},{5,13},{9,1},{13,5},{2,10},{6,14},... | collective-permute-start | bytes 73736 | tf_op jit(solution)/shard_map/ppermute | solution.py:462
  (1 other events, 6.4 us)
